TPU v7x, 32 devices: a whole 2x2x4 slice. The times are simulated.
32 devices in a mesh: dp: 2 (over y), context: 4 (over z), tensor: 4 (over x, core).
Axes of the slice: x: 2, y: 2, z: 4, core: 2. Of those that a mesh axis runs over, the one named last changes fastest.
Arguments:
- hidden_in: bfloat16 [2, 4, 1024, 768], P(None, 'dp', 'context'), may hold values from -6 to 6
- segment_ids: int32 [2, 4, 1024], P(None, 'dp'), may hold values from 0 to 17, as said below
- norm_gain: float32 [768], replicated, may hold values from 0.5 to 1.5
- head_projection: bfloat16 [768, 2, 1536], P(('dp', 'context'), None, 'tensor'), may hold values from -0.21875 to 0.21875
- shared_projection: bfloat16 [768, 256], P(('dp', 'context')), may hold values from -0.21875 to 0.21875
- step_projection: bfloat16 [768, 24], P(('dp', 'context'), 'tensor'), may hold values from -0.21875 to 0.21875
- conv_heads: float32 [4, 1536], P(None, 'tensor'), may hold values from -3 to 3
- bias_heads: float32 [1536], P('tensor'), may hold values from -0.5 to 0.5
- conv_shared: float32 [4, 256], replicated, may hold values from -3 to 3
- bias_shared: float32 [256], replicated, may hold values from -0.5 to 0.5
- step_bias: float32 [24], P('tensor'), may hold values from -7 to -4
- log_decay: float32 [24], P('tensor'), may hold values from 0 to 1.5
- skip_gain: float32 [24], P('tensor'), may hold values from 0.5 to 1.5
- gate_gain: float32 [1536], P('tensor'), may hold values from 0.5 to 1.5
- output_weight: bfloat16 [1536, 768], P('tensor', ('dp', 'context')), may hold values from -0.15625 to 0.15625
- out_cotangent: bfloat16 [2, 4, 1024, 768], P(None, 'dp', 'context'), may hold values from -6 to 6
Outputs:
- block_out: bfloat16 [2, 4, 1024, 768], P(None, 'dp', 'context')
- input_grad: bfloat16 [2, 4, 1024, 768], P(None, 'dp', 'context')
- grad_norm_gain: float32 [768], replicated
- grad_proj_heads: float32 [768, 2, 1536], P(('dp', 'context'), None, 'tensor')
- grad_proj_shared: float32 [768, 256], P(('dp', 'context'), 'tensor')
- grad_proj_step: float32 [768, 24], P(('dp', 'context'), 'tensor')
- grad_conv_heads: float32 [4, 1536], P(None, 'tensor')
- grad_bias_heads: float32 [1536], P('tensor')
- grad_conv_shared: float32 [4, 256], replicated
- grad_bias_shared: float32 [256], replicated
- grad_step_bias: float32 [24], P('tensor')
- grad_log_decay: float32 [24], P('tensor')
- grad_skip_gain: float32 [24], P('tensor')
- grad_gate_gain: float32 [1536], P('tensor')
- grad_out_weight: float32 [1536, 768], P('tensor', ('dp', 'context'))
Inputs may be any that keep to these rules, and one draw needn't show every extreme that they name: `segment_ids`: in each row segment numbers start at 0, never fall and rise by one at each document boundary.
All inputs are finite; a program needn't handle non-finite values.
Results may differ from a plain program's by a relative error of at most 0.014.
Values may be sent and summed in bfloat16 or wider, within the bound.
A program may use at most 128 MiB of HBM per device.

v0:
```python
import jax
import jax.numpy as jnp
from jax import lax
from jax.sharding import PartitionSpec as P

EPS = 1e-05
HIGH_ACCURACY = lax.Precision.HIGHEST


def from_behind(value, axis, steps):
    count = lax.axis_size(axis)
    leading, last = (max(0, -steps), min(count, count - steps))
    return lax.ppermute(value, axis, [(source, source + steps) for source in range(leading, last)])


def prefix(value, axis, join, neutral, backward):
    count, mine = (lax.axis_size(axis), lax.axis_index(axis))
    pieces = jax.tree.map(lambda part: lax.all_gather(part, axis), value)
    if backward:
        pieces = jax.tree.map(lambda part: part[::-1], pieces)
        mine = count - 1 - mine
    running = jax.tree.map(
        lambda part, zero: jnp.full_like(part, 0) + jnp.asarray(zero, part.dtype), value, neutral
    )

    def turn(position, running):
        longer = join(running, jax.tree.map(lambda part: part[position], pieces))
        return jax.tree.map(lambda new, old: jnp.where(position < mine, new, old), longer, running)

    return lax.fori_loop(0, count - 1, turn, running)


def conv_ext(extended, kernel, offsets, seg_ext):
    margin = kernel.shape[0] - 1
    length = extended.shape[1] - margin
    current = seg_ext[:, margin:]
    summed = extended[:, margin:] * kernel[0] + offsets
    for lagging in range(1, margin + 1):
        anchor = margin - lagging
        linked = (seg_ext[:, anchor : anchor + length] == current).astype(jnp.float32)
        summed = (
            summed + extended[:, anchor : anchor + length] * kernel[lagging] * linked[:, :, None]
        )
    return summed


def ssd_local(heads_x, steps, decay_rate, b_matrix, c_matrix, segments, previous):
    length = segments.shape[1]
    growth = steps * decay_rate
    running = jnp.cumsum(growth, axis=1)
    places = jnp.arange(length)
    causal = places[:, None] >= places[None, :]
    linked = (segments[:, :, None] == segments[:, None, :]) & causal[None]
    by_head = jnp.swapaxes(running, 1, 2)
    spread = by_head[:, :, :, None] - by_head[:, :, None, :]
    masked = jnp.broadcast_to(linked[:, None], spread.shape)
    decays = jnp.where(masked, jnp.exp(jnp.where(masked, spread, 0.0)), 0.0)
    scores = jnp.einsum("stn,sun->stu", c_matrix, b_matrix, precision=HIGH_ACCURACY)
    weights = decays * scores[:, None] * jnp.swapaxes(steps, 1, 2)[:, :, None, :]
    inside = jnp.einsum("shtu,suhp->sthp", weights, heads_x, precision=HIGH_ACCURACY)
    carried = (segments == previous[:, None]).astype(jnp.float32)
    leading = jnp.exp(running) * carried[:, :, None]
    closing = (segments == segments[:, -1:]).astype(jnp.float32)
    trailing = jnp.exp(running[:, -1:, :] - running) * closing[:, :, None] * steps
    scaled_x = heads_x * trailing[..., None]
    fresh = jnp.einsum("suhp,sun->shpn", scaled_x, b_matrix, precision=HIGH_ACCURACY)
    return (inside, fresh, leading)


def apply_state(c_matrix, leading, state_in):
    readout = jnp.einsum("stn,shpn->sthp", c_matrix, state_in, precision=HIGH_ACCURACY)
    return readout * leading[..., None]


def forward_combine(earlier, later):
    retain_first, state_first = earlier
    retain_second, state_second = later
    return (
        retain_first * retain_second,
        retain_second[:, :, None, None] * state_first + state_second,
    )


def backward_combine(earlier, later):
    retain_first, grad_first = earlier
    retain_second, grad_second = later
    return (
        retain_first * retain_second,
        grad_second + retain_second[:, :, None, None] * grad_first,
    )


def silu_slope(values):
    logistic = jax.nn.sigmoid(values)
    return logistic * (1.0 + values * (1.0 - logistic))


def on_device(
    hidden_in,
    segment_ids,
    norm_gain,
    head_projection,
    shared_projection,
    step_projection,
    conv_heads,
    bias_heads,
    conv_shared,
    bias_shared,
    step_bias,
    log_decay,
    skip_gain,
    gate_gain,
    output_weight,
    out_cotangent,
):
    micro_count, seq_count, tokens, model_width = hidden_in.shape
    heads_here = step_bias.shape[0]
    inner_here = gate_gain.shape[0]
    head_size = inner_here // heads_here
    shared_width = shared_projection.shape[1]
    state_size = shared_width // 2
    tensor_count = lax.axis_size("tensor")
    inner_all = inner_here * tensor_count
    slice_width = shared_width // tensor_count
    tensor_rank = lax.axis_index("tensor")
    margin = conv_heads.shape[0] - 1
    begin = lax.axis_index("context") * tokens
    seg_padded = jnp.pad(segment_ids, ((0, 0), (0, 0), (margin, 0)), constant_values=-1)
    kernel = jnp.concatenate([conv_heads, conv_shared], axis=1)
    offsets = jnp.concatenate([bias_heads, bias_shared])
    decay_rate = -jnp.exp(log_decay)
    norm_total = jnp.zeros_like(norm_gain)
    kernel_total = jnp.zeros_like(kernel)
    offset_total = jnp.zeros_like(offsets)
    step_bias_total = jnp.zeros_like(step_bias)
    rate_total = jnp.zeros_like(log_decay)
    skip_total = jnp.zeros_like(skip_gain)
    gain_total = jnp.zeros_like(gate_gain)
    big_total = None
    results = []
    input_grads = []
    for index in range(micro_count):
        fetched = (
            lax.all_gather(head_projection, ("dp", "context"), axis=0, tiled=True),
            lax.all_gather(shared_projection, ("dp", "context"), axis=0, tiled=True),
            lax.all_gather(step_projection, ("dp", "context"), axis=0, tiled=True),
            lax.all_gather(output_weight, ("dp", "context"), axis=1, tiled=True),
        )
        heads_full, shared_full, complete_step, complete_output = fetched
        widened_value = jnp.concatenate([heads_full[:, 0], heads_full[:, 1], shared_full], axis=1)
        hidden = hidden_in[index].astype(jnp.float32)
        rms_in = lax.rsqrt(jnp.mean(hidden * hidden, axis=-1, keepdims=True) + EPS)
        unit = hidden * rms_in
        normalized_input = (unit * norm_gain).astype(jnp.bfloat16)
        projected = jnp.einsum(
            "tfn,no->tfo", normalized_input, widened_value, preferred_element_type=jnp.float32
        ).astype(jnp.bfloat16)
        unshaped_step = jnp.einsum(
            "anp,py->any", normalized_input, complete_step, preferred_element_type=jnp.float32
        ).astype(jnp.bfloat16)
        gate_in = projected[..., :inner_here]
        channels = projected[..., inner_here:]
        rim = from_behind(channels[:, tokens - margin :], "context", 1)
        extended = jnp.concatenate([rim, channels], axis=1).astype(jnp.float32)
        seg_ext = lax.dynamic_slice_in_dim(seg_padded[index], begin, tokens + margin, 1)
        segments = seg_ext[:, margin:]
        previous = seg_ext[:, margin - 1]

        def conv_act(values, taps, shifts):
            return jax.nn.silu(conv_ext(values, taps, shifts, seg_ext))

        activated, conv_back = jax.vjp(conv_act, extended, kernel, offsets)
        mixed = activated.astype(jnp.bfloat16)
        heads_x = (
            mixed[..., :inner_here]
            .astype(jnp.float32)
            .reshape(seq_count, tokens, heads_here, head_size)
        )
        b_matrix = mixed[..., inner_here : inner_here + state_size].astype(jnp.float32)
        c_matrix = mixed[..., inner_here + state_size :].astype(jnp.float32)
        step_pre = unshaped_step.astype(jnp.float32) + step_bias
        steps = jax.nn.softplus(step_pre)

        def local_part(part_x, part_step, part_rate, part_b, part_c):
            return ssd_local(part_x, part_step, part_rate, part_b, part_c, segments, previous)

        (inside, fresh, leading), ssd_back = jax.vjp(
            local_part, heads_x, steps, decay_rate, b_matrix, c_matrix
        )
        retain = leading[:, -1, :]
        _, state_in = prefix(
            (retain, fresh),
            "context",
            forward_combine,
            (jnp.ones_like(retain), jnp.zeros_like(fresh)),
            False,
        )
        ssd = inside + apply_state(c_matrix, leading, state_in) + skip_gain[:, None] * heads_x
        ssd_flat = ssd.reshape(seq_count, tokens, inner_here)
        gate_value = gate_in.astype(jnp.float32)
        gate_act = jax.nn.silu(gate_value)
        gated = ssd_flat * gate_act
        square_sum = lax.psum(jnp.sum(gated * gated, axis=-1), "tensor")
        rms_gate = lax.rsqrt(square_sum[..., None] / inner_all + EPS)
        normal_gate = gated * rms_gate
        normalized_output = (normal_gate * gate_gain).astype(jnp.bfloat16)
        partial_output = jnp.einsum(
            "xrm,mz->xrz", normalized_output, complete_output, preferred_element_type=jnp.float32
        )
        branch_result = lax.psum(partial_output, "tensor")
        results.append((hidden + branch_result).astype(jnp.bfloat16))
        output_adjoint = out_cotangent[index]
        output_portion = jnp.einsum(
            "pwx,pwu->xu", normalized_output, output_adjoint, preferred_element_type=jnp.float32
        )
        normalized_gradient = jnp.einsum(
            "ijv,ev->ije", output_adjoint, complete_output, preferred_element_type=jnp.float32
        )
        gain_total = gain_total + jnp.sum(normalized_gradient * normal_gate, axis=(0, 1))
        d_scaled = normalized_gradient * gate_gain
        dot_sum = lax.psum(jnp.sum(d_scaled * gated, axis=-1), "tensor")
        d_gated = rms_gate * d_scaled - gated * rms_gate**3 * dot_sum[..., None] / inner_all
        d_ssd_flat = d_gated * gate_act
        d_gate_in = (d_gated * ssd_flat * silu_slope(gate_value)).astype(jnp.bfloat16)
        d_ssd = d_ssd_flat.reshape(seq_count, tokens, heads_here, head_size)
        skip_total = skip_total + jnp.sum(d_ssd * heads_x, axis=(0, 1, 3))
        readout = jnp.einsum("stn,shpn->sthp", c_matrix, state_in, precision=HIGH_ACCURACY)
        weighted = d_ssd * leading[..., None]
        d_leading = jnp.sum(d_ssd * readout, axis=-1)
        local_grad = jnp.einsum("sthp,stn->shpn", weighted, c_matrix, precision=HIGH_ACCURACY)
        _, d_end = prefix(
            (retain, local_grad),
            "context",
            backward_combine,
            (jnp.ones_like(retain), jnp.zeros_like(local_grad)),
            True,
        )
        d_leading = d_leading.at[:, -1, :].add(jnp.sum(d_end * state_in, axis=(2, 3)))
        d_heads_x, d_steps, d_rate, d_b, d_c = ssd_back((d_ssd, d_end, d_leading))
        d_c = d_c + jnp.einsum("sthp,shpn->stn", weighted, state_in, precision=HIGH_ACCURACY)
        d_heads_x = d_heads_x + skip_gain[:, None] * d_ssd
        rate_total = rate_total + d_rate * decay_rate
        d_shared_post = lax.psum(jnp.concatenate([d_b, d_c], axis=-1), "tensor")
        d_mixed = jnp.concatenate(
            [d_heads_x.reshape(seq_count, tokens, inner_here), d_shared_post], axis=-1
        )
        d_extended, d_kernel, d_offsets = conv_back(d_mixed)
        kernel_total = kernel_total + d_kernel
        offset_total = offset_total + d_offsets
        returned = from_behind(d_extended[:, :margin], "context", -1)
        d_channels = d_extended[:, margin:].at[:, tokens - margin :].add(returned)
        d_channels_low = d_channels.astype(jnp.bfloat16)
        d_step_pre = d_steps * jax.nn.sigmoid(step_pre)
        step_bias_total = step_bias_total + jnp.sum(d_step_pre, axis=(0, 1))
        unshaped_step_gradient = d_step_pre.astype(jnp.bfloat16)
        d_heads_low = d_channels_low[..., :inner_here]
        d_shared_low = d_channels_low[..., inner_here:]
        d_mine = lax.dynamic_slice_in_dim(d_shared_low, tensor_rank * slice_width, slice_width, 2)
        shared_mine = lax.dynamic_slice_in_dim(
            shared_full, tensor_rank * slice_width, slice_width, 1
        )
        local_gradient = jnp.concatenate([d_gate_in, d_heads_low, d_mine], axis=-1)
        local_weight_slice = jnp.concatenate(
            [heads_full[:, 0], heads_full[:, 1], shared_mine], axis=1
        )
        local_gradient_list = jnp.einsum(
            "jbn,jbv->nv", normalized_input, local_gradient, preferred_element_type=jnp.float32
        )
        heads_part = local_gradient_list[:, : 2 * inner_here].reshape(model_width, 2, inner_here)
        shared_part = local_gradient_list[:, 2 * inner_here :]
        step_part = jnp.einsum(
            "hsn,hsm->nm",
            normalized_input,
            unshaped_step_gradient,
            preferred_element_type=jnp.float32,
        )
        d_normed = jnp.einsum(
            "kmu,ru->kmr", local_gradient, local_weight_slice, preferred_element_type=jnp.float32
        )
        d_normed = d_normed + jnp.einsum(
            "urt,wt->urw", unshaped_step_gradient, complete_step, preferred_element_type=jnp.float32
        )
        d_normed = lax.psum(d_normed, "tensor")
        norm_total = norm_total + jnp.sum(d_normed * unit, axis=(0, 1))
        d_unit = d_normed * norm_gain
        d_hidden = rms_in * (d_unit - unit * jnp.mean(d_unit * unit, axis=-1, keepdims=True))
        input_grads.append((output_adjoint.astype(jnp.float32) + d_hidden).astype(jnp.bfloat16))
        terms = (heads_part, shared_part, step_part, output_portion)
        big_total = terms if big_total is None else jax.tree.map(jnp.add, big_total, terms)
    big_total = (
        lax.psum_scatter(big_total[0], ("dp", "context"), scatter_dimension=0, tiled=True),
        lax.psum_scatter(big_total[1], ("dp", "context"), scatter_dimension=0, tiled=True),
        lax.psum_scatter(big_total[2], ("dp", "context"), scatter_dimension=0, tiled=True),
        lax.psum_scatter(big_total[3], ("dp", "context"), scatter_dimension=1, tiled=True),
    )
    small = lax.psum(
        (
            norm_total,
            kernel_total,
            offset_total,
            step_bias_total,
            rate_total,
            skip_total,
            gain_total,
        ),
        ("dp", "context"),
    )
    norm_sum, kernel_sum, offset_sum, step_bias_sum, rate_sum, skip_sum, gain_sum = small
    block_out = jnp.stack(results)
    input_grad = jnp.stack(input_grads)
    return (
        block_out,
        input_grad,
        norm_sum,
        big_total[0],
        big_total[1],
        big_total[2],
        kernel_sum[:, :inner_here],
        offset_sum[:inner_here],
        kernel_sum[:, inner_here:],
        offset_sum[inner_here:],
        step_bias_sum,
        rate_sum,
        skip_sum,
        gain_sum,
        big_total[3],
    )


def solution(mesh):
    return jax.shard_map(
        on_device,
        mesh=mesh,
        in_specs=(
            P(None, "dp", "context", None),
            P(None, "dp", None),
            P(),
            P(("dp", "context"), None, "tensor"),
            P(("dp", "context"), None),
            P(("dp", "context"), "tensor"),
            P(None, "tensor"),
            P("tensor"),
            P(),
            P(),
            P("tensor"),
            P("tensor"),
            P("tensor"),
            P("tensor"),
            P("tensor", ("dp", "context")),
            P(None, "dp", "context", None),
        ),
        out_specs=(
            P(None, "dp", "context", None),
            P(None, "dp", "context", None),
            P(),
            P(("dp", "context"), None, "tensor"),
            P(("dp", "context"), "tensor"),
            P(("dp", "context"), "tensor"),
            P(None, "tensor"),
            P("tensor"),
            P(),
            P(),
            P("tensor"),
            P("tensor"),
            P("tensor"),
            P("tensor"),
            P("tensor", ("dp", "context")),
        ),
        check_vma=False,
    )
```

profile of v0, /device:TPU:0, one launch (start us, length us, event | category | flops | bytes accessed | tf_op | source)
XLA Modules:
  0.0 914.0 jit_solution(14735230995396833574)
XLA Ops:
  10.9 28.7 %all-gather.6 = bf16[8,96,6]{1,2,0:T(8,128)(2,1)S(1)} all-gather(bf16[1,96,6]{1,2,0:T(8,128)(2,1)S(1)} %bitcast.402), channel_id=1, replica_groups=mesh['dp'=2,'context'=4,'tensor'=4] {'dp','context'}, dimensions={0}, use_global_device_ids=true | all-gather | bytes 10368 | tf_op jit(solution)/shard_map/all_gather | solution.py:146
  51.2 31.7 %all_gather.49 = bf16[768,256]{1,0:T(8,128)(2,1)S(1)} all-gather(bf16[96,256]{1,0:T(8,128)(2,1)S(1)} %copy-done.77), channel_id=1, replica_groups=mesh['dp'=2,'context'=4,'tensor'=4] {'dp','context'}, dimensions={0}, use_global_device_ids=true | all-gather | bytes 442368 | tf_op jit(solution)/shard_map/all_gather | solution.py:145
  110.6 11.8 %all-gather = f32[8,1,6]{2,1,0:T(1,128)} all-gather(f32[2,1,6]{2,1,0:T(1,128)} %copy.316), channel_id=2, replica_groups=mesh['dp'=2,'context'=4,'tensor'=4] {'context'}, dimensions={0}, use_global_device_ids=true | all-gather | bytes 240 | tf_op jit(solution)/shard_map/all_gather | solution.py:18
  122.4 8.8 all-gather.2
  132.9 34.6 %all_gather.54 = bf16[384,768]{0,1:T(8,128)(2,1)S(1)} all-gather(bf16[384,96]{0,1:T(8,128)(2,1)} %param.46), channel_id=1, replica_groups=mesh['dp'=2,'context'=4,'tensor'=4] {'dp','context'}, dimensions={1}, use_global_device_ids=true | all-gather | bytes 663552 | tf_op jit(solution)/shard_map/all_gather | solution.py:147
  186.1 7.1 while.60
  194.7 5.2 fusion.110
  205.3 12.8 %all-gather.17.cloned.1.call-done = f32[8,6,64,128]{3,2,1,0:T(8,128)} async-done(((f32[2,6,64,128]{3,2,1,0:T(8,128)}), f32[8,6,64,128]{3,2,1,0:T(8,128)}) %all-gather.17.cloned.1.call-update) | async-done | bytes 1572880 | tf_op jit(solution)/shard_map/all_gather | solution.py:18
  218.1 7.1 while.61
  237.1 6.4 all-reduce.22
  250.0 7.2 all-reduce.21
  279.8 5.9 fusion.27
  304.5 5.4 while.63
  314.2 24.9 %all-gather.19.cloned.1.call-done = f32[8,6,64,128]{3,2,1,0:T(8,128)} async-done(((f32[2,6,64,128]{3,2,1,0:T(8,128)}), f32[8,6,64,128]{3,2,1,0:T(8,128)}) %all-gather.19.cloned.1.call-update) | async-done | bytes 1572880 | tf_op jit(solution)/shard_map/all_gather | solution.py:18
  341.9 7.0 while.62
  368.2 16.3 %reduce-window.36 = f32[2,6,2,128]{3,2,1,0:T(2,128)} reduce-window(f32[2,6,2,128]{3,2,1,0:T(2,128)} %reshape.497, f32[]{:T(128)} %constant.233.clone.1), window={size=1x1x1x128 pad=0_0x0_0x0_0x0_127}, to_apply=%region_46.47 | reduce-window | flops 390144 | bytes 24580 | tf_op jit(solution)/shard_map/reduce-window.6
  402.4 16.3 %reduce-window.34 = f32[2,6,2,128]{3,2,1,0:T(2,128)} reduce-window(f32[2,6,2,128]{3,2,1,0:T(2,128)} %reshape.495, f32[]{:T(128)} %constant.233.clone.1), window={size=1x1x1x128 pad=0_0x0_0x0_0x0_127}, to_apply=%region_29.30 | reduce-window | flops 390144 | bytes 24580 | tf_op jit(solution)/shard_map/reduce-window.4
  451.6 23.7 %all-reduce.33.cloned.1.call-done = (f32[2,256,256]{2,1,0:T(8,128)}, f32[2,256,256]{2,1,0:T(8,128)}) async-done(((f32[2,256,256]{2,1,0:T(8,128)}, f32[2,256,256]{2,1,0:T(8,128)}), (f32[2,256,256]{2,1,0:T(8,128)}, f32[2,256,256]{2,1,0:T(8,128)})) %all-reduce.33.cloned.1.call-update) | async-done | bytes 1048592 | tf_op jit(solution)/shard_map/psum | solution.py:243
  522.7 17.9 %reduce-scatter.12.cloned.1.call-done = f32[96,6]{1,0:T(8,128)} async-done(((f32[768,6]{1,0:T(8,128)}), f32[96,6]{1,0:T(8,128)}) %reduce-scatter.12.cloned.1.call-update) | async-done | bytes 2320
  542.2 62.4 %reduce-scatter.10.cloned.1.call-done = f32[96,64]{1,0:T(8,128)} async-done(((f32[768,64]{1,0:T(8,128)}), f32[96,64]{1,0:T(8,128)}) %reduce-scatter.10.cloned.1.call-update) | async-done | bytes 24592
  606.1 110.3 %all-reduce.29.cloned.1.call-done = f32[768,2,384]{2,1,0:T(2,128)} async-done(((f32[768,2,384]{2,1,0:T(2,128)}), f32[768,2,384]{2,1,0:T(2,128)}) %all-reduce.29.cloned.1.call-update) | async-done | bytes 2359312
  718.2 120.5 %all-reduce.31.cloned.1.call-done = (f32[2,256,768]{2,1,0:T(8,128)}, f32[2,256,768]{2,1,0:T(8,128)}, f32[2,256,768]{2,1,0:T(8,128)}, f32[2,256,768]{2,1,0:T(8,128)}) async-done(((f32[2,256,768]{2,1,0:T(8,128)}, f32[2,256,768]{2,1,0:T(8,128)}, f32[2,256,768]{2,1,0:T(8,128)}, f32[2,256,768]{2,1,0:T(8,128)}), (f32[2,256,768]{2,1,0:T(8,128)}, f32[2,256,768]{2,1,0:T(8,128)}, f32[2,256,768]{2,1,0:T(8,128)}, ...) | async-done | bytes 6291472 | tf_op jit(solution)/shard_map/psum | solution.py:210
  841.5 38.0 %all-reduce.20 = (f32[768]{0:T(1024)}, f32[4,640]{1,0:T(4,128)S(1)}, f32[640]{0:T(1024)S(1)}, f32[6]{0:T(128)}, f32[6]{0:T(128)}, /*index=5*/f32[6]{0:T(128)}, f32[384]{0:T(512)}) all-reduce(f32[768]{0:T(1024)S(1)} %add.485, f32[4,640]{1,0:T(4,128)S(1)} %add_add_fusion.2, ...), channel_id=1, replica_groups=mesh['dp'=2,'context'=4,'tensor'=4] {'dp','context'}, use_global_device_ids=true, to_apply=%region_52.53 | all-reduce | flops 4370 | bytes 34960 | tf_op jit(solution)/shard_map/psum | solution.py:296
  888.3 18.7 %reduce-scatter.8.cloned.1.call-done = f32[384,96]{0,1:T(8,128)} async-done(((f32[384,768]{0,1:T(8,128)}), f32[384,96]{0,1:T(8,128)}) %reduce-scatter.8.cloned.1.call-update) | async-done | bytes 147472 | tf_op jit(solution)/shard_map/reduce_scatter | solution.py:294
  (538 shorter events, 294.7 us)
Async XLA Ops:
  7.2 77.2 %all-gather.13.cloned.1.call-start = ((), (), s32[]{:S(2)}) async-start(), calls=%async_computation.3 | async-start | bytes 1327104 | tf_op jit(solution)/shard_map/all_gather | solution.py:144
  9.0 177.1 %all-gather.15.cloned.1.call-start = ((), (), s32[]{:S(2)}) async-start(), calls=%async_computation.5 | async-start | bytes 1966080 | tf_op jit(solution)/shard_map/all_gather | solution.py:18
  10.8 75.0 %copy-start.102 = (f32[2,256]{1,0:T(2,128)}, f32[2,256]{1,0:T(2,128)S(1)}, u32[]{:S(2)}) copy-start(f32[2,256]{1,0:T(2,128)S(1)} %add_rsqrt_fusion.1) | copy-start | bytes 6148
  10.8 76.0 %copy-start.104 = (f32[2,256]{1,0:T(2,128)}, f32[2,256]{1,0:T(2,128)S(1)}, u32[]{:S(2)}) copy-start(f32[2,256]{1,0:T(2,128)S(1)} %add_rsqrt_fusion.3) | copy-start | bytes 6148
  40.7 67.8 %copy-start.55 = (f32[2,256,6]{1,2,0:T(8,128)}, f32[2,256,6]{1,2,0:T(8,128)S(1)}, u32[]{:S(2)}) copy-start(f32[2,256,6]{1,2,0:T(8,128)S(1)} %get-tuple-element.694) | copy-start | bytes 36868
  51.2 43.4 %copy-start.78 = (f32[640]{0:T(1024)}, f32[640]{0:T(1024)S(1)}, u32[]{:S(2)}) copy-start(f32[640]{0:T(1024)S(1)} %get-tuple-element.545) | copy-start | bytes 7684
  51.2 43.4 %copy-start.80 = (f32[640]{0:T(1024)}, f32[640]{0:T(1024)S(1)}, u32[]{:S(2)}) copy-start(f32[640]{0:T(1024)S(1)} %get-tuple-element.546) | copy-start | bytes 7684
  51.2 43.4 %copy-start.82 = (f32[640]{0:T(1024)}, f32[640]{0:T(1024)S(1)}, u32[]{:S(2)}) copy-start(f32[640]{0:T(1024)S(1)} %get-tuple-element.547) | copy-start | bytes 7684
  51.2 43.4 %copy-start.84 = (f32[640]{0:T(1024)}, f32[640]{0:T(1024)S(1)}, u32[]{:S(2)}) copy-start(f32[640]{0:T(1024)S(1)} %get-tuple-element.548) | copy-start | bytes 7684
  88.0 5.0 collective-permute-start.1
  90.4 3.9 collective-permute-start
  103.0 115.1 %all-gather.17.cloned.1.call-start = ((), (), s32[]{:S(2)}) async-start(), calls=%async_computation.6 | async-start | bytes 1966080 | tf_op jit(solution)/shard_map/all_gather | solution.py:18
  181.8 120.0 %all-gather.21.cloned.1.call-start = ((), (), s32[]{:S(2)}) async-start(), calls=%async_computation.8 | async-start | bytes 1966080 | tf_op jit(solution)/shard_map/all_gather | solution.py:18
  266.0 73.1 %all-gather.19.cloned.1.call-start = ((), (), s32[]{:S(2)}) async-start(), calls=%async_computation.7 | async-start | bytes 1966080 | tf_op jit(solution)/shard_map/all_gather | solution.py:18
  285.8 189.5 %all-reduce.33.cloned.1.call-start = ((), (), s32[]{:S(2)}) async-start(), calls=%async_computation.13 | async-start | bytes 2097152 | tf_op jit(solution)/shard_map/psum | solution.py:243
  358.2 72.9 %copy-start.21 = (f32[2,256,384]{1,2,0:T(8,128)S(1)}, f32[2,256,384]{1,2,0:T(8,128)}, u32[]{:S(2)}) copy-start(f32[2,256,384]{1,2,0:T(8,128)} %copy.332) | copy-start | bytes 2359300
  440.1 100.6 %reduce-scatter.12.cloned.1.call-start = ((), (), s32[]{:S(2)}) async-start(), calls=%async_computation.10 | async-start | bytes 442368
  451.5 153.1 %reduce-scatter.10.cloned.1.call-start = ((), (), s32[]{:S(2)}) async-start(), calls=%async_computation.9 | async-start | bytes 442368
  481.7 5.7 collective-permute-start.2
  484.5 7.8 collective-permute-start.3
  500.9 215.5 %all-reduce.29.cloned.1.call-start = ((), (), s32[]{:S(2)}) async-start(), calls=%async_computation.11 | async-start | bytes 4718592
  506.8 331.9 %all-reduce.31.cloned.1.call-start = ((), (), s32[]{:S(2)}) async-start(), calls=%async_computation.12 | async-start | bytes 12582912 | tf_op jit(solution)/shard_map/psum | solution.py:210
  517.1 389.9 %reduce-scatter.8.cloned.1.call-start = ((), (), s32[]{:S(2)}) async-start(), calls=%async_computation.4 | async-start | bytes 1327104 | tf_op jit(solution)/shard_map/reduce_scatter | solution.py:294
  520.9 317.7 %copy-start.11 = (bf16[2,2,256,768]{3,2,1,0:T(8,128)(2,1)S(1)}, bf16[2,2,256,768]{3,2,1,0:T(8,128)(2,1)}, u32[]{:S(2)}) copy-start(bf16[2,2,256,768]{3,2,1,0:T(8,128)(2,1)} %param.32) | copy-start | bytes 4718596
  (127 other events, 856.8 us)
Sparse Core Ops, SparseCore 0:
  10.8 43.9 all-gather.12
  103.1 46.4 all-gather.14
  181.9 36.1 all-gather.16
  266.1 35.5 all-gather.20
  303.1 35.9 all-gather.18
  440.2 35.0 all-reduce.32
  478.9 61.7 reduce-scatter.11
  544.2 60.3 reduce-scatter.9
  608.6 107.7 all-reduce.28
  719.4 119.1 all-reduce.30
  842.6 64.3 reduce-scatter.7
where the time goes:
time: 925 us; the launch traced here: 914 us
  waiting for transfers between devices  397 us (43%)
  blocking collectives  167 us (18%)
  other arithmetic  124 us (13%)
  local copies, waits for them, and re-layouts  99.8 us (11%)
  matrix products  99.5 us (11%)
  between operations  16.9 us (2%)
    unnamed x14, waiting for transfers between devices  191 us
    psum x1, waiting for transfers between devices, on_device(): branch_result = lax.psum(partial_output, 'tensor')  120 us
    another operation x14, other arithmetic  48.4 us
    all_gather x4, waiting for transfers between devices, prefix(): pieces = jax.tree.map(lambda part: lax.all_gather(part, axis), value)  41.2 us
    psum x1, blocking collectives, on_device(): lax.psum((norm_total, kernel_total, offset_total, step_bias_total, rate_t...  38 us
    all_gather x1, blocking collectives, on_device(): lax.all_gather(output_weight, ('dp', 'context'), axis=1, tiled=True)  34.6 us
    all_gather x1, blocking collectives, on_device(): lax.all_gather(shared_projection, ('dp', 'context'), axis=0, tiled=True)  31.7 us
    dot_general x6, matrix products, ssd_local(): jnp.einsum('shtu,suhp->sthp', weights, heads_x, precision=HIGH_ACCURACY)  29.6 us
  transfers between devices with their start and end apart: 15, of which 11 were waited for; matrix products, arithmetic and copies ran while one was open for 18% of the time, Pallas kernels for 0%

commit v1 on v0

v1 whole, which is shorter than its diff:
```python
import functools
import types

import jax
import jax.numpy as jnp
from jax import lax
from jax.experimental import pallas as pl
from jax.experimental.pallas import tpu as pltpu
from jax.sharding import PartitionSpec as P

EPS = 1e-05
F32 = jnp.float32
BF16 = jnp.bfloat16
MESH = pl.DeviceIdType.MESH
LANES = 128
HALO = 16
EDGE = 8


def nn(a, b):
    return lax.dot_general(a, b, (((1,), (0,)), ((), ())), preferred_element_type=F32)


def nt(a, b):
    return lax.dot_general(a, b, (((1,), (1,)), ((), ())), preferred_element_type=F32)


def tn(a, b):
    return lax.dot_general(a, b, (((0,), (0,)), ((), ())), preferred_element_type=F32)


def pieces_of(value, count):
    pieces = []
    for _ in range(count):
        piece = value.astype(BF16)
        pieces.append(piece)
        value = value - piece.astype(F32)
    return pieces


def exact_left(ones, value):
    return sum(nn(ones, piece) for piece in pieces_of(value, 3))


def exact_right(value, ones):
    return sum(nn(piece, ones) for piece in pieces_of(value, 2))


def sigmoid(value):
    return 1.0 / (1.0 + jnp.exp(-value))


def iota(shape, dim):
    return lax.broadcasted_iota(jnp.int32, shape, dim)


def kernel(z, names, *refs):
    m = types.SimpleNamespace(**dict(zip(names, refs)))
    R, T, D, C, H, S = z.R, z.T, z.D, z.C, z.H, z.S
    rp, nd, nc, ntn = z.rp, z.nd, z.nc, z.ntn
    pairs = H // 2
    head = C // H
    V = C + S
    half = T // 2
    d, c, t = lax.axis_index("dp"), lax.axis_index("context"), lax.axis_index("tensor")
    odd = lax.rem(t, 2)
    across = t + 1 - 2 * odd
    far = lax.rem(t + 2, 4) if ntn == 4 else t

    def at_ctx(k):
        return lax.rem(c + k, nc)

    def at_dp(k):
        return lax.rem(d + k, nd)

    def at_ten(k):
        return lax.rem(t + k, ntn)

    def block(dd, cc):
        return pl.ds(pl.multiple_of((dd * nc + cc) * rp, 16), rp)

    def row(r):
        return pl.ds(pl.multiple_of(r * T, 16), T)

    def copy(src, dst, send, recv, dev):
        return pltpu.make_async_remote_copy(
            src_ref=src, dst_ref=dst, send_sem=send, recv_sem=recv, device_id=dev, device_id_type=MESH
        )

    barrier = pltpu.get_barrier_semaphore()
    peers = [(d, at_ctx(k), t) for k in range(1, nc)]
    peers += [(at_dp(k), c, t) for k in range(1, nd)]
    peers += [(d, c, at_ten(k)) for k in range(1, ntn)]
    for peer in peers:
        pl.semaphore_signal(barrier, inc=1, device_id=peer, device_id_type=MESH)
    pl.semaphore_wait(barrier, len(peers))

    wsrc, wall = (m.w0, m.w1), (m.wg0, m.wg1)

    def w_own(part):
        whole = wall[part].at[block(d, c)]
        out = []
        for k in range(1, nc):
            out.append(
                copy(wsrc[part], whole, m.w_send.at[part, k, 0], m.w_recv.at[part, d, c], (d, at_ctx(k), t))
            )
        for k in range(1, nd):
            out.append(
                copy(wsrc[part], whole, m.w_send.at[part, 0, k], m.w_recv.at[part, d, c], (at_dp(k), c, t))
            )
        return out

    def w_pass(part, j):
        cc = at_ctx(nc - j)
        whole = wall[part].at[block(d, cc)]
        return [
            copy(whole, whole, m.w_send.at[part, j, k], m.w_recv.at[part, d, cc], (at_dp(k), c, t))
            for k in range(1, nd)
        ]

    def w_arrived(part, dd, cc):
        whole = wall[part].at[block(dd, cc)]
        copy(wsrc[part], whole, m.w_send.at[part, 0, 0], m.w_recv.at[part, dd, cc], (d, c, t)).wait_recv()

    def w_relay(part):
        for j in range(1, nc):
            w_arrived(part, d, at_ctx(nc - j))
            for one in w_pass(part, j):
                one.start()

    def w_rest(part):
        for k in range(1, nd):
            for j in range(nc):
                w_arrived(part, at_dp(nd - k), at_ctx(nc - j))
        wall[part][block(d, c), :] = wsrc[part][...]

    def w_sent(part):
        for one in w_own(part):
            one.wait_send()
        for j in range(1, nc):
            for one in w_pass(part, j):
                one.wait_send()

    def halo_copy(r):
        return copy(
            m.hid.at[pl.ds(pl.multiple_of(r * T + T - HALO, 16), HALO)],
            m.hh.at[pl.ds(pl.multiple_of(r * HALO, 16), HALO)],
            m.h_send.at[r],
            m.h_recv.at[r],
            (d, c + 1, t),
        )

    for one in w_own(0):
        one.start()

    @pl.when(c < nc - 1)
    def _():
        for r in range(R):
            halo_copy(r).start()

    gain_in = m.ng[0:1, :]

    def normalize(u):
        u = u.astype(F32)
        mean = jnp.sum(u * u, axis=-1, keepdims=True) * (1.0 / z.d_true)
        return (u * lax.rsqrt(mean + EPS)) * gain_in

    @pl.loop(0, R)
    def _(r):
        value = normalize(m.hid[row(r), :]).astype(BF16)
        m.nrm[row(r), :] = value
        m.nrmt[:, row(r)] = jnp.transpose(value)
        m.cott[:, row(r)] = jnp.transpose(m.cot[row(r), :])

    w_relay(0)
    for one in w_own(1):
        one.start()

    @pl.when(c == 0)
    def _():
        m.hh[...] = jnp.zeros_like(m.hh)
        m.sin[...] = jnp.zeros_like(m.sin)

    @pl.when(c == nc - 1)
    def _():
        m.gin[...] = jnp.zeros_like(m.gin)
        m.dce[...] = jnp.zeros_like(m.dce)

    m.sm[t] = jnp.zeros((8, z.WL), F32)
    m.drow[...] = jnp.zeros_like(m.drow)
    m.tot[...] = jnp.zeros_like(m.tot)

    @pl.when(c > 0)
    def _():
        for r in range(R):
            halo_copy(r).wait_recv()

    m.nrmh[...] = normalize(m.hh[...]).astype(BF16)
    w_rest(0)

    def rounded(value):
        return value.astype(BF16).astype(F32)

    halo_v = rounded(nn(m.nrmh[...], m.wg0[:, :V]))
    for r in range(R):
        m.vext[r, 0:EDGE, :] = halo_v[r * HALO + HALO - EDGE : (r + 1) * HALO]

    low_lanes = iota((T, LANES), 1) < head
    lane = iota((T, LANES), 1)
    lower = (iota((T, T), 0) >= iota((T, T), 1)).astype(BF16)
    upper = (iota((T, T), 0) <= iota((T, T), 1)).astype(BF16)
    fold = (iota((C, LANES), 0) // head == iota((C, LANES), 1)).astype(BF16)

    def spread(values):
        return jnp.concatenate(
            [
                jnp.where(low_lanes, values[:, 2 * p : 2 * p + 1], values[:, 2 * p + 1 : 2 * p + 2])
                for p in range(pairs)
            ],
            axis=1,
        )

    def state_copy(r):
        return copy(m.ssend.at[r], m.sin.at[r], m.s_send.at[r], m.s_recv.at[r], (d, c + 1, t))

    def grad_copy(r):
        return copy(m.gsend.at[r], m.gin.at[r], m.g_send.at[r], m.g_recv.at[r], (d, c - 1, t))

    def edge_copy(r):
        return copy(m.dconv.at[r, pl.ds(0, EDGE)], m.dce.at[r], m.e_send.at[r], m.e_recv.at[r], (d, c - 1, t))

    def leads(r):
        run = m.run[row(r), :]
        seg = m.segc[row(r), :]
        last = run[T - 1 : T, :]
        lead = jnp.exp(run) * seg[:, 6:7]
        trail = jnp.exp(last - run) * seg[:, 7:8]
        return lead, trail

    @pl.loop(0, R)
    def _(r):
        acc = nn(m.nrm[row(r), :], m.wg0[...])
        m.vext[r, pl.ds(EDGE, T), :] = rounded(acc[:, :V])
        raw = rounded(acc[:, V : V + LANES])
        seg = m.segc[row(r), :]
        for a in range(0, V, LANES):
            part = slice(a, a + LANES)
            conv = m.vext[r, pl.ds(EDGE, T), part] * m.par[0:1, part] + m.par[4:5, part]
            for j in range(1, z.K):
                conv = conv + m.vext[r, pl.ds(EDGE - j, T), part] * m.par[j : j + 1, part] * seg[:, j - 1 : j]
            logistic = sigmoid(conv)
            m.mix[row(r), part] = (conv * logistic).astype(BF16)
            m.slope[row(r), part] = logistic * (1.0 + conv * (1.0 - logistic))
        pre = raw + m.par[7:8, :LANES]
        step = jnp.maximum(pre, 0.0) + jnp.log1p(jnp.exp(-jnp.abs(pre)))
        m.pre[row(r), :] = pre
        m.step[row(r), :] = step
        run = exact_left(lower, step * m.par[8:9, :LANES])
        m.run[row(r), :] = run
        m.runr[r] = jnp.transpose(run)[0:8, :]
        lead, trail = leads(r)
        scaled = m.mix[row(r), :C].astype(F32) * spread(step)
        m.xs[row(r), :] = scaled.astype(BF16)
        ending = (scaled * spread(trail)).astype(BF16)
        m.fresh[r] = tn(ending, m.mix[row(r), C : C + LANES])

        @pl.when(c == 0)
        def _():
            m.ssend[r] = m.fresh[r].astype(BF16)
            state_copy(r).start()

    w_relay(1)

    @pl.loop(0, R)
    def _(r):
        b, cm = m.mix[row(r), C : C + LANES], m.mix[row(r), C + LANES : V]
        same = (m.segc[row(r), 8:9] == m.segr[pl.ds(r, 1), :]) & (iota((T, T), 0) >= iota((T, T), 1))
        m.scores[...] = jnp.where(same, nt(cm, b), 0.0)
        run = m.run[row(r), :]
        for p in range(pairs):
            part = slice(p * LANES, (p + 1) * LANES)
            both = []
            for h in (2 * p, 2 * p + 1):
                decay = jnp.exp(jnp.minimum(run[:, h : h + 1] - m.runr[r, h : h + 1, :], 0.0))
                both.append(nn((decay * m.scores[...]).astype(BF16), m.xs[row(r), part]))
            m.ins[row(r), part] = jnp.where(low_lanes, both[0], both[1])

        @pl.when(c > 0)
        def _():
            state_copy(r).wait_recv()

            @pl.when(c < nc - 1)
            def _():
                lead, _ = leads(r)
                for h in range(H):
                    here = slice(h * head, (h + 1) * head)
                    keep = lead[T - 1 : T, h : h + 1]
                    m.ssend[r, here, :] = (
                        m.fresh[r, here, :] + keep * m.sin[r, here, :].astype(F32)
                    ).astype(BF16)
                state_copy(r).start()

    w_rest(1)

    def sums_copy(r, k):
        return copy(
            m.sums.at[t, r], m.sums.at[t, r], m.x_send.at[r, k], m.x_recv.at[r, t], (d, c, at_ten(k))
        )

    def sums_arrived(r, who):
        copy(
            m.sums.at[who, r], m.sums.at[who, r], m.x_send.at[r, 0], m.x_recv.at[r, who], (d, c, t)
        ).wait_recv()

    def mine(r):
        return pl.ds(pl.multiple_of(r * T + odd * half, 16), half)

    def theirs(r):
        return pl.ds(pl.multiple_of(r * T + (1 - odd) * half, 16), half)

    def near_copy(a, r):
        return copy(m.as_.at[a, r], m.ar_.at[a, r], m.a_send.at[a, r], m.a_recv.at[a, r], (d, c, across))

    def far_copy(a, r):
        return copy(m.bs_.at[a, r], m.br_.at[a, r], m.b_send.at[a, r], m.b_recv.at[a, r], (d, c, far))

    def back_copy(a, r):
        out = (m.out, m.ing)[a].at[mine(r)]
        return copy(out, out, m.c_send.at[a, r], m.c_recv.at[a, r], (d, c, across))

    def back_arrived(a, r):
        out = (m.out, m.ing)[a].at[theirs(r)]
        copy(out, out, m.c_send.at[a, r], m.c_recv.at[a, r], (d, c, across)).wait_recv()

    def chip_sum(a, r):
        near_copy(a, r).wait_recv()
        m.bs_[a, r] = (m.keep[a, r].astype(F32) + m.ar_[a, r].astype(F32)).astype(BF16)
        if ntn == 4:
            far_copy(a, r).start()

    def full_sum(a, r):
        total = m.bs_[a, r].astype(F32)
        if ntn == 4:
            far_copy(a, r).wait_recv()
            total = total + m.br_[a, r].astype(F32)
        return total

    @pl.loop(0, R)
    def _(r):
        b, cm = m.mix[row(r), C : C + LANES], m.mix[row(r), C + LANES : V]
        lead, _ = leads(r)
        carried = nt(cm, m.sin[r]) * spread(lead)
        m.ys[row(r), :] = carried
        ssd = m.ins[row(r), :] + carried + m.par[6:7, :C] * m.mix[row(r), :C].astype(F32)
        m.ssd[row(r), :] = ssd
        gate = rounded(nn(m.nrm[row(r), :], m.wg1[:, :C]))
        m.zv[row(r), :] = gate.astype(BF16)
        gated = ssd * (gate * sigmoid(gate))
        m.gated[row(r), :C] = gated
        dy = nn(m.cot[row(r), :], m.wg1[:, C:])
        m.dy[row(r), :] = dy
        gain = m.par[5:6, :C]
        squares = jnp.sum(gated * gated, axis=-1, keepdims=True)
        inner = jnp.sum(dy * gain * gated, axis=-1, keepdims=True)
        both = jnp.where(lane == 0, squares, jnp.where(lane == 1, inner, 0.0))
        m.sums[t, r] = jnp.transpose(both)[0:8, :]
        for k in range(1, ntn):
            sums_copy(r, k).start()
        m.yg[row(r), :] = (gated * gain).astype(BF16)
        m.as_[0, r] = nt(m.yg[theirs(r), :], m.wg1[:, C:]).astype(BF16)
        near_copy(0, r).start()
        m.keep[0, r] = nt(m.yg[mine(r), :], m.wg1[:, C:])

    @pl.loop(0, R)
    def _(r):
        chip_sum(0, r)
        for k in range(1, ntn):
            sums_arrived(r, at_ten(k))
        total = m.sums[0, r]
        for who in range(1, ntn):
            total = total + m.sums[who, r]
        m.tot[0:8, :] = total
        columns = jnp.transpose(m.tot[...])
        scale = lax.rsqrt(columns[:, 0:1] * (1.0 / (C * ntn)) + EPS)
        m.rms[row(r), :] = jnp.broadcast_to(scale, (T, LANES))
        inner = columns[:, 1:2] * (1.0 / (C * ntn)) * scale * scale * scale
        gated, dy, gate, ssd = m.gated[row(r), :C], m.dy[row(r), :], m.zv[row(r), :].astype(F32), m.ssd[row(r), :]
        gain = m.par[5:6, :C]
        normal = gated * scale
        m.sm[t, 5:6, :C] += jnp.sum(dy * normal, axis=0, keepdims=True)
        m.yg[row(r), :] = (normal * gain).astype(BF16)
        d_gated = scale * dy * gain - gated * inner
        logistic = sigmoid(gate)
        m.dz[row(r), :] = (d_gated * ssd * (logistic * (1.0 + gate * (1.0 - logistic)))).astype(BF16)
        d_ssd = d_gated * (gate * logistic)
        m.ssd[row(r), :] = d_ssd
        lead, _ = leads(r)
        weighted = (d_ssd * spread(lead)).astype(BF16)
        m.wds[row(r), :] = weighted
        m.local[r] = tn(weighted, m.mix[row(r), C + LANES : V])

        @pl.when(c == nc - 1)
        def _():
            m.gsend[r] = m.local[r].astype(BF16)
            if nc > 1:
                grad_copy(r).start()

    gall, gyr, gzs, gzr = (m.ga0, m.ga1), (m.gy0, m.gy1), (m.gz0, m.gz1), (m.gr0, m.gr1)
    gwide = (z.G0, 2 * C)

    def rs_dp(part, j, k):
        cc = at_ctx(j)
        return copy(
            gall[part].at[block(at_dp(k), cc)],
            gyr[part].at[k - 1, pl.ds(pl.multiple_of(cc * rp, 16), rp)],
            m.ry_send.at[part, j, k - 1],
            m.ry_recv.at[part, j, k - 1],
            (at_dp(k), c, t),
        )

    def rs_ctx(part, j):
        cc = at_ctx(j)
        return copy(
            gzs[part].at[pl.ds(pl.multiple_of(cc * rp, 16), rp)],
            gzr[part].at[c],
            m.rz_send.at[part, j],
            m.rz_recv.at[part, c],
            (d, cc, t),
        )

    def rs_arrived(part, cc):
        copy(gzr[part].at[cc], gzr[part].at[cc], m.rz_send.at[part, 0], m.rz_recv.at[part, cc], (d, c, t)).wait_recv()

    order = [j for j in range(1, nc)] + [0]

    def rs_start(part):
        for j in order:
            for k in range(1, nd):
                rs_dp(part, j, k).start()

    def rs_middle(part):
        for j in order:
            cc = at_ctx(j)
            total = gall[part][block(d, cc), :].astype(F32)
            for k in range(1, nd):
                rs_dp(part, j, k).wait_recv()
                total = total + gyr[part][k - 1, pl.ds(pl.multiple_of(cc * rp, 16), rp), :].astype(F32)
            if j == 0:
                gzr[part][c] = total.astype(BF16)
            else:
                gzs[part][pl.ds(pl.multiple_of(cc * rp, 16), rp), :] = total.astype(BF16)
                rs_ctx(part, j).start()

    def rs_end(part):
        for k in range(1, nc):
            rs_arrived(part, at_ctx(k))
        total = gzr[part][0].astype(F32)
        for cc in range(1, nc):
            total = total + gzr[part][cc].astype(F32)
        return total

    def rs_sent(part):
        for j in range(nc):
            for k in range(1, nd):
                rs_dp(part, j, k).wait_send()
            if j:
                rs_ctx(part, j).wait_send()

    m.ga1[:, C:] = nn(m.cott[...], m.yg[...]).astype(BF16)
    m.ga1[:, :C] = nn(m.nrmt[...], m.dz[...]).astype(BF16)
    rs_start(1)

    @pl.loop(0, R)
    def _(r):
        b, cm = m.mix[row(r), C : C + LANES], m.mix[row(r), C + LANES : V]
        same = (m.segc[row(r), 8:9] == m.segr[pl.ds(r, 1), :]) & (iota((T, T), 0) <= iota((T, T), 1))
        m.scores[...] = jnp.where(same, nt(b, cm), 0.0)
        run = m.run[row(r), :]
        losses = jnp.zeros((T, LANES), F32)
        for p in range(pairs):
            part = slice(p * LANES, (p + 1) * LANES)
            ds_pair = m.ssd[row(r), part].astype(BF16)
            xs_pair = m.xs[row(r), part]
            both = []
            for h in (2 * p, 2 * p + 1):
                pick = low_lanes if h % 2 == 0 else ~low_lanes
                decay = jnp.exp(jnp.minimum(m.runr[r, h : h + 1, :] - run[:, h : h + 1], 0.0))
                weight = decay * m.scores[...]
                both.append(nn(weight.astype(BF16), ds_pair))
                d_weight = nt(jnp.where(pick, xs_pair, jnp.zeros_like(xs_pair)), ds_pair)
                flow = d_weight * weight
                if h == 0:
                    m.dsc[...] = d_weight * decay
                else:
                    m.dsc[...] += d_weight * decay
                losses = jnp.where(lane == h, jnp.sum(flow, axis=1, keepdims=True), losses)
                m.drow[h : h + 1, :] = jnp.sum(flow, axis=0, keepdims=True)
            m.ins[row(r), part] = jnp.where(low_lanes, both[0], both[1])
        d_scores = jnp.where(same, m.dsc[...], 0.0).astype(BF16)
        m.gated[row(r), :LANES] = nn(d_scores, cm)
        m.gated[row(r), LANES:S] = tn(d_scores, b)
        m.drun[row(r), :] = (
            jnp.transpose(m.drow[...])
            - losses
            + exact_right(m.ssd[row(r), :] * m.ys[row(r), :], fold)
        )

        @pl.when(c < nc - 1)
        def _():
            grad_copy(r).wait_recv()

            @pl.when(c > 0)
            def _():
                lead, _ = leads(r)
                for h in range(H):
                    here = slice(h * head, (h + 1) * head)
                    keep = lead[T - 1 : T, h : h + 1]
                    m.gsend[r, here, :] = (
                        m.local[r, here, :] + keep * m.gin[r, here, :].astype(F32)
                    ).astype(BF16)
                grad_copy(r).start()

    rs_middle(1)

    @pl.loop(0, R)
    def _(r):
        value = m.hid[mine(r), :].astype(F32) + m.rms[mine(r), 0:1] * full_sum(0, r)
        m.out[mine(r), :] = value.astype(BF16)
        back_copy(0, r).start()

    @pl.loop(0, R)
    def _(r):
        b, cm = m.mix[row(r), C : C + LANES], m.mix[row(r), C + LANES : V]
        lead, trail = leads(r)
        grad = m.gin[r]
        trailing = spread(trail)
        reach = nt(b, grad)
        scaled = m.xs[row(r), :].astype(F32) * trailing
        through = exact_right(scaled * reach, fold)
        d_run = m.drun[row(r), :] - through
        ends = jnp.sum(through, axis=0, keepdims=True)
        for h in range(H):
            here = slice(h * head, (h + 1) * head)
            joint = m.gin[r, here, :].astype(F32) * m.sin[r, here, :].astype(F32)
            joint = jnp.sum(jnp.sum(joint, axis=0, keepdims=True), axis=1, keepdims=True)
            ends = ends + jnp.where(lane[0:1] == h, joint * lead[T - 1 : T, :], 0.0)
        d_run = d_run + jnp.where(iota((T, LANES), 0) == T - 1, ends, 0.0)
        d_growth = exact_left(upper, d_run)
        step = m.step[row(r), :]
        d_xs = m.ins[row(r), :] + trailing * reach
        x = m.mix[row(r), :C].astype(F32)
        d_ssd = m.ssd[row(r), :]
        rate = m.par[8:9, :LANES]
        d_step = exact_right(d_xs * x, fold) + rate * d_growth
        m.sm[t, 7:8, LANES : 2 * LANES] += jnp.sum(step * d_growth, axis=0, keepdims=True) * rate
        m.sm[t, 7:8, 3 * LANES : 3 * LANES + C] += jnp.sum(d_ssd * x, axis=0, keepdims=True)
        d_pre = d_step * sigmoid(m.pre[row(r), :])
        m.sm[t, 7:8, :LANES] += jnp.sum(d_pre, axis=0, keepdims=True)
        m.dv[row(r), V:] = jnp.where(lane < H, d_pre, 0.0).astype(BF16)
        m.dconv[r, pl.ds(0, T), :C] = (d_xs * spread(step) + m.par[6:7, :C] * d_ssd) * m.slope[row(r), :C]
        m.dconv[r, pl.ds(0, T), C : C + LANES] = (
            m.gated[row(r), :LANES] + nn(scaled.astype(BF16), grad)
        ) * m.slope[row(r), C : C + LANES]
        m.dconv[r, pl.ds(0, T), C + LANES :] = (
            m.gated[row(r), LANES:S] + nn(m.wds[row(r), :], m.sin[r])
        ) * m.slope[row(r), C + LANES :]

        @pl.when(c > 0)
        def _():
            edge_copy(r).start()

        seg = m.segc[row(r), :]
        for a in range(0, V, LANES):
            part = slice(a, a + LANES)
            d_conv = m.dconv[r, pl.ds(0, T), part]
            m.sm[t, 4:5, part] += jnp.sum(d_conv, axis=0, keepdims=True)
            m.sm[t, 0:1, part] += jnp.sum(d_conv * m.vext[r, pl.ds(EDGE, T), part], axis=0, keepdims=True)
            for j in range(1, z.K):
                m.sm[t, j : j + 1, part] += jnp.sum(
                    d_conv * m.vext[r, pl.ds(EDGE - j, T), part] * seg[:, j - 1 : j], axis=0, keepdims=True
                )

    @pl.loop(0, R)
    def _(r):
        @pl.when(c < nc - 1)
        def _():
            edge_copy(r).wait_recv()

        m.dconv[r, pl.ds(T, EDGE), :] = m.dce[r]
        seg = m.segc[row(r), :]
        for a in range(0, V, LANES):
            part = slice(a, a + LANES)
            d_v = m.dconv[r, pl.ds(0, T), part] * m.par[0:1, part]
            for j in range(1, z.K):
                d_v = d_v + m.dconv[r, pl.ds(j, T), part] * m.par[j : j + 1, part] * seg[:, j + 2 : j + 3]
            m.dv[row(r), part] = d_v.astype(BF16)

        def d_normed(rows):
            return nt(m.dv[rows, :], m.wg0[...]) + nt(m.dz[rows, :], m.wg1[:, :C])

        def unit_of(rows):
            u = m.hid[rows, :].astype(F32)
            mean = jnp.sum(u * u, axis=-1, keepdims=True) * (1.0 / z.d_true)
            return u * lax.rsqrt(mean + EPS)

        value = d_normed(theirs(r))
        m.as_[1, r] = value.astype(BF16)
        near_copy(1, r).start()
        m.sm[t, 6:7, :D] += jnp.sum(value * unit_of(theirs(r)), axis=0, keepdims=True)
        value = d_normed(mine(r))
        m.keep[1, r] = value
        m.sm[t, 6:7, :D] += jnp.sum(value * unit_of(mine(r)), axis=0, keepdims=True)

    width = S // ntn
    m.ga0[:, :C] = nn(m.nrmt[...], m.dv[:, :C]).astype(BF16)
    m.ga0[:, C : C + LANES] = nn(m.nrmt[...], m.dv[:, V:]).astype(BF16)

    def share_copy():
        return copy(m.shs, m.shr, m.sh_send.at[0], m.sh_recv.at[0], (d, c, across))

    quarters = [m.dv[:, C + k * width : C + (k + 1) * width] for k in range(ntn)]
    for parity in range(2):
        chosen = jnp.concatenate(quarters[parity::2], axis=1)
        value = nn(m.nrmt[...], chosen)

        @pl.when(odd == parity)
        def _():
            m.shk[...] = value

        @pl.when(odd != parity)
        def _():
            m.shs[...] = value.astype(BF16)

    share_copy().start()

    @pl.loop(0, R)
    def _(r):
        chip_sum(1, r)

    share_copy().wait_recv()
    m.ga0[:, C + LANES : C + LANES + z.Q] = (m.shk[...] + m.shr[...].astype(F32)).astype(BF16)
    rs_start(0)

    def small_ten(k):
        return copy(m.sm.at[t], m.sm.at[t], m.st_send.at[k], m.st_recv.at[t], (d, c, at_ten(k)))

    def small_dp(k):
        return copy(m.sd.at[d], m.sd.at[d], m.sd_send.at[k], m.sd_recv.at[d], (at_dp(k), c, t))

    def small_ctx(k):
        return copy(m.sc.at[c], m.sc.at[c], m.sc_send.at[k], m.sc_recv.at[c], (d, at_ctx(k), t))

    def arrived(buf, sems, who):
        copy(buf.at[who], buf.at[who], sems.at[who], sems.at[who], (d, c, t)).wait_recv()

    for k in range(1, ntn):
        small_ten(k).start()
    for k in range(1, ntn):
        arrived(m.sm, m.st_recv, at_ten(k))
    common = m.sm[0]
    for who in range(1, ntn):
        common = common + m.sm[who]
    rows8, lanes8 = iota((8, z.WL), 0), iota((8, z.WL), 1)
    shared_here = (rows8 == 6) | ((rows8 < 5) & (lanes8 >= C))
    m.sd[d] = jnp.where(shared_here, common, m.sm[t])
    for k in range(1, nd):
        small_dp(k).start()

    @pl.loop(0, R)
    def _(r):
        u = m.hid[mine(r), :].astype(F32)
        mean = jnp.sum(u * u, axis=-1, keepdims=True) * (1.0 / z.d_true)
        scale = lax.rsqrt(mean + EPS)
        unit = u * scale
        d_unit = full_sum(1, r) * gain_in
        inner = jnp.sum(d_unit * unit, axis=-1, keepdims=True) * (1.0 / z.d_true)
        value = m.cot[mine(r), :].astype(F32) + scale * (d_unit - unit * inner)
        m.ing[mine(r), :] = value.astype(BF16)
        back_copy(1, r).start()

    rs_middle(0)

    for k in range(1, nd):
        arrived(m.sd, m.sd_recv, at_dp(k))
    total = m.sd[0]
    for who in range(1, nd):
        total = total + m.sd[who]
    m.sc[c] = total
    for k in range(1, nc):
        small_ctx(k).start()

    m.gw1[...] = rs_end(1)
    m.gw0[...] = rs_end(0)

    if ntn == 4:
        def last_copy():
            return copy(m.ls, m.lr, m.sh_send.at[1], m.sh_recv.at[1], (d, c, far))

        m.ls[...] = m.gw0[:, C + LANES : C + LANES + z.Q]
        last_copy().start()

    for k in range(1, nc):
        arrived(m.sc, m.sc_recv, at_ctx(k))
    total = m.sc[0]
    for who in range(1, nc):
        total = total + m.sc[who]
    m.small[...] = total

    if ntn == 4:
        last_copy().wait_recv()
        m.gw0[:, C + LANES : C + LANES + z.Q] = m.ls[...] + m.lr[...]
        last_copy().wait_send()

    for a in range(2):
        for r in range(R):
            back_arrived(a, r)
            back_copy(a, r).wait_send()
            near_copy(a, r).wait_send()
            if ntn == 4:
                far_copy(a, r).wait_send()
    for part in range(2):
        w_sent(part)
        rs_sent(part)
    for r in range(R):
        for k in range(1, ntn):
            sums_copy(r, k).wait_send()

        @pl.when(c < nc - 1)
        def _():
            halo_copy(r).wait_send()
            state_copy(r).wait_send()

        @pl.when(c > 0)
        def _():
            grad_copy(r).wait_send()
            edge_copy(r).wait_send()

    share_copy().wait_send()
    for k in range(1, ntn):
        small_ten(k).wait_send()
    for k in range(1, nd):
        small_dp(k).wait_send()
    for k in range(1, nc):
        small_ctx(k).wait_send()


def on_device(z, hidden_in, segment_ids, norm_gain, head_projection, shared_projection, step_projection,
              conv_heads, bias_heads, conv_shared, bias_shared, step_bias, log_decay, skip_gain, gate_gain,
              output_weight, out_cotangent):
    R, T, D, C, H, S = z.R, z.T, z.D, z.C, z.H, z.S
    rp, nd, nc, ntn = z.rp, z.nd, z.nc, z.ntn
    V = C + S
    blocks = nd * nc

    def widen(value):
        if rp == z.rows:
            return value
        value = value.reshape(value.shape[:-1] + (blocks, z.rows))
        value = jnp.pad(value, [(0, 0)] * (value.ndim - 1) + [(0, rp - z.rows)])
        return value.reshape(value.shape[:-2] + (D,))

    def narrow(value):
        if rp == z.rows:
            return value
        return value.reshape(value.shape[:-1] + (blocks, rp))[..., : z.rows].reshape(value.shape[:-1] + (z.d_true,))

    hid = widen(hidden_in.reshape(R * T, z.d_true))
    cot = widen(out_cotangent.reshape(R * T, z.d_true))
    w0 = jnp.concatenate(
        [head_projection[:, 1], shared_projection, jnp.pad(step_projection, ((0, 0), (0, LANES - H)))], axis=1
    )
    w1 = jnp.concatenate([head_projection[:, 0], output_weight.T], axis=1)
    if rp != z.rows:
        w0 = jnp.pad(w0, ((0, rp - z.rows), (0, 0)))
        w1 = jnp.pad(w1, ((0, rp - z.rows), (0, 0)))
    begin = lax.axis_index("context") * T
    margin = z.K - 1
    ids = segment_ids.reshape(R, segment_ids.shape[-1])
    ids = jnp.pad(ids, ((0, 0), (margin, 0)), constant_values=-1)
    ids = jnp.pad(ids, ((0, 0), (0, margin)), constant_values=-2)
    ids = lax.dynamic_slice_in_dim(ids, begin, T + 2 * margin, 1)
    now = ids[:, margin : margin + T]
    columns = [now == ids[:, margin - j : margin - j + T] for j in range(1, z.K)]
    columns += [now == ids[:, margin + j : margin + j + T] for j in range(1, z.K)]
    columns += [now == ids[:, margin - 1 : margin], now == now[:, T - 1 : T]]
    columns = [value.astype(F32) for value in columns] + [now.astype(F32)]
    columns += [jnp.zeros((R, T), F32)] * (16 - len(columns))
    segc = jnp.stack(columns, axis=-1).reshape(R * T, 16)
    segr = jnp.pad(now.astype(F32), ((0, -R % 8), (0, 0)))

    def line(value):
        value = value.reshape(-1, value.shape[-1])
        return jnp.pad(value, ((0, 0), (0, V - value.shape[-1])))

    par = jnp.concatenate(
        [
            jnp.concatenate([conv_heads, conv_shared], axis=1),
            jnp.concatenate([bias_heads, bias_shared])[None],
            line(gate_gain),
            line(jnp.repeat(skip_gain, C // H)),
            line(step_bias),
            line(-jnp.exp(log_decay)),
        ],
        axis=0,
    )
    par = jnp.pad(par, ((0, 16 - par.shape[0]), (0, 0)))
    ng = jnp.broadcast_to(widen(norm_gain[None]), (8, D))

    dma, vmem = pltpu.SemaphoreType.DMA, pltpu.VMEM
    N = R * T
    half = T // 2
    k0 = max(nd - 1, 1)
    ins = dict(hid=hid, cot=cot, w0=w0, w1=w1, segc=segc, segr=segr, par=par, ng=ng)
    outs = dict(
        out=jax.ShapeDtypeStruct((N, D), BF16),
        ing=jax.ShapeDtypeStruct((N, D), BF16),
        gw0=jax.ShapeDtypeStruct((rp, z.G0), F32),
        gw1=jax.ShapeDtypeStruct((rp, 2 * C), F32),
        small=jax.ShapeDtypeStruct((8, z.WL), F32),
    )
    scratch = dict(
        wg0=vmem((D, V + LANES), BF16), wg1=vmem((D, 2 * C), BF16),
        hh=vmem((R * HALO, D), BF16), nrmh=vmem((R * HALO, D), BF16),
        nrm=vmem((N, D), BF16), nrmt=vmem((D, N), BF16), cott=vmem((D, N), BF16),
        vext=vmem((R, EDGE + T, V), F32), mix=vmem((N, V), BF16), slope=vmem((N, V), F32),
        pre=vmem((N, LANES), F32), step=vmem((N, LANES), F32), run=vmem((N, LANES), F32),
        runr=vmem((R, 8, T), F32), xs=vmem((N, C), BF16),
        fresh=vmem((R, C, LANES), F32), local=vmem((R, C, LANES), F32),
        ssend=vmem((R, C, LANES), BF16), sin=vmem((R, C, LANES), BF16),
        gsend=vmem((R, C, LANES), BF16), gin=vmem((R, C, LANES), BF16),
        scores=vmem((T, T), F32), dsc=vmem((T, T), F32), drow=vmem((LANES, T), F32), tot=vmem((LANES, T), F32),
        ins=vmem((N, C), F32), ys=vmem((N, C), F32), ssd=vmem((N, C), F32), zv=vmem((N, C), BF16),
        gated=vmem((N, max(C, S)), F32), dy=vmem((N, C), F32),
        yg=vmem((N, C), BF16), dz=vmem((N, C), BF16), wds=vmem((N, C), BF16),
        rms=vmem((N, LANES), F32), sums=vmem((ntn, R, 8, T), F32),
        as_=vmem((2, R, half, D), BF16), ar_=vmem((2, R, half, D), BF16),
        bs_=vmem((2, R, half, D), BF16), br_=vmem((2, R, half, D), BF16), keep=vmem((2, R, half, D), F32),
        ga0=vmem((D, z.G0), BF16), ga1=vmem((D, 2 * C), BF16),
        gy0=vmem((k0, nc * rp, z.G0), BF16), gy1=vmem((k0, nc * rp, 2 * C), BF16),
        gz0=vmem((nc * rp, z.G0), BF16), gz1=vmem((nc * rp, 2 * C), BF16),
        gr0=vmem((nc, rp, z.G0), BF16), gr1=vmem((nc, rp, 2 * C), BF16),
        drun=vmem((N, LANES), F32),
        dconv=vmem((R, T + EDGE, V), F32), dce=vmem((R, EDGE, V), F32), dv=vmem((N, V + LANES), BF16),
        shs=vmem((D, z.Q), BF16), shr=vmem((D, z.Q), BF16), shk=vmem((D, z.Q), F32),
        ls=vmem((rp, z.Q), F32), lr=vmem((rp, z.Q), F32),
        sm=vmem((ntn, 8, z.WL), F32), sd=vmem((nd, 8, z.WL), F32), sc=vmem((nc, 8, z.WL), F32),
        w_send=dma((2, nc, nd)), w_recv=dma((2, nd, nc)), h_send=dma((R,)), h_recv=dma((R,)),
        s_send=dma((R,)), s_recv=dma((R,)), g_send=dma((R,)), g_recv=dma((R,)), e_send=dma((R,)), e_recv=dma((R,)),
        x_send=dma((R, ntn)), x_recv=dma((R, ntn)),
        a_send=dma((2, R)), a_recv=dma((2, R)), b_send=dma((2, R)), b_recv=dma((2, R)),
        c_send=dma((2, R)), c_recv=dma((2, R)),
        ry_send=dma((2, nc, k0)), ry_recv=dma((2, nc, k0)), rz_send=dma((2, nc)), rz_recv=dma((2, nc)),
        sh_send=dma((2,)), sh_recv=dma((2,)),
        st_send=dma((ntn,)), st_recv=dma((ntn,)), sd_send=dma((nd,)), sd_recv=dma((nd,)),
        sc_send=dma((nc,)), sc_recv=dma((nc,)),
    )
    names = list(ins) + list(outs) + list(scratch)
    whole = pl.BlockSpec(memory_space=pltpu.VMEM)
    out, ing, gw0, gw1, small = pl.pallas_call(
        functools.partial(kernel, z, names),
        out_shape=list(outs.values()),
        in_specs=[whole] * len(ins),
        out_specs=[whole] * len(outs),
        scratch_shapes=list(scratch.values()),
        compiler_params=pltpu.CompilerParams(
            collective_id=0, has_side_effects=True, vmem_limit_bytes=z.limit
        ),
    )(*ins.values())

    block_out = narrow(out).reshape(hidden_in.shape)
    input_grad = narrow(ing).reshape(hidden_in.shape)
    gw0, gw1 = gw0[: z.rows], gw1[: z.rows]
    grad_heads = jnp.stack([gw1[:, :C], gw0[:, :C]], axis=1)
    rank = lax.axis_index("tensor")
    width = S // ntn
    grad_shared = lax.dynamic_slice_in_dim(gw0, C + LANES + (rank // 2) * width, width, 1)
    grad_step = gw0[:, C : C + H]
    skip = small[7, 3 * LANES : 3 * LANES + C].reshape(H, C // H).sum(axis=1)
    return (
        block_out,
        input_grad,
        narrow(small[6, :D]),
        grad_heads,
        grad_shared,
        grad_step,
        small[0 : z.K, :C],
        small[4, :C],
        small[0 : z.K, C:V],
        small[4, C:V],
        small[7, :H],
        small[7, LANES : LANES + H],
        skip,
        small[5, :C],
        gw1[:, C:].T,
    )


def solution(mesh):
    nd, nc, ntn = (mesh.shape[name] for name in ("dp", "context", "tensor"))

    def body(*args):
        hidden, heads, shared = args[0], args[3], args[4]
        micro, seqs, tokens, width = hidden.shape
        rows = heads.shape[0]
        rp = -(-rows // 16) * 16
        inner = heads.shape[2]
        z = types.SimpleNamespace(
            R=micro * seqs, T=tokens, d_true=width, D=rp * nd * nc, rows=rows, rp=rp, nd=nd, nc=nc, ntn=ntn,
            C=inner, H=args[10].shape[0], S=shared.shape[1], K=args[6].shape[0],
            Q=shared.shape[1] // 2, G0=inner + LANES + shared.shape[1] // 2, limit=62 << 20,
        )
        z.WL = max(inner + z.S, z.D, 3 * LANES + inner)
        return on_device(z, *args)

    return jax.shard_map(
        body,
        mesh=mesh,
        in_specs=(
            P(None, "dp", "context", None),
            P(None, "dp", None),
            P(),
            P(("dp", "context"), None, "tensor"),
            P(("dp", "context"), None),
            P(("dp", "context"), "tensor"),
            P(None, "tensor"),
            P("tensor"),
            P(),
            P(),
            P("tensor"),
            P("tensor"),
            P("tensor"),
            P("tensor"),
            P("tensor", ("dp", "context")),
            P(None, "dp", "context", None),
        ),
        out_specs=(
            P(None, "dp", "context", None),
            P(None, "dp", "context", None),
            P(),
            P(("dp", "context"), None, "tensor"),
            P(("dp", "context"), "tensor"),
            P(("dp", "context"), "tensor"),
            P(None, "tensor"),
            P("tensor"),
            P(),
            P(),
            P("tensor"),
            P("tensor"),
            P("tensor"),
            P("tensor"),
            P("tensor", ("dp", "context")),
        ),
        check_vma=False,
    )
```

time: 925 us -> 164 us (0.18)
  waiting for transfers between devices: 397 us -> 0 us
  blocking collectives: 167 us -> 0 us
  Pallas kernels: 0 us -> 129 us
  other arithmetic: 124 us -> 4.36 us
  matrix products: 99.5 us -> 0 us
  local copies, waits for them, and re-layouts: 99.8 us -> 26.6 us
  between operations: 16.9 us -> 0.84 us
    unnamed x14 -> x0, waiting for transfers between devices: 191 us -> none
    psum x2 -> x0, waiting for transfers between devices: 144 us -> none  [the longest x1 120 us: on_device(): branch_result = lax.psum(partial_output, 'tensor')]
    pallas_call x0 -> x1, Pallas kernels: none -> 129 us  [on_device(): pl.pallas_call(functools.partial(kernel, z, names), out_shape=list(outs.v...]
    all_gather x5 -> x0, blocking collectives: 116 us -> none  [the longest x1 34.6 us: on_device(): lax.all_gather(output_weight, ('dp', 'context'), axis=1, tiled=True)]
    dot_general x42 -> x0, matrix products: 99.5 us -> none  [the longest x6 29.6 us: ssd_local(): jnp.einsum('shtu,suhp->sthp', weights, heads_x, precision=HIGH_ACCURACY)]
    another operation x17 -> x1, other arithmetic: 54.9 us -> 0.04 us  [on_device(): grad_heads = jnp.stack([gw1[:, :C], gw0[:, :C]], axis=1)]
    psum x3 -> x0, blocking collectives: 51.6 us -> none  [the longest x1 38 us: on_device(): lax.psum((norm_total, kernel_total, offset_total, step_bias_total, rate_t...]
    all_gather x5 -> x0, waiting for transfers between devices: 41.2 us -> none  [the longest x4 41.2 us: prefix(): pieces = jax.tree.map(lambda part: lax.all_gather(part, axis), value)]
  transfers between devices with their start and end apart: 15 -> 0, of which waited for: 11 -> 0; matrix products, arithmetic and copies ran while one was open for 18% -> 0% of each run, Pallas kernels for 0% -> 0%
where the time goes in v1:
time: 164 us; the launch traced here: 161 us
  Pallas kernels  129 us (79%)
  local copies, waits for them, and re-layouts  26.6 us (16%)
  other arithmetic  4.36 us (3%)
    pallas_call x1, Pallas kernels, on_device(): pl.pallas_call(functools.partial(kernel, z, names), out_shape=list(outs.v...  129 us
    unnamed x23, local copies, waits for them, and re-layouts  6.29 us

profile of v1, /device:TPU:0, one launch (start us, length us, event | category | flops | bytes accessed | tf_op | source)
XLA Modules:
  0.0 161.3 jit_solution(5645664331668369928)
XLA Ops:
  2.7 0.7 pad_maximum_fusion.3
  3.4 0.7 broadcast_in_dim.13
  4.3 0.7 pad_maximum_fusion.2
  5.0 0.7 reshape.87
  7.4 1.3 broadcast_in_dim.14.refs_7_
  8.7 0.8 copy.62
  9.8 1.3 fusion.4
  12.5 1.0 copy.64.refs_4_
  13.5 129.5 %shard_map.271 = (bf16[1024,768]{1,0:T(8,128)(2,1)}, bf16[1024,768]{1,0:T(8,128)(2,1)}, f32[96,640]{1,0:T(8,128)}, f32[96,768]{1,0:T(8,128)}, f32[8,768]{1,0:T(8,128)}) custom-call(bf16[1024,768]{1,0:T(8,128)(2,1)} %bitcast.70, bf16[1024,768]{1,0:T(8,128)(2,1)} %bitcast.71, bf16[96,768]{1,0:T(8,128)(2,1)} %fusion.1.refs_2_, ...), custom_call_target="tpu_custom_call" | custom-call | tf_op jit(solution)/shard_map/pallas_call | solution.py:859
  142.9 1.4 slice.91
  144.3 1.2 slice_bitcast_fusion.3
  145.5 1.3 slice.90
  146.8 1.3 slice_reduce_fusion
  148.1 1.3 slice.88
  149.4 1.4 slice_reduce_fusion.3
  151.5 0.9 constant_dynamic-slice_fusion
  152.4 0.7 copy.66
  153.1 0.8 slice.87
  153.9 0.9 slice_bitcast_fusion.1
  155.5 1.7 %slice_bitcast_fusion = (f32[384,96]{0,1:T(8,128)}, f32[96,1,384]{2,0,1:T(8,128)S(1)}) fusion(f32[96,768]{1,0:T(8,128)} %get-tuple-element.23), kind=kLoop, calls=%fused_computation.5 | loop fusion | bytes 589824 | tf_op jit(solution)/shard_map/transpose | solution.py:894
  157.2 0.9 copy.65
  158.1 1.1 copy.83
  159.3 0.8 copy-done
  160.1 1.1 copy.84
  (42 shorter events, 6.8 us)
Async XLA Ops:
  0.6 10.4 %copy-start.2 = (bf16[384,96]{0,1:T(8,128)(2,1)S(1)}, bf16[384,96]{0,1:T(8,128)(2,1)}, u32[]{:S(2)}) copy-start(bf16[384,96]{0,1:T(8,128)(2,1)} %param.30) | copy-start | bytes 221188
  0.7 11.1 %copy-start.3 = (bf16[96,256]{1,0:T(8,128)(2,1)S(1)}, bf16[96,256]{1,0:T(8,128)(2,1)}, u32[]{:S(2)}) copy-start(bf16[96,256]{1,0:T(8,128)(2,1)} %param.20) | copy-start | bytes 147460
  142.9 15.2 %copy-start.1 = (bf16[1024,768]{1,0:T(8,128)(2,1)S(1)}, bf16[1024,768]{1,0:T(8,128)(2,1)}, u32[]{:S(2)}) copy-start(bf16[1024,768]{1,0:T(8,128)(2,1)} %get-tuple-element.20) | copy-start | bytes 4718596
  158.1 2.0 %copy-start = (bf16[1024,768]{1,0:T(8,128)(2,1)S(1)}, bf16[1024,768]{1,0:T(8,128)(2,1)}, u32[]{:S(2)}) copy-start(bf16[1024,768]{1,0:T(8,128)(2,1)} %get-tuple-element.21) | copy-start | bytes 4718596

commit v2 on v1

v2 whole, which is shorter than its diff:
```python
import functools
import types

import jax
import jax.numpy as jnp
from jax import lax
from jax.experimental import pallas as pl
from jax.experimental.pallas import tpu as pltpu
from jax.sharding import PartitionSpec as P

EPS = 1e-05
F32 = jnp.float32
BF16 = jnp.bfloat16
MESH = pl.DeviceIdType.MESH
LANES = 128
HALO = 16
EDGE = 8
PIECES = 5


def nn(a, b):
    return lax.dot_general(a, b, (((1,), (0,)), ((), ())), preferred_element_type=F32)


def nt(a, b):
    return lax.dot_general(a, b, (((1,), (1,)), ((), ())), preferred_element_type=F32)


def tn(a, b):
    return lax.dot_general(a, b, (((0,), (0,)), ((), ())), preferred_element_type=F32)


def pieces_of(value, count):
    pieces = []
    for _ in range(count):
        piece = value.astype(BF16)
        pieces.append(piece)
        value = value - piece.astype(F32)
    return pieces


def exact_left(ones, value):
    return sum(nn(ones, piece) for piece in pieces_of(value, 3))


def exact_right(value, ones):
    return sum(nn(piece, ones) for piece in pieces_of(value, 2))


def sigmoid(value):
    return 0.5 * jnp.tanh(0.5 * value) + 0.5


def iota(shape, dim):
    return lax.broadcasted_iota(jnp.int32, shape, dim)


def kernel(z, names, *refs):
    m = types.SimpleNamespace(**dict(zip(names, refs)))
    R, T, D, C, H, S = z.R, z.T, z.D, z.C, z.H, z.S
    rp, nd, nc, ntn = z.rp, z.nd, z.nc, z.ntn
    pairs = H // 2
    head = C // H
    V = C + S
    half = T // 2
    d, c, t = lax.axis_index("dp"), lax.axis_index("context"), lax.axis_index("tensor")
    odd = lax.rem(t, 2)
    across = t + 1 - 2 * odd
    far = lax.rem(t + 2, 4) if ntn == 4 else t

    def at_ctx(k):
        return lax.rem(c + k, nc)

    def at_dp(k):
        return lax.rem(d + k, nd)

    def at_ten(k):
        return lax.rem(t + k, ntn)

    def rows_at(place, size):
        return pl.ds(pl.multiple_of(place * size, 16), size)

    def block(dd, cc):
        return rows_at(dd * nc + cc, rp)

    def row(r):
        return rows_at(r, T)

    def copy(src, dst, send, recv, dev):
        return pltpu.make_async_remote_copy(
            src_ref=src, dst_ref=dst, send_sem=send, recv_sem=recv, device_id=dev, device_id_type=MESH
        )

    def load(which):
        return pltpu.make_async_copy((m.hid, m.cot)[which], (m.hv, m.cv)[which], m.l_in.at[which])

    load(0).start()
    load(1).start()
    barrier = pltpu.get_barrier_semaphore()
    peers = [(d, at_ctx(k), t) for k in range(1, nc)]
    peers += [(at_dp(k), c, t) for k in range(1, nd)]
    peers += [(d, c, at_ten(k)) for k in range(1, ntn)]
    for peer in peers:
        pl.semaphore_signal(barrier, inc=1, device_id=peer, device_id_type=MESH)

    m.wx[block(d, c), :] = m.hp[1]
    m.ws[block(d, c), pl.ds(pl.multiple_of(odd * z.Q, LANES), z.Q)] = jnp.where(
        odd == 0, m.shp[:, : z.Q], m.shp[:, z.Q :]
    )
    m.tile[...] = jnp.zeros_like(m.tile)
    m.tile[0:rp, 0:H] = m.stp[...].astype(F32)
    m.wt[d * nc + c] = jnp.transpose(m.tile[...])[0:HALO, :].astype(BF16)
    pl.semaphore_wait(barrier, len(peers))

    def slot(p, dd, cc):
        if p == 2:
            return m.wt.at[dd * nc + cc]
        if p == 1:
            return m.ws.at[block(dd, cc), pl.ds(pl.multiple_of(odd * z.Q, LANES), z.Q)]
        return (m.wx, m.ws, m.wt, m.wz, m.wo)[p].at[block(dd, cc)]

    def w_ctx(p, s, right):
        to = c + s if right else c - s
        here = slot(p, d, c)
        return copy(here, here, m.wz_send.at[p, int(right), s], m.w_recv.at[p, d, c], (d, to, t))

    def w_dp(p, cc, k):
        here = slot(p, d, cc)
        return copy(here, here, m.wd_send.at[p, cc, k], m.w_recv.at[p, d, cc], (at_dp(k), c, t))

    def w_arrived(p, dd, cc):
        there = slot(p, dd, cc)
        copy(there, there, m.wd_send.at[p, cc, 0], m.w_recv.at[p, dd, cc], (d, c, t)).wait_recv()

    def w_start(p):
        for k in range(1, nd):
            w_dp(p, c, k).start()
        for s in range(1, nc):
            pl.when(c + s < nc)(lambda: w_ctx(p, s, True).start())
            pl.when(c - s >= 0)(lambda: w_ctx(p, s, False).start())

    def w_relay(p):
        def one(cc):
            w_arrived(p, d, cc)
            for k in range(1, nd):
                w_dp(p, cc, k).start()

        for s in range(1, nc):
            pl.when(c - s >= 0)(lambda: one(c - s))
            pl.when(c + s < nc)(lambda: one(c + s))

    def w_rest(p):
        for k in range(1, nd):
            for cc in range(nc):
                w_arrived(p, at_dp(k), cc)

    def w_sent(p):
        for cc in range(nc):
            for k in range(1, nd):
                w_dp(p, cc, k).wait_send()
        for s in range(1, nc):
            pl.when(c + s < nc)(lambda: w_ctx(p, s, True).wait_send())
            pl.when(c - s >= 0)(lambda: w_ctx(p, s, False).wait_send())

    def half_copy():
        here = m.ws.at[:, pl.ds(pl.multiple_of(odd * z.Q, LANES), z.Q)]
        return copy(here, here, m.sh_send.at[2], m.sh_recv.at[2], (d, c, across))

    def half_arrived():
        there = m.ws.at[:, pl.ds(pl.multiple_of((1 - odd) * z.Q, LANES), z.Q)]
        copy(there, there, m.sh_send.at[2], m.sh_recv.at[2], (d, c, across)).wait_recv()

    def halo_copy(r):
        return copy(
            m.hv.at[pl.ds(pl.multiple_of(r * T + T - HALO, 16), HALO)],
            m.hh.at[rows_at(r, HALO)],
            m.h_send.at[r],
            m.h_recv.at[r],
            (d, c + 1, t),
        )

    for p in range(3):
        w_start(p)
    load(0).wait()

    @pl.when(c < nc - 1)
    def _():
        for r in range(R):
            halo_copy(r).start()

    m.par[...] = jnp.zeros_like(m.par)
    m.par[0 : z.K, :C] = m.ch[...]
    m.par[0 : z.K, C:] = m.cs[...]
    m.par[4:5, :C] = m.bh[...]
    m.par[4:5, C:] = m.bs[...]
    m.par[5:6, :C] = m.gg[...]
    for h in range(H):
        m.par[6:7, h * head : (h + 1) * head] = jnp.broadcast_to(m.sk[0:1, h : h + 1], (1, head))
    m.par[7:8, 0:H] = m.sb[...]
    m.par[8:9, 0:H] = -jnp.exp(m.ld[...])
    m.wz[block(d, c), :] = m.hp[0]
    eye = (iota((rp, rp), 0) == iota((rp, rp), 1)).astype(BF16)
    m.wo[block(d, c), :] = nt(eye, m.ow[...]).astype(BF16)

    gain_in = m.ng[...]

    def normalize(u):
        u = u.astype(F32)
        mean = jnp.sum(u * u, axis=-1, keepdims=True) * (1.0 / z.d_true)
        return (u * lax.rsqrt(mean + EPS)) * gain_in

    @pl.loop(0, R)
    def _(r):
        m.nrm[row(r), :] = normalize(m.hv[row(r), :]).astype(BF16)

    length = m.seg.shape[-1]
    begin = c * T
    seqs = m.seg.shape[1]

    def ids_at(place, size):
        place = pl.multiple_of(place, LANES)
        lines = [m.seg[r // seqs, r % seqs : r % seqs + 1, pl.ds(place, size)] for r in range(R)]
        return jnp.concatenate(lines + [jnp.zeros_like(lines[0])] * (-R % 8), axis=0).astype(F32)

    now = ids_at(begin, T)
    before = jnp.where(c == 0, -1.0, ids_at(jnp.maximum(begin - LANES, 0), LANES))
    behind = jnp.where(c == nc - 1, -2.0, ids_at(jnp.minimum(begin + T, length - LANES), LANES))
    m.segr[...] = now
    m.segb[...] = before
    m.sega[...] = behind
    carried = (now == before[:, LANES - 1 : LANES]).astype(F32)
    closing = (now == now[:, T - 1 : T]).astype(F32)
    m.tot[...] = jnp.zeros_like(m.tot)
    for r in range(R):
        m.tot[0:1, :] = now[r : r + 1]
        m.tot[1:2, :] = carried[r : r + 1]
        m.tot[2:3, :] = closing[r : r + 1]
        m.segc[r * T : (r + 1) * T, :] = jnp.transpose(m.tot[...])
    away = iota((T, T), 0) - iota((T, T), 1)
    for j in range(1, z.K):
        m.diag[j - 1] = (away == j).astype(BF16)
        m.diag[z.K + j - 2] = (away == -j).astype(BF16)
    m.lower[...] = (away >= 0).astype(BF16)
    m.upper[...] = (away <= 0).astype(BF16)

    @pl.loop(0, R)
    def _(r):
        m.same[r] = (m.segc[row(r), 0:1] == m.segr[pl.ds(r, 1), :]).astype(BF16)

    @pl.when(c == 0)
    def _():
        m.hh[...] = jnp.zeros_like(m.hh)
        m.sin[...] = jnp.zeros_like(m.sin)

    @pl.when(c == nc - 1)
    def _():
        m.gin[...] = jnp.zeros_like(m.gin)
        m.dce[...] = jnp.zeros_like(m.dce)

    m.sm[t] = jnp.zeros((8, z.WL), F32)
    m.drow[...] = jnp.zeros_like(m.drow)

    w_relay(0)
    w_start(3)

    @pl.when(c > 0)
    def _():
        for r in range(R):
            halo_copy(r).wait_recv()

    m.nrmh[...] = normalize(m.hh[...]).astype(BF16)
    w_relay(1)
    w_relay(2)
    w_start(4)
    w_rest(0)

    low_lanes = iota((T, LANES), 1) < head
    lane = iota((T, LANES), 1)
    fold = (iota((C, LANES), 0) // head == iota((C, LANES), 1)).astype(BF16)

    def spread(values):
        return jnp.concatenate(
            [
                jnp.where(low_lanes, values[:, 2 * p : 2 * p + 1], values[:, 2 * p + 1 : 2 * p + 2])
                for p in range(pairs)
            ],
            axis=1,
        )

    def state_copy(r):
        return copy(m.ssend.at[r], m.sin.at[r], m.s_send.at[r], m.s_recv.at[r], (d, c + 1, t))

    def grad_copy(r):
        return copy(m.gsend.at[r], m.gin.at[r], m.g_send.at[r], m.g_recv.at[r], (d, c - 1, t))

    def edge_copy(r):
        return copy(m.edge.at[r], m.dce.at[r], m.e_send.at[r], m.e_recv.at[r], (d, c - 1, t))

    def leads(r):
        run = m.run[row(r), :]
        seg = m.segc[row(r), :]
        last = run[T - 1 : T, :]
        lead = jnp.exp(run) * seg[:, 1:2]
        trail = jnp.exp(last - run) * seg[:, 2:3]
        return lead, trail

    def convolve(r, lanes):
        seg = m.segc[row(r), :]
        reach = iota((EDGE, HALO), 1) - HALO - iota((EDGE, HALO), 0)
        near = seg[0:EDGE, 0:1] == m.segb[pl.ds(r, 1), LANES - HALO : LANES]
        for a in range(lanes[0], lanes[1], LANES):
            part = slice(a, a + LANES)
            value = m.v[row(r), part]
            before = m.vh[rows_at(r, HALO), part]
            conv = value.astype(F32) * m.par[0:1, part] + m.par[4:5, part]
            first = jnp.zeros((EDGE, LANES), F32)
            for j in range(1, z.K):
                tap = m.par[j : j + 1, part]
                conv = conv + nn(m.diag[j - 1] * m.same[r], value) * tap
                first = first + nn((near & (reach == -j)).astype(BF16), before) * tap
            conv = jnp.concatenate([conv[0:EDGE] + first, conv[EDGE:]], axis=0)
            logistic = sigmoid(conv)
            m.mix[row(r), part] = (conv * logistic).astype(BF16)
            m.slope[row(r), part] = logistic * (1.0 + conv * (1.0 - logistic))

    m.vh[:, :C] = nn(m.nrmh[...], m.wx[...]).astype(BF16)

    @pl.loop(0, R)
    def _(r):
        m.v[row(r), :C] = nn(m.nrm[row(r), :], m.wx[...]).astype(BF16)
        convolve(r, (0, C))

    w_rest(1)
    half_copy().start()
    w_rest(2)
    m.tile[...] = jnp.zeros_like(m.tile)

    @pl.loop(0, nd * nc)
    def _(b):
        m.tile[0:HALO, :] = m.wt[b].astype(F32)
        m.wst[rows_at(b, rp), :] = jnp.transpose(m.tile[...])[0:rp, :].astype(BF16)

    half_arrived()
    w_relay(3)
    m.vh[:, C:] = nn(m.nrmh[...], m.ws[...]).astype(BF16)

    @pl.loop(0, R)
    def _(r):
        m.v[row(r), C:] = nn(m.nrm[row(r), :], m.ws[...]).astype(BF16)
        raw = nn(m.nrm[row(r), :], m.wst[...]).astype(BF16).astype(F32)
        convolve(r, (C, V))
        pre = raw + m.par[7:8, :LANES]
        step = jnp.maximum(pre, 0.0) + jnp.log1p(jnp.exp(-jnp.abs(pre)))
        m.pre[row(r), :] = pre
        m.step[row(r), :] = step
        run = exact_left(m.lower[...], step * m.par[8:9, :LANES])
        m.run[row(r), :] = run
        m.runr[r] = jnp.transpose(run)[0:8, :]
        lead, trail = leads(r)
        scaled = m.mix[row(r), :C].astype(F32) * spread(step)
        m.xs[row(r), :] = scaled.astype(BF16)
        ending = (scaled * spread(trail)).astype(BF16)
        m.fresh[r] = tn(ending, m.mix[row(r), C : C + LANES])

        @pl.when(c == 0)
        def _():
            m.ssend[r] = m.fresh[r].astype(BF16)
            state_copy(r).start()

    load(1).wait()

    @pl.loop(0, R)
    def _(r):
        b, cm = m.mix[row(r), C : C + LANES], m.mix[row(r), C + LANES : V]
        m.scores[...] = nt(cm, b) * (m.same[r] * m.lower[...]).astype(F32)
        run = m.run[row(r), :]
        for p in range(pairs):
            part = slice(p * LANES, (p + 1) * LANES)
            both = []
            for h in (2 * p, 2 * p + 1):
                decay = jnp.exp(jnp.minimum(run[:, h : h + 1] - m.runr[r, h : h + 1, :], 0.0))
                both.append(nn((decay * m.scores[...]).astype(BF16), m.xs[row(r), part]))
            m.ins[row(r), part] = jnp.where(low_lanes, both[0], both[1])
        m.nrmt[:, row(r)] = jnp.transpose(m.nrm[row(r), :])
        m.cott[:, row(r)] = jnp.transpose(m.cv[row(r), :])

        @pl.when(c > 0)
        def _():
            state_copy(r).wait_recv()

            @pl.when(c < nc - 1)
            def _():
                lead, _ = leads(r)
                for h in range(H):
                    here = slice(h * head, (h + 1) * head)
                    keep = lead[T - 1 : T, h : h + 1]
                    m.ssend[r, here, :] = (
                        m.fresh[r, here, :] + keep * m.sin[r, here, :].astype(F32)
                    ).astype(BF16)
                state_copy(r).start()

    w_relay(4)
    w_rest(3)
    w_rest(4)

    def sums_copy(r, k):
        return copy(
            m.sums.at[t, r], m.sums.at[t, r], m.x_send.at[r, k], m.x_recv.at[r, t], (d, c, at_ten(k))
        )

    def sums_arrived(r, who):
        copy(
            m.sums.at[who, r], m.sums.at[who, r], m.x_send.at[r, 0], m.x_recv.at[r, who], (d, c, t)
        ).wait_recv()

    def mine(r):
        return pl.ds(pl.multiple_of(r * T + odd * half, 16), half)

    def theirs(r):
        return pl.ds(pl.multiple_of(r * T + (1 - odd) * half, 16), half)

    def near_copy(a, r):
        return copy(m.as_.at[a, r], m.ar_.at[a, r], m.a_send.at[a, r], m.a_recv.at[a, r], (d, c, across))

    def far_copy(a, r):
        return copy(m.bs_.at[a, r], m.br_.at[a, r], m.b_send.at[a, r], m.b_recv.at[a, r], (d, c, far))

    def back_copy(a, r):
        out = (m.ov, m.iv)[a].at[mine(r)]
        return copy(out, out, m.c_send.at[a, r], m.c_recv.at[a, r], (d, c, across))

    def back_arrived(a, r):
        out = (m.ov, m.iv)[a].at[theirs(r)]
        copy(out, out, m.c_send.at[a, r], m.c_recv.at[a, r], (d, c, across)).wait_recv()

    def chip_sum(a, r):
        near_copy(a, r).wait_recv()
        m.bs_[a, r] = (m.keep[a, r].astype(F32) + m.ar_[a, r].astype(F32)).astype(BF16)
        if ntn == 4:
            far_copy(a, r).start()

    def full_sum(a, r):
        total = m.bs_[a, r].astype(F32)
        if ntn == 4:
            far_copy(a, r).wait_recv()
            total = total + m.br_[a, r].astype(F32)
        return total

    @pl.loop(0, R)
    def _(r):
        b, cm = m.mix[row(r), C : C + LANES], m.mix[row(r), C + LANES : V]
        lead, _ = leads(r)
        carried = nt(cm, m.sin[r]) * spread(lead)
        m.ys[row(r), :] = carried
        ssd = m.ins[row(r), :] + carried + m.par[6:7, :C] * m.mix[row(r), :C].astype(F32)
        m.ssd[row(r), :] = ssd
        gate = nn(m.nrm[row(r), :], m.wz[...]).astype(BF16).astype(F32)
        m.zv[row(r), :] = gate.astype(BF16)
        gated = ssd * (gate * sigmoid(gate))
        m.gated[row(r), :C] = gated
        dy = nn(m.cv[row(r), :], m.wo[...])
        m.dy[row(r), :] = dy
        gain = m.par[5:6, :C]
        squares = jnp.sum(gated * gated, axis=-1, keepdims=True)
        inner = jnp.sum(dy * gain * gated, axis=-1, keepdims=True)
        both = jnp.where(lane == 0, squares, jnp.where(lane == 1, inner, 0.0))
        m.sums[t, r] = jnp.transpose(both)[0:8, :]
        for k in range(1, ntn):
            sums_copy(r, k).start()
        m.yg[row(r), :] = (gated * gain).astype(BF16)
        m.as_[0, r] = nt(m.yg[theirs(r), :], m.wo[...]).astype(BF16)
        near_copy(0, r).start()
        m.keep[0, r] = nt(m.yg[mine(r), :], m.wo[...])

    @pl.loop(0, R)
    def _(r):
        chip_sum(0, r)
        for k in range(1, ntn):
            sums_arrived(r, at_ten(k))
        total = m.sums[0, r]
        for who in range(1, ntn):
            total = total + m.sums[who, r]
        m.tot[0:8, :] = total
        columns = jnp.transpose(m.tot[...])
        scale = lax.rsqrt(columns[:, 0:1] * (1.0 / (C * ntn)) + EPS)
        m.rms[row(r), :] = jnp.broadcast_to(scale, (T, LANES))
        inner = columns[:, 1:2] * (1.0 / (C * ntn)) * scale * scale * scale
        gated, dy, gate, ssd = m.gated[row(r), :C], m.dy[row(r), :], m.zv[row(r), :].astype(F32), m.ssd[row(r), :]
        gain = m.par[5:6, :C]
        normal = gated * scale
        m.sm[t, 5:6, :C] += jnp.sum(dy * normal, axis=0, keepdims=True)
        m.yg[row(r), :] = (normal * gain).astype(BF16)
        d_gated = scale * dy * gain - gated * inner
        logistic = sigmoid(gate)
        m.dz[row(r), :] = (d_gated * ssd * (logistic * (1.0 + gate * (1.0 - logistic)))).astype(BF16)
        d_ssd = d_gated * (gate * logistic)
        m.ssd[row(r), :] = d_ssd
        lead, _ = leads(r)
        weighted = (d_ssd * spread(lead)).astype(BF16)
        m.wds[row(r), :] = weighted
        m.local[r] = tn(weighted, m.mix[row(r), C + LANES : V])

        @pl.when(c == nc - 1)
        def _():
            m.gsend[r] = m.local[r].astype(BF16)
            if nc > 1:
                grad_copy(r).start()

    gall, gyr, gzs, gzr = (m.ga0, m.ga1, m.ga2), (m.gy0, m.gy1, m.gy2), (m.gz0, m.gz1, m.gz2), (m.gr0, m.gr1, m.gr2)
    tall = (rp, rp, rp + HALO)

    def rs_dp(part, j, k):
        cc = at_ctx(j)
        return copy(
            gall[part].at[rows_at(at_dp(k) * nc + cc, tall[part])],
            gyr[part].at[k - 1, rows_at(cc, tall[part])],
            m.ry_send.at[part, j, k - 1],
            m.ry_recv.at[part, j, k - 1],
            (at_dp(k), c, t),
        )

    def rs_ctx(part, j):
        cc = at_ctx(j)
        return copy(
            gzs[part].at[rows_at(cc, tall[part])],
            gzr[part].at[c],
            m.rz_send.at[part, j],
            m.rz_recv.at[part, c],
            (d, cc, t),
        )

    def rs_arrived(part, cc):
        copy(gzr[part].at[cc], gzr[part].at[cc], m.rz_send.at[part, 0], m.rz_recv.at[part, cc], (d, c, t)).wait_recv()

    def rs_start(part):
        for j in list(range(1, nc)) + [0]:
            for k in range(1, nd):
                rs_dp(part, j, k).start()

    def rs_middle(part, j):
        cc = at_ctx(j)
        total = gall[part][rows_at(d * nc + cc, tall[part]), :].astype(F32)
        for k in range(1, nd):
            rs_dp(part, j, k).wait_recv()
            total = total + gyr[part][k - 1, rows_at(cc, tall[part]), :].astype(F32)
        own = j == 0

        def keep():
            gzr[part][c] = total.astype(BF16)

        def send():
            gzs[part][rows_at(cc, tall[part]), :] = total.astype(BF16)
            rs_ctx(part, j).start()

        if isinstance(j, int):
            keep() if own else send()
        else:
            pl.when(own)(keep)
            pl.when(jnp.logical_not(own))(send)

    def rs_end(part):
        for k in range(1, nc):
            rs_arrived(part, at_ctx(k))
        total = gzr[part][0].astype(F32)
        for cc in range(1, nc):
            total = total + gzr[part][cc].astype(F32)
        return total

    def rs_sent(part):
        for j in range(nc):
            for k in range(1, nd):
                rs_dp(part, j, k).wait_send()
            if j:
                rs_ctx(part, j).wait_send()

    m.ga1[:, C:] = nn(m.cott[...], m.yg[...]).astype(BF16)
    m.ga1[:, :C] = nn(m.nrmt[...], m.dz[...]).astype(BF16)
    rs_start(1)

    @pl.loop(0, R)
    def _(r):
        b, cm = m.mix[row(r), C : C + LANES], m.mix[row(r), C + LANES : V]
        m.mask[...] = (m.same[r] * m.upper[...]).astype(F32)
        m.scores[...] = nt(b, cm) * m.mask[...]
        run = m.run[row(r), :]
        losses = jnp.zeros((T, LANES), F32)
        for p in range(pairs):
            part = slice(p * LANES, (p + 1) * LANES)
            ds_pair = m.ssd[row(r), part].astype(BF16)
            xs_pair = m.xs[row(r), part]
            both = []
            for h in (2 * p, 2 * p + 1):
                pick = low_lanes if h % 2 == 0 else ~low_lanes
                decay = jnp.exp(jnp.minimum(m.runr[r, h : h + 1, :] - run[:, h : h + 1], 0.0))
                weight = decay * m.scores[...]
                both.append(nn(weight.astype(BF16), ds_pair))
                d_weight = nt(jnp.where(pick, xs_pair, jnp.zeros_like(xs_pair)), ds_pair)
                flow = d_weight * weight
                if h == 0:
                    m.dsc[...] = d_weight * decay
                else:
                    m.dsc[...] += d_weight * decay
                losses = jnp.where(lane == h, jnp.sum(flow, axis=1, keepdims=True), losses)
                m.drow[h : h + 1, :] = jnp.sum(flow, axis=0, keepdims=True)
            m.ins[row(r), part] = jnp.where(low_lanes, both[0], both[1])
        d_scores = (m.dsc[...] * m.mask[...]).astype(BF16)
        m.gated[row(r), :LANES] = nn(d_scores, cm)
        m.gated[row(r), LANES:S] = tn(d_scores, b)
        m.drun[row(r), :] = (
            jnp.transpose(m.drow[...])
            - losses
            + exact_right(m.ssd[row(r), :] * m.ys[row(r), :], fold)
        )

        @pl.when(c < nc - 1)
        def _():
            grad_copy(r).wait_recv()

            @pl.when(c > 0)
            def _():
                lead, _ = leads(r)
                for h in range(H):
                    here = slice(h * head, (h + 1) * head)
                    keep = lead[T - 1 : T, h : h + 1]
                    m.gsend[r, here, :] = (
                        m.local[r, here, :] + keep * m.gin[r, here, :].astype(F32)
                    ).astype(BF16)
                grad_copy(r).start()

    def final_out(r):
        value = m.hv[mine(r), :].astype(F32) + m.rms[mine(r), 0:1] * full_sum(0, r)
        m.ov[mine(r), :] = value.astype(BF16)
        back_copy(0, r).start()

    def adjoint(r):
        b, cm = m.mix[row(r), C : C + LANES], m.mix[row(r), C + LANES : V]
        lead, trail = leads(r)
        grad = m.gin[r]
        trailing = spread(trail)
        reach = nt(b, grad)
        scaled = m.xs[row(r), :].astype(F32) * trailing
        through = exact_right(scaled * reach, fold)
        d_run = m.drun[row(r), :] - through
        ends = jnp.sum(through, axis=0, keepdims=True)
        for h in range(H):
            here = slice(h * head, (h + 1) * head)
            joint = m.gin[r, here, :].astype(F32) * m.sin[r, here, :].astype(F32)
            joint = jnp.sum(jnp.sum(joint, axis=0, keepdims=True), axis=1, keepdims=True)
            ends = ends + jnp.where(lane[0:1] == h, joint * lead[T - 1 : T, :], 0.0)
        d_run = d_run + jnp.where(iota((T, LANES), 0) == T - 1, ends, 0.0)
        d_growth = exact_left(m.upper[...], d_run)
        step = m.step[row(r), :]
        d_xs = m.ins[row(r), :] + trailing * reach
        x = m.mix[row(r), :C].astype(F32)
        d_ssd = m.ssd[row(r), :]
        rate = m.par[8:9, :LANES]
        d_step = exact_right(d_xs * x, fold) + rate * d_growth
        m.sm[t, 7:8, LANES : 2 * LANES] += jnp.sum(step * d_growth, axis=0, keepdims=True) * rate
        m.sm[t, 7:8, 3 * LANES : 3 * LANES + C] += jnp.sum(d_ssd * x, axis=0, keepdims=True)
        d_pre = d_step * sigmoid(m.pre[row(r), :])
        m.sm[t, 7:8, :LANES] += jnp.sum(d_pre, axis=0, keepdims=True)
        m.dv[row(r), V:] = jnp.where(lane < H, d_pre, 0.0).astype(BF16)
        ring = lax.rem(r, 2)
        m.dcf[ring, :, :C] = (d_xs * spread(step) + m.par[6:7, :C] * d_ssd) * m.slope[row(r), :C]
        m.dcf[ring, :, C : C + LANES] = (
            m.gated[row(r), :LANES] + nn(scaled.astype(BF16), grad)
        ) * m.slope[row(r), C : C + LANES]
        m.dcf[ring, :, C + LANES :] = (
            m.gated[row(r), LANES:S] + nn(m.wds[row(r), :], m.sin[r])
        ) * m.slope[row(r), C + LANES :]

        @pl.when(c > 0)
        def _():
            m.edge[r] = m.dcf[ring, 0:EDGE, :]
            edge_copy(r).start()

    def finish(r):
        @pl.when(c < nc - 1)
        def _():
            edge_copy(r).wait_recv()

        ring = lax.rem(r, 2)
        seg = m.segc[row(r), :]
        reach = iota((EDGE, HALO), 1) + EDGE - iota((EDGE, HALO), 0)
        near = seg[T - EDGE : T, 0:1] == m.sega[pl.ds(r, 1), 0:HALO]
        for a in range(0, V, LANES):
            part = slice(a, a + LANES)
            d_conv = m.dcf[ring, :, part]
            low = d_conv.astype(BF16)
            after = m.dce[r, :, part]
            after = jnp.concatenate([after, jnp.zeros_like(after)], axis=0).astype(BF16)
            value = m.v[row(r), part].astype(F32)
            m.sm[t, 4:5, part] += jnp.sum(d_conv, axis=0, keepdims=True)
            m.sm[t, 0:1, part] += jnp.sum(d_conv * value, axis=0, keepdims=True)
            d_v = d_conv * m.par[0:1, part]
            for j in range(1, z.K):
                moved = nn(m.diag[z.K + j - 2] * m.same[r], low)
                last = nn((near & (reach == j)).astype(BF16), after)
                moved = jnp.concatenate([moved[: T - EDGE], moved[T - EDGE :] + last], axis=0)
                d_v = d_v + moved * m.par[j : j + 1, part]
                m.sm[t, j : j + 1, part] += jnp.sum(moved * value, axis=0, keepdims=True)
            m.dv[row(r), part] = d_v.astype(BF16)

        def d_normed(rows):
            return (
                nt(m.dv[rows, :C], m.wx[...])
                + nt(m.dv[rows, C:V], m.ws[...])
                + nt(m.dv[rows, V:], m.wst[...])
                + nt(m.dz[rows, :], m.wz[...])
            )

        def unit_of(rows):
            u = m.hv[rows, :].astype(F32)
            mean = jnp.sum(u * u, axis=-1, keepdims=True) * (1.0 / z.d_true)
            return u * lax.rsqrt(mean + EPS)

        value = d_normed(theirs(r))
        m.as_[1, r] = value.astype(BF16)
        near_copy(1, r).start()
        m.sm[t, 6:7, :D] += jnp.sum(value * unit_of(theirs(r)), axis=0, keepdims=True)
        value = d_normed(mine(r))
        m.keep[1, r] = value
        m.sm[t, 6:7, :D] += jnp.sum(value * unit_of(mine(r)), axis=0, keepdims=True)

    @pl.loop(0, max(R + 2, nc))
    def _(i):
        @pl.when(i < R)
        def _():
            final_out(i)
            adjoint(i)

        @pl.when(i < nc)
        def _():
            rs_middle(1, lax.rem(i + 1, nc))

        @pl.when((i >= 1) & (i < R + 1))
        def _():
            finish(i - 1)

        @pl.when((i >= 2) & (i < R + 2))
        def _():
            chip_sum(1, i - 2)

    width = S // ntn
    quarters = [m.dv[:, C + k * width : C + (k + 1) * width] for k in range(ntn)]
    value = nn(m.nrmt[...], jnp.concatenate(quarters[0::2] + quarters[1::2], axis=1))

    def share_copy():
        return copy(m.shs, m.shr, m.sh_send.at[0], m.sh_recv.at[0], (d, c, across))

    m.shk[...] = jnp.where(odd == 0, value[:, : z.Q], value[:, z.Q :])
    m.shs[...] = jnp.where(odd == 0, value[:, z.Q :], value[:, : z.Q]).astype(BF16)
    share_copy().start()
    steps = tn(m.dv[:, V:], m.nrm[...])[0:HALO, :]

    def small_ten(k):
        return copy(m.sm.at[t], m.sm.at[t], m.st_send.at[k], m.st_recv.at[t], (d, c, at_ten(k)))

    def small_dp(k):
        return copy(m.sd.at[d], m.sd.at[d], m.sd_send.at[k], m.sd_recv.at[d], (at_dp(k), c, t))

    def small_ctx(k):
        return copy(m.sc.at[c], m.sc.at[c], m.sc_send.at[k], m.sc_recv.at[c], (d, at_ctx(k), t))

    def arrived(buf, sems, who):
        copy(buf.at[who], buf.at[who], sems.at[who], sems.at[who], (d, c, t)).wait_recv()

    for k in range(1, ntn):
        small_ten(k).start()

    m.ga0[...] = nn(m.nrmt[...], m.dv[:, :C]).astype(BF16)
    share_copy().wait_recv()
    for b in range(nd * nc):
        here = slice(b * rp, (b + 1) * rp)
        there = b * (rp + HALO)
        m.ga2[there : there + rp, :] = (m.shk[here, :] + m.shr[here, :].astype(F32)).astype(BF16)
        m.ga2[there + rp : there + rp + HALO, :] = jnp.concatenate(
            [steps[:, here], jnp.zeros((HALO, LANES - rp), F32)], axis=1
        ).astype(BF16)
    rs_start(2)
    rs_start(0)

    for k in range(1, ntn):
        arrived(m.sm, m.st_recv, at_ten(k))
    common = m.sm[0]
    for who in range(1, ntn):
        common = common + m.sm[who]
    rows8, lanes8 = iota((8, z.WL), 0), iota((8, z.WL), 1)
    shared_here = (rows8 == 6) | ((rows8 < 5) & (lanes8 >= C))
    m.sd[d] = jnp.where(shared_here, common, m.sm[t])
    for k in range(1, nd):
        small_dp(k).start()

    def store(a, r):
        return pltpu.make_async_copy((m.ov, m.iv)[a].at[row(r)], (m.out, m.ing)[a].at[row(r)], m.l_out.at[a, r])

    for r in range(R):
        back_arrived(0, r)
        store(0, r).start()
    for j in list(range(1, nc)) + [0]:
        rs_middle(2, j)

    @pl.loop(0, R)
    def _(r):
        u = m.hv[mine(r), :].astype(F32)
        mean = jnp.sum(u * u, axis=-1, keepdims=True) * (1.0 / z.d_true)
        scale = lax.rsqrt(mean + EPS)
        unit = u * scale
        d_unit = full_sum(1, r) * gain_in
        inner = jnp.sum(d_unit * unit, axis=-1, keepdims=True) * (1.0 / z.d_true)
        value = m.cv[mine(r), :].astype(F32) + scale * (d_unit - unit * inner)
        m.iv[mine(r), :] = value.astype(BF16)
        back_copy(1, r).start()

        @pl.when(r < nc)
        def _():
            rs_middle(0, lax.rem(r + 1, nc))

    for j in range(R + 1, nc + 1):
        rs_middle(0, j % nc)

    for k in range(1, nd):
        arrived(m.sd, m.sd_recv, at_dp(k))
    total = m.sd[0]
    for who in range(1, nd):
        total = total + m.sd[who]
    m.sc[c] = total
    for k in range(1, nc):
        small_ctx(k).start()

    def last_copy():
        return copy(m.ls, m.lr, m.sh_send.at[1], m.sh_recv.at[1], (d, c, far))

    value = rs_end(2)
    if ntn == 4:
        m.ls[...] = value
        last_copy().start()
    else:
        m.gw2[...] = value
    m.gw1[...] = rs_end(1)

    for r in range(R):
        back_arrived(1, r)
        store(1, r).start()

    for k in range(1, nc):
        arrived(m.sc, m.sc_recv, at_ctx(k))
    total = m.sc[0]
    for who in range(1, nc):
        total = total + m.sc[who]
    m.small[...] = total

    if ntn == 4:
        last_copy().wait_recv()
        m.gw2[0:rp, :] = m.ls[0:rp, :] + m.lr[0:rp, :]
        m.gw2[rp:, :] = m.ls[rp:, :]
        last_copy().wait_send()

    m.gw0[...] = rs_end(0)

    for a in range(2):
        for r in range(R):
            store(a, r).wait()
            back_copy(a, r).wait_send()
            near_copy(a, r).wait_send()
            if ntn == 4:
                far_copy(a, r).wait_send()
    for p in range(PIECES):
        w_sent(p)
    half_copy().wait_send()
    for part in range(3):
        rs_sent(part)
    for r in range(R):
        for k in range(1, ntn):
            sums_copy(r, k).wait_send()

        @pl.when(c < nc - 1)
        def _():
            halo_copy(r).wait_send()
            state_copy(r).wait_send()

        @pl.when(c > 0)
        def _():
            grad_copy(r).wait_send()
            edge_copy(r).wait_send()

    share_copy().wait_send()
    for k in range(1, ntn):
        small_ten(k).wait_send()
    for k in range(1, nd):
        small_dp(k).wait_send()
    for k in range(1, nc):
        small_ctx(k).wait_send()


def finishing(z, out, ing, gw0, gw1, gw2, small, *outs):
    (o_out, o_ing, norm, heads, shared, step, taps, bias, staps, sbias, dsb, drate, dskip, gain, outw, tile, wide, sems) = outs
    C, S, D, H, rp, rows = z.C, z.S, z.D, z.H, z.rp, z.rows
    V = C + S
    head = C // H
    moves = [pltpu.make_async_copy(out, o_out, sems.at[0]), pltpu.make_async_copy(ing, o_ing, sems.at[1])]
    for move in moves:
        move.start()
    norm[...] = small[6:7, :D]
    heads[:, 0, :] = gw1[0:rows, :C]
    heads[:, 1, :] = gw0[0:rows, :]
    width = S // z.ntn
    pair = gw2[0:rows, :]
    if z.ntn == 4:
        upper = lax.axis_index("tensor") >= 2
        shared[...] = jnp.where(upper, pair[:, width:], pair[:, :width])
    else:
        shared[...] = pair
    tile[...] = jnp.zeros_like(tile)
    tile[0:HALO, :] = gw2[rp : rp + HALO, :]
    step[...] = jnp.transpose(tile[...])[0:rows, 0:H]
    taps[...] = small[0 : z.K, :C]
    bias[...] = small[4:5, :C]
    staps[...] = small[0 : z.K, C:V]
    sbias[...] = small[4:5, C:V]
    dsb[...] = small[7:8, :H]
    drate[...] = small[7:8, LANES : LANES + H]
    lanes = iota((1, H), 1)
    skip = jnp.zeros((1, H), F32)
    for h in range(H):
        begin = 3 * LANES + h * head
        skip = jnp.where(lanes == h, jnp.sum(small[7:8, begin : begin + head], axis=1, keepdims=True), skip)
    dskip[...] = skip
    gain[...] = small[5:6, :C]
    wide[...] = jnp.zeros_like(wide)
    wide[0:rp, :] = gw1[:, C:]
    outw[...] = jnp.transpose(wide[...])[:, 0:rows]
    for move in moves:
        move.wait()


def on_device(z, hidden_in, segment_ids, norm_gain, head_projection, shared_projection, step_projection,
              conv_heads, bias_heads, conv_shared, bias_shared, step_bias, log_decay, skip_gain, gate_gain,
              output_weight, out_cotangent):
    R, T, D, C, H, S = z.R, z.T, z.D, z.C, z.H, z.S
    rp, nd, nc, ntn, rows = z.rp, z.nd, z.nc, z.ntn, z.rows
    V = C + S
    blocks = nd * nc

    def widen(value):
        if rp == rows:
            return value
        value = value.reshape(value.shape[:-1] + (blocks, rows))
        value = jnp.pad(value, [(0, 0)] * (value.ndim - 1) + [(0, rp - rows)])
        return value.reshape(value.shape[:-2] + (D,))

    def narrow(value):
        if rp == rows:
            return value
        return value.reshape(value.shape[:-1] + (blocks, rp))[..., :rows].reshape(value.shape[:-1] + (z.d_true,))

    def taller(value, dim):
        if rp == rows:
            return value
        return jnp.pad(value, [(0, rp - rows if k == dim else 0) for k in range(value.ndim)])

    dma, vmem = pltpu.SemaphoreType.DMA, pltpu.VMEM
    N = R * T
    half = T // 2
    k0 = max(nd - 1, 1)
    ins = dict(
        hid=widen(hidden_in.reshape(N, z.d_true)), cot=widen(out_cotangent.reshape(N, z.d_true)),
        seg=segment_ids, ng=widen(norm_gain[None]), hp=taller(jnp.moveaxis(head_projection, 1, 0), 1),
        shp=taller(shared_projection, 0), stp=taller(step_projection, 0), ow=taller(output_weight, 1),
        ch=conv_heads, bh=bias_heads[None], cs=conv_shared, bs=bias_shared[None], sb=step_bias[None],
        ld=log_decay[None], sk=skip_gain[None], gg=gate_gain[None],
    )
    outs = dict(
        out=jax.ShapeDtypeStruct((N, D), BF16),
        ing=jax.ShapeDtypeStruct((N, D), BF16),
        gw0=jax.ShapeDtypeStruct((rp, C), F32),
        gw1=jax.ShapeDtypeStruct((rp, 2 * C), F32),
        gw2=jax.ShapeDtypeStruct((rp + HALO, z.Q), F32),
        small=jax.ShapeDtypeStruct((8, z.WL), F32),
    )
    scratch = dict(
        hv=vmem((N, D), BF16), cv=vmem((N, D), BF16), ov=vmem((N, D), BF16), iv=vmem((N, D), BF16),
        wx=vmem((D, C), BF16), ws=vmem((D, S), BF16), wt=vmem((blocks, HALO, LANES), BF16), wst=vmem((D, LANES), BF16),
        wz=vmem((D, C), BF16), wo=vmem((D, C), BF16), tile=vmem((LANES, LANES), F32), par=vmem((16, V), F32),
        segc=vmem((N, LANES), F32), segr=vmem((8 * -(-R // 8), T), F32),
        segb=vmem((8 * -(-R // 8), LANES), F32), sega=vmem((8 * -(-R // 8), LANES), F32),
        diag=vmem((2 * z.K - 2, T, T), BF16), lower=vmem((T, T), BF16), upper=vmem((T, T), BF16),
        same=vmem((R, T, T), BF16), mask=vmem((T, T), F32),
        hh=vmem((R * HALO, D), BF16), nrmh=vmem((R * HALO, D), BF16), vh=vmem((R * HALO, V), BF16),
        nrm=vmem((N, D), BF16), nrmt=vmem((D, N), BF16), cott=vmem((D, N), BF16),
        v=vmem((N, V), BF16), mix=vmem((N, V), BF16), slope=vmem((N, V), F32),
        pre=vmem((N, LANES), F32), step=vmem((N, LANES), F32), run=vmem((N, LANES), F32),
        runr=vmem((R, 8, T), F32), xs=vmem((N, C), BF16),
        fresh=vmem((R, C, LANES), F32), local=vmem((R, C, LANES), F32),
        ssend=vmem((R, C, LANES), BF16), sin=vmem((R, C, LANES), BF16),
        gsend=vmem((R, C, LANES), BF16), gin=vmem((R, C, LANES), BF16),
        scores=vmem((T, T), F32), dsc=vmem((T, T), F32), drow=vmem((LANES, T), F32), tot=vmem((LANES, T), F32),
        ins=vmem((N, C), F32), ys=vmem((N, C), F32), ssd=vmem((N, C), F32), zv=vmem((N, C), BF16),
        gated=vmem((N, max(C, S)), F32), dy=vmem((N, C), F32),
        yg=vmem((N, C), BF16), dz=vmem((N, C), BF16), wds=vmem((N, C), BF16),
        rms=vmem((N, LANES), F32), sums=vmem((ntn, R, 8, T), F32),
        as_=vmem((2, R, half, D), BF16), ar_=vmem((2, R, half, D), BF16),
        bs_=vmem((2, R, half, D), BF16), br_=vmem((2, R, half, D), BF16), keep=vmem((2, R, half, D), F32),
        ga0=vmem((D, C), BF16), ga1=vmem((D, 2 * C), BF16), ga2=vmem((blocks * (rp + HALO), z.Q), BF16),
        gy0=vmem((k0, nc * rp, C), BF16), gy1=vmem((k0, nc * rp, 2 * C), BF16), gy2=vmem((k0, nc * (rp + HALO), z.Q), BF16),
        gz0=vmem((nc * rp, C), BF16), gz1=vmem((nc * rp, 2 * C), BF16), gz2=vmem((nc * (rp + HALO), z.Q), BF16),
        gr0=vmem((nc, rp, C), BF16), gr1=vmem((nc, rp, 2 * C), BF16), gr2=vmem((nc, rp + HALO, z.Q), BF16),
        drun=vmem((N, LANES), F32), dcf=vmem((2, T, V), F32), edge=vmem((R, EDGE, V), F32),
        dce=vmem((R, EDGE, V), F32), dv=vmem((N, V + LANES), BF16),
        shs=vmem((D, z.Q), BF16), shr=vmem((D, z.Q), BF16), shk=vmem((D, z.Q), F32),
        ls=vmem((rp + HALO, z.Q), F32), lr=vmem((rp + HALO, z.Q), F32),
        sm=vmem((ntn, 8, z.WL), F32), sd=vmem((nd, 8, z.WL), F32), sc=vmem((nc, 8, z.WL), F32),
        l_in=dma((2,)), l_out=dma((2, R)),
        wz_send=dma((PIECES, 2, nc)), wd_send=dma((PIECES, nc, nd)), w_recv=dma((PIECES, nd, nc)),
        h_send=dma((R,)), h_recv=dma((R,)),
        s_send=dma((R,)), s_recv=dma((R,)), g_send=dma((R,)), g_recv=dma((R,)), e_send=dma((R,)), e_recv=dma((R,)),
        x_send=dma((R, ntn)), x_recv=dma((R, ntn)),
        a_send=dma((2, R)), a_recv=dma((2, R)), b_send=dma((2, R)), b_recv=dma((2, R)),
        c_send=dma((2, R)), c_recv=dma((2, R)),
        ry_send=dma((3, nc, k0)), ry_recv=dma((3, nc, k0)), rz_send=dma((3, nc)), rz_recv=dma((3, nc)),
        sh_send=dma((3,)), sh_recv=dma((3,)),
        st_send=dma((ntn,)), st_recv=dma((ntn,)), sd_send=dma((nd,)), sd_recv=dma((nd,)),
        sc_send=dma((nc,)), sc_recv=dma((nc,)),
    )
    names = list(ins) + list(outs) + list(scratch)
    whole = pl.BlockSpec(memory_space=pltpu.VMEM)
    large = pl.BlockSpec(memory_space=pl.ANY)
    raw = pl.pallas_call(
        functools.partial(kernel, z, names),
        out_shape=list(outs.values()),
        in_specs=[large] * 2 + [whole] * (len(ins) - 2),
        out_specs=[large] * 2 + [whole] * (len(outs) - 2),
        scratch_shapes=list(scratch.values()),
        compiler_params=pltpu.CompilerParams(
            collective_id=0, has_side_effects=True, vmem_limit_bytes=z.limit
        ),
    )(*ins.values())

    shapes = [
        ((N, D), BF16), ((N, D), BF16), ((1, D), F32), ((rows, 2, C), F32), ((rows, S // ntn), F32), ((rows, H), F32),
        ((z.K, C), F32), ((1, C), F32), ((z.K, S), F32), ((1, S), F32), ((1, H), F32), ((1, H), F32), ((1, H), F32),
        ((1, C), F32), ((C, rows), F32),
    ]
    outs = pl.pallas_call(
        functools.partial(finishing, z),
        out_shape=[jax.ShapeDtypeStruct(*shape) for shape in shapes],
        in_specs=[large] * 2 + [whole] * 4,
        out_specs=[large] * 2 + [whole] * (len(shapes) - 2),
        scratch_shapes=[vmem((LANES, LANES), F32), vmem((LANES, C), F32), dma((2,))],
    )(*raw)
    (block_out, input_grad, norm, heads, shared, step, taps, bias, staps, sbias, dsb, drate, dskip, gain, outw) = outs
    return (
        narrow(block_out).reshape(hidden_in.shape),
        narrow(input_grad).reshape(hidden_in.shape),
        narrow(norm)[0],
        heads, shared, step, taps, bias[0], staps, sbias[0], dsb[0], drate[0], dskip[0], gain[0], outw,
    )


def solution(mesh):
    nd, nc, ntn = (mesh.shape[name] for name in ("dp", "context", "tensor"))

    def body(*args):
        hidden, heads, shared = args[0], args[3], args[4]
        micro, seqs, tokens, width = hidden.shape
        rows = heads.shape[0]
        rp = -(-rows // 16) * 16
        inner = heads.shape[2]
        z = types.SimpleNamespace(
            R=micro * seqs, T=tokens, d_true=width, D=rp * nd * nc, rows=rows, rp=rp, nd=nd, nc=nc, ntn=ntn,
            C=inner, H=args[10].shape[0], S=shared.shape[1], K=args[6].shape[0],
            Q=shared.shape[1] // 2, limit=62 << 20,
        )
        z.WL = max(inner + z.S, z.D, 3 * LANES + inner)
        return on_device(z, *args)

    return jax.shard_map(
        body,
        mesh=mesh,
        in_specs=(
            P(None, "dp", "context", None),
            P(None, "dp", None),
            P(),
            P(("dp", "context"), None, "tensor"),
            P(("dp", "context"), None),
            P(("dp", "context"), "tensor"),
            P(None, "tensor"),
            P("tensor"),
            P(),
            P(),
            P("tensor"),
            P("tensor"),
            P("tensor"),
            P("tensor"),
            P("tensor", ("dp", "context")),
            P(None, "dp", "context", None),
        ),
        out_specs=(
            P(None, "dp", "context", None),
            P(None, "dp", "context", None),
            P(),
            P(("dp", "context"), None, "tensor"),
            P(("dp", "context"), "tensor"),
            P(("dp", "context"), "tensor"),
            P(None, "tensor"),
            P("tensor"),
            P(),
            P(),
            P("tensor"),
            P("tensor"),
            P("tensor"),
            P("tensor"),
            P("tensor", ("dp", "context")),
        ),
        check_vma=False,
    )
```

time: 164 us -> 246 us (1.50); the launches traced: 161 us -> 246 us
  Pallas kernels: 129 us -> 228 us
  local copies, waits for them, and re-layouts: 26.6 us -> 13 us
    pallas_call x0 -> x1, Pallas kernels: none -> 98.3 us  [on_device(): pl.pallas_call(functools.partial(finishing, z), out_shape=[jax.ShapeDtype...]
    slice x8 -> x0, local copies, waits for them, and re-layouts: 8.96 us -> none  [the longest x1 1.38 us: on_device(): small[5, :C]]
    pallas_call x0 -> x3, other arithmetic: none -> 3.84 us  [on_device(): pl.pallas_call(functools.partial(finishing, z), out_shape=[jax.ShapeDtype...]
    unnamed x23 -> x6, local copies, waits for them, and re-layouts: 6.29 us -> 9.28 us
    concatenate x4 -> x0, other arithmetic: 2.77 us -> none  [the longest x1 0.71 us: on_device(): jnp.concatenate([conv_heads, conv_shared], axis=1)]
where the time goes in v2:
time: 246 us
  Pallas kernels  228 us (93%)
  local copies, waits for them, and re-layouts  13 us (5%)
  other arithmetic  3.84 us (2%)
    pallas_call x1, Pallas kernels, on_device(): pl.pallas_call(functools.partial(kernel, z, names), out_shape=list(outs.v...  130 us
    pallas_call x1, Pallas kernels, on_device(): pl.pallas_call(functools.partial(finishing, z), out_shape=[jax.ShapeDtype...  98.3 us
    unnamed x6, local copies, waits for them, and re-layouts  9.28 us

profile of v2, /device:TPU:0, one launch (start us, length us, event | category | flops | bytes accessed | tf_op | source)
XLA Modules:
  0.0 245.8 jit_solution(8471704777033543764)
XLA Ops:
  0.6 1.2 broadcast_in_dim.22.refs_9_
  1.9 1.2 broadcast_in_dim.27.refs_15_
  3.1 1.3 broadcast_in_dim.21.refs_3_
  4.4 1.4 copy.32.refs_6_
  5.8 1.6 copy.33.refs_7_
  7.4 1.6 copy.38
  9.0 129.9 %shard_map.271 = (bf16[1024,768]{1,0:T(8,128)(2,1)}, bf16[1024,768]{1,0:T(8,128)(2,1)}, f32[96,384]{1,0:T(8,128)}, f32[96,768]{1,0:T(8,128)}, f32[112,128]{1,0:T(8,128)}, /*index=5*/f32[8,768]{1,0:T(8,128)}) custom-call(bf16[1024,768]{1,0:T(8,128)(2,1)} %bitcast.15, bf16[1024,768]{1,0:T(8,128)(2,1)} %bitcast.16, s32[2,2,1024]{2,1,0:T(2,128)} %refs_2_.1, ...), custom_call_target="tpu_custom_call" | custom-call | tf_op jit(solution)/shard_map/pallas_call | solution.py:1028
  139.0 98.3 %shard_map.272 = (bf16[1024,768]{1,0:T(8,128)(2,1)}, bf16[1024,768]{1,0:T(8,128)(2,1)}, f32[1,768]{1,0:T(1,128)}, f32[96,2,384]{2,1,0:T(2,128)}, f32[96,64]{1,0:...) custom-call(bf16[1024,768]{1,0:T(8,128)(2,1)} %get-tuple-element.36., ...), custom_call_target="tpu_custom_call" | custom-call | tf_op jit(solution)/shard_map/pallas_call | solution.py:1044
  237.2 1.3 reduce.1
  238.5 1.3 reduce.2
  239.8 1.3 reduce
  241.1 1.5 copy.35
  242.6 1.5 copy.34
  244.0 1.7 copy.36

commit v3 on v2

v3 whole, which is shorter than its diff:
```python
import functools
import types

import jax
import jax.numpy as jnp
from jax import lax
from jax.experimental import pallas as pl
from jax.experimental.pallas import tpu as pltpu
from jax.sharding import PartitionSpec as P

EPS = 1e-05
F32 = jnp.float32
BF16 = jnp.bfloat16
MESH = pl.DeviceIdType.MESH
LANES = 128
HALO = 16
EDGE = 8
PIECES = 5
WIDE = 256
GROUP = 8


def nn(a, b):
    return lax.dot_general(a, b, (((1,), (0,)), ((), ())), preferred_element_type=F32)


def nt(a, b):
    return lax.dot_general(a, b, (((1,), (1,)), ((), ())), preferred_element_type=F32)


def tn(a, b):
    return lax.dot_general(a, b, (((0,), (0,)), ((), ())), preferred_element_type=F32)


def pieces_of(value, count):
    pieces = []
    for _ in range(count):
        piece = value.astype(BF16)
        pieces.append(piece)
        value = value - piece.astype(F32)
    return pieces


def exact_rows(value, ones):
    pieces = [piece.astype(F32) for piece in pieces_of(value, 3)]
    stacked = jnp.concatenate(pieces + [jnp.zeros_like(value)], axis=0).astype(BF16)
    out = nn(stacked, ones)
    return out[0:8] + out[8:16] + out[16:24]


def exact_right(value, ones):
    return sum(nn(piece, ones) for piece in pieces_of(value, 2))


def sigmoid(value):
    return 0.5 * jnp.tanh(0.5 * value) + 0.5


def iota(shape, dim):
    return lax.broadcasted_iota(jnp.int32, shape, dim)


def kernel(z, names, *refs):
    m = types.SimpleNamespace(**dict(zip(names, refs)))
    R, T, D, C, H, S = z.R, z.T, z.D, z.C, z.H, z.S
    rp, nd, nc, ntn = z.rp, z.nd, z.nc, z.ntn
    pairs = H // 2
    head = C // H
    V = C + S
    Z = V + LANES
    half = T // 2
    d, c, t = lax.axis_index("dp"), lax.axis_index("context"), lax.axis_index("tensor")
    odd = lax.rem(t, 2)
    across = t + 1 - 2 * odd
    far = lax.rem(t + 2, 4) if ntn == 4 else t

    def at_ctx(k):
        return lax.rem(c + k, nc)

    def at_dp(k):
        return lax.rem(d + k, nd)

    def at_ten(k):
        return lax.rem(t + k, ntn)

    def rows_at(place, size):
        return pl.ds(pl.multiple_of(place * size, 16), size)

    def block(dd, cc):
        return rows_at(dd * nc + cc, rp)

    def row(r):
        return rows_at(r, T)

    def lanes_at(place, size):
        return pl.ds(pl.multiple_of(place, LANES), size)

    def copy(src, dst, send, recv, dev):
        return pltpu.make_async_remote_copy(
            src_ref=src, dst_ref=dst, send_sem=send, recv_sem=recv, device_id=dev, device_id_type=MESH
        )

    def load(which):
        return pltpu.make_async_copy((m.hid, m.cot)[which], (m.hv, m.cv)[which], m.l_in.at[which])

    load(0).start()
    load(1).start()
    barrier = pltpu.get_barrier_semaphore()
    peers = [(d, at_ctx(k), t) for k in range(1, nc)]
    peers += [(at_dp(k), c, t) for k in range(1, nd)]
    peers += [(d, c, at_ten(k)) for k in range(1, ntn)]
    for peer in peers:
        pl.semaphore_signal(barrier, inc=1, device_id=peer, device_id_type=MESH)

    m.wall[block(d, c), 0:C] = m.hp[:, 1, :]
    m.wall[block(d, c), lanes_at(C + odd * z.Q, z.Q)] = jnp.where(odd == 0, m.shp[:, : z.Q], m.shp[:, z.Q :])
    m.wt[d * nc + c] = jnp.zeros((GROUP, LANES), F32)
    m.wt[d * nc + c, 0:H, 0:rp] = m.stp[...].astype(F32)
    pl.semaphore_wait(barrier, len(peers))

    def slot(p, dd, cc):
        if p == 2:
            return m.wt.at[dd * nc + cc]
        if p == 4:
            return m.wo.at[block(dd, cc)]
        place, size = ((0, C), (C + odd * z.Q, z.Q), None, (Z, C))[p]
        return m.wall.at[block(dd, cc), lanes_at(place, size)]

    def w_ctx(p, s, right):
        to = c + s if right else c - s
        here = slot(p, d, c)
        return copy(here, here, m.wz_send.at[p, int(right), s], m.w_recv.at[p, d, c], (d, to, t))

    def w_dp(p, cc, k):
        here = slot(p, d, cc)
        return copy(here, here, m.wd_send.at[p, cc, k], m.w_recv.at[p, d, cc], (at_dp(k), c, t))

    def w_arrived(p, dd, cc):
        there = slot(p, dd, cc)
        copy(there, there, m.wd_send.at[p, cc, 0], m.w_recv.at[p, dd, cc], (d, c, t)).wait_recv()

    def w_start(p):
        for k in range(1, nd):
            w_dp(p, c, k).start()
        for s in range(1, nc):
            pl.when(c + s < nc)(lambda: w_ctx(p, s, True).start())
            pl.when(c - s >= 0)(lambda: w_ctx(p, s, False).start())

    def w_relay(p):
        def one(cc):
            w_arrived(p, d, cc)
            for k in range(1, nd):
                w_dp(p, cc, k).start()

        for s in range(1, nc):
            pl.when(c - s >= 0)(lambda: one(c - s))
            pl.when(c + s < nc)(lambda: one(c + s))

    def w_rest(p):
        for k in range(1, nd):
            for cc in range(nc):
                w_arrived(p, at_dp(k), cc)

    def w_sent(p):
        for cc in range(nc):
            for k in range(1, nd):
                w_dp(p, cc, k).wait_send()
        for s in range(1, nc):
            pl.when(c + s < nc)(lambda: w_ctx(p, s, True).wait_send())
            pl.when(c - s >= 0)(lambda: w_ctx(p, s, False).wait_send())

    def half_copy():
        here = m.wall.at[:, lanes_at(C + odd * z.Q, z.Q)]
        return copy(here, here, m.sh_send.at[2], m.sh_recv.at[2], (d, c, across))

    def half_arrived():
        there = m.wall.at[:, lanes_at(C + (1 - odd) * z.Q, z.Q)]
        copy(there, there, m.sh_send.at[2], m.sh_recv.at[2], (d, c, across)).wait_recv()

    def halo_copy(r):
        return copy(
            m.hv.at[pl.ds(pl.multiple_of(r * T + T - HALO, 16), HALO)],
            m.hh.at[rows_at(r, HALO)],
            m.h_send.at[r],
            m.h_recv.at[r],
            (d, c + 1, t),
        )

    for p in range(3):
        w_start(p)
    load(0).wait()

    @pl.when(c < nc - 1)
    def _():
        for r in range(R):
            halo_copy(r).start()

    m.wall[block(d, c), Z:] = m.hp[:, 0, :]
    m.wo[block(d, c), :] = m.ow[...]

    m.par[0 : z.K, :C] = m.ch[...]
    m.par[0 : z.K, C:] = m.cs[...]
    m.par[4:5, :C] = m.bh[...][None]
    m.par[4:5, C:] = m.bs[...][None]
    m.par[5:6, :C] = m.gg[...][None]
    for h in range(H):
        m.par[6:7, h * head : (h + 1) * head] = jnp.broadcast_to(m.sk[0:1, h : h + 1], (1, head))
    m.gain[0:1, :] = m.ng[...][None]
    m.tile[...] = jnp.zeros_like(m.tile)
    m.tile[0:1, 0:H] = m.sb[...]
    m.tile[1:2, 0:H] = -jnp.exp(m.ld[...])
    turned = jnp.transpose(m.tile[...])
    m.hcol[...] = turned[0:GROUP, :]
    bias_col, rate_col = m.hcol[:, 0:1], m.hcol[:, 1:2]
    gain_in = m.gain[0:1, :]

    def normalize(u):
        u = u.astype(F32)
        mean = jnp.sum(u * u, axis=-1, keepdims=True) * (1.0 / z.d_true)
        return (u * lax.rsqrt(mean + EPS)) * gain_in

    length = m.seg.shape[-1]
    begin = c * T
    seqs = m.seg.shape[1]

    def ids_at(place, size):
        place = pl.multiple_of(place, LANES)
        lines = [m.seg[r // seqs, r % seqs : r % seqs + 1, pl.ds(place, size)] for r in range(R)]
        return jnp.concatenate(lines + [jnp.zeros_like(lines[0])] * (-R % 8), axis=0).astype(F32)

    now = ids_at(begin, T)
    before = jnp.where(c == 0, -1.0, ids_at(jnp.maximum(begin - LANES, 0), LANES))
    behind = jnp.where(c == nc - 1, -2.0, ids_at(jnp.minimum(begin + T, length - LANES), LANES))
    m.segr[...] = now
    m.segb[...] = before
    m.sega[...] = behind
    m.carried[...] = (now == before[:, LANES - 1 : LANES]).astype(F32)
    m.closing[...] = (now == now[:, T - 1 : T]).astype(F32)
    m.tot[...] = jnp.zeros_like(m.tot)
    m.tot[0 : now.shape[0], :] = now
    m.segc[...] = jnp.transpose(m.tot[...])
    away = iota((T, T), 0) - iota((T, T), 1)
    m.lower[...] = (away >= 0).astype(BF16)
    m.upper[...] = (away <= 0).astype(BF16)
    for r in range(R):
        same = m.segc[:, r : r + 1] == m.segr[r : r + 1, :]
        m.past[r] = (same & (away >= 0)).astype(BF16)
        m.next[r] = (same & (away <= 0)).astype(BF16)
        for j in range(1, z.K):
            m.down[r, j - 1] = (same & (away == j)).astype(BF16)
            m.up[r, j - 1] = (same & (away == -j)).astype(BF16)

    @pl.when(c == 0)
    def _():
        m.hh[...] = jnp.zeros_like(m.hh)
        m.sin[...] = jnp.zeros_like(m.sin)

    @pl.when(c == nc - 1)
    def _():
        m.gin[...] = jnp.zeros_like(m.gin)
        m.dce[...] = jnp.zeros_like(m.dce)

    m.sm[t] = jnp.zeros((8, z.WL), F32)
    m.hacc[...] = jnp.zeros_like(m.hacc)
    m.drow[...] = jnp.zeros_like(m.drow)
    m.gstep[...] = jnp.zeros_like(m.gstep)

    @pl.loop(0, R)
    def _(r):
        value = normalize(m.hv[row(r), :]).astype(BF16)
        m.nrm[row(r), :] = value
        m.nrmt[:, row(r)] = jnp.transpose(value)

    w_relay(0)
    w_start(3)
    load(1).wait()

    @pl.loop(0, R)
    def _(r):
        m.cott[:, row(r)] = jnp.transpose(m.cv[row(r), :])

    @pl.when(c > 0)
    def _():
        for r in range(R):
            halo_copy(r).wait_recv()

    m.nrmh[...] = normalize(m.hh[...]).astype(BF16)
    w_relay(1)
    w_relay(2)
    w_start(4)
    w_rest(0)

    low_lanes = iota((T, LANES), 1) < head
    lane = iota((T, LANES), 1)
    fold = (iota((C, LANES), 0) // head == iota((C, LANES), 1)).astype(F32)
    fold_run = fold.astype(BF16)
    fold_through = (
        (iota((C, LANES), 0) // head == iota((C, LANES), 1) - GROUP).astype(F32) - fold
    ).astype(BF16)
    fold_step = (iota((C, LANES), 0) // head == iota((C, LANES), 1) - 2 * GROUP).astype(BF16)
    RUN, STEP, LEAD, TRAIL = 0, GROUP, 2 * GROUP, 3 * GROUP

    def widened(values, base, p):
        a = base + 2 * p
        return jnp.where(low_lanes[: values.shape[0]], values[:, a : a + 1], values[:, a + 1 : a + 2])

    def spread(values, base):
        return jnp.concatenate([widened(values, base, p) for p in range(pairs)], axis=1)

    def state_copy(r):
        return copy(m.ssend.at[r], m.sin.at[r], m.s_send.at[r], m.s_recv.at[r], (d, c + 1, t))

    def grad_copy(r):
        return copy(m.gsend.at[r], m.gin.at[r], m.g_send.at[r], m.g_recv.at[r], (d, c - 1, t))

    def edge_copy(r):
        return copy(m.edge.at[r], m.dce.at[r], m.e_send.at[r], m.e_recv.at[r], (d, c - 1, t))

    def kept(r):
        return spread(m.cols[pl.ds(r * T + T - 1, 1), :], LEAD)

    def pair(p):
        return slice(p * LANES, (p + 1) * LANES)

    def convolve(r, lanes):
        reach = iota((EDGE, HALO), 1) - HALO - iota((EDGE, HALO), 0)
        seg = m.past[r]
        for a in range(lanes[0], lanes[1], WIDE):
            part = slice(a, min(a + WIDE, lanes[1]))
            value = m.v[row(r), part]
            before = m.vh[rows_at(r, HALO), part]
            conv = value.astype(F32) * m.par[0:1, part] + m.par[4:5, part]
            first = jnp.zeros((EDGE, conv.shape[1]), F32)
            for j in range(1, z.K):
                tap = m.par[j : j + 1, part]
                conv = conv + nn(m.down[r, j - 1], value) * tap
                first = first + nn(m.early[r, j - 1], before) * tap
            conv = jnp.concatenate([conv[0:EDGE] + first, conv[EDGE:]], axis=0)
            logistic = sigmoid(conv)
            m.mix[row(r), part] = (conv * logistic).astype(BF16)
            m.slope[row(r), part] = logistic * (1.0 + conv * (1.0 - logistic))

    reach = iota((HALO, HALO), 1) - HALO - iota((HALO, HALO), 0)
    ahead = iota((HALO, HALO), 1) + HALO - iota((HALO, HALO), 0)
    for r in range(R):
        near = m.segc[0:HALO, r : r + 1] == m.segb[r : r + 1, LANES - HALO : LANES]
        late = m.segc[T - HALO : T, r : r + 1] == m.sega[r : r + 1, 0:HALO]
        for j in range(1, z.K):
            m.early[r, j - 1] = (near & (reach == -j)).astype(BF16)[0:EDGE]
            m.late[r, j - 1] = (late & (ahead == j)).astype(BF16)

    m.vh[:, :C] = nn(m.nrmh[...], m.wall[:, :C]).astype(BF16)

    @pl.loop(0, R)
    def _(r):
        m.v[row(r), :C] = nn(m.nrm[row(r), :], m.wall[:, :C]).astype(BF16)
        convolve(r, (0, C))

    w_rest(1)
    half_copy().start()
    w_rest(2)
    m.wst[...] = jnp.concatenate([m.wt[b, :, 0:rp] for b in range(nd * nc)], axis=1)
    raw = nn(
        jnp.concatenate([m.wst[...], jnp.zeros((GROUP, D), F32)], axis=0).astype(BF16), m.nrmt[...]
    )[0:GROUP]
    pre = raw.astype(BF16).astype(F32) + bias_col
    m.pre[...] = pre
    m.step[...] = jnp.maximum(pre, 0.0) + jnp.log1p(jnp.exp(-jnp.abs(pre)))

    m.tile[...] = jnp.zeros_like(m.tile)
    for b in range(nd * nc):
        m.tile[0:GROUP, :] = m.wt[b]
        m.wall[b * rp : (b + 1) * rp, V:Z] = jnp.transpose(m.tile[...])[0:rp, :].astype(BF16)

    @pl.loop(0, R)
    def _(r):
        step = m.step[:, row(r)]
        run = exact_rows(step * rate_col, m.upper[...])
        m.runr[r] = run
        m.tot[0:GROUP, :] = run
        m.tot[GROUP : 2 * GROUP, :] = step
        m.tot[2 * GROUP : 3 * GROUP, :] = jnp.exp(run) * m.carried[pl.ds(r, 1), :]
        m.tot[3 * GROUP : 4 * GROUP, :] = jnp.exp(run[:, T - 1 : T] - run) * m.closing[pl.ds(r, 1), :]
        m.cols[row(r), :] = jnp.transpose(m.tot[...])
        for p in range(pairs):
            scaled = m.mix[row(r), pair(p)].astype(F32) * widened(m.cols[row(r), :], STEP, p)
            m.xs[row(r), pair(p)] = scaled.astype(BF16)
            m.xt[row(r), pair(p)] = (scaled * widened(m.cols[row(r), :], TRAIL, p)).astype(BF16)

    half_arrived()
    w_relay(3)
    m.vh[:, C:] = nn(m.nrmh[...], m.wall[:, C:V]).astype(BF16)

    @pl.loop(0, R)
    def _(r):
        m.v[row(r), C:] = nn(m.nrm[row(r), :], m.wall[:, C:V]).astype(BF16)
        convolve(r, (C, V))
        m.fresh[r] = tn(m.mix[row(r), C : C + LANES], m.xt[row(r), :])

        @pl.when(c == 0)
        def _():
            m.ssend[r] = m.fresh[r].astype(BF16)
            state_copy(r).start()

    @pl.loop(0, R)
    def _(r):
        b, cm = m.mix[row(r), C : C + LANES], m.mix[row(r), C + LANES : V]
        m.scores[...] = nt(cm, b) * m.past[r].astype(F32)
        for p in range(pairs):
            for a in range(0, T, LANES):
                rows, seen = slice(a, a + LANES), a + LANES
                here = pl.ds(pl.multiple_of(r * T, 16) + a, LANES)
                both = []
                for h in (2 * p, 2 * p + 1):
                    decay = jnp.exp(jnp.minimum(m.cols[here, h : h + 1] - m.runr[r, h : h + 1, :seen], 0.0))
                    weight = (decay * m.scores[rows, :seen]).astype(BF16)
                    both.append(nn(weight, m.xs[pl.ds(pl.multiple_of(r * T, 16), seen), pair(p)]))
                m.ins[here, pair(p)] = jnp.where(low_lanes[:LANES], both[0], both[1])

        @pl.when(c > 0)
        def _():
            state_copy(r).wait_recv()

            @pl.when(c < nc - 1)
            def _():
                m.ssend[r] = (m.fresh[r] + kept(r) * m.sin[r].astype(F32)).astype(BF16)
                state_copy(r).start()

    w_relay(4)
    w_rest(3)
    w_rest(4)

    def sums_copy(r, k):
        return copy(
            m.sums.at[t, r], m.sums.at[t, r], m.x_send.at[r, k], m.x_recv.at[r, t], (d, c, at_ten(k))
        )

    def sums_arrived(r, who):
        copy(
            m.sums.at[who, r], m.sums.at[who, r], m.x_send.at[r, 0], m.x_recv.at[r, who], (d, c, t)
        ).wait_recv()

    def mine(r):
        return pl.ds(pl.multiple_of(r * T + odd * half, 16), half)

    def theirs(r):
        return pl.ds(pl.multiple_of(r * T + (1 - odd) * half, 16), half)

    def near_copy(a, r):
        return copy(m.as_.at[a, r], m.ar_.at[a, r], m.a_send.at[a, r], m.a_recv.at[a, r], (d, c, across))

    def far_copy(a, r):
        return copy(m.bs_.at[a, r], m.br_.at[a, r], m.b_send.at[a, r], m.b_recv.at[a, r], (d, c, far))

    def back_copy(a, r):
        out = (m.ov, m.iv)[a].at[mine(r)]
        return copy(out, out, m.c_send.at[a, r], m.c_recv.at[a, r], (d, c, across))

    def back_arrived(a, r):
        out = (m.ov, m.iv)[a].at[theirs(r)]
        copy(out, out, m.c_send.at[a, r], m.c_recv.at[a, r], (d, c, across)).wait_recv()

    def give(a, r, value):
        first, second = value[:half], value[half:]
        m.as_[a, r] = jnp.where(odd == 0, second, first).astype(BF16)
        near_copy(a, r).start()
        m.keep[r] = jnp.where(odd == 0, first, second)

    def chip_sum(a, r):
        near_copy(a, r).wait_recv()
        m.bs_[a, r] = (m.keep[r] + m.ar_[a, r].astype(F32)).astype(BF16)
        if ntn == 4:
            far_copy(a, r).start()

    def full_sum(a, r):
        total = m.bs_[a, r].astype(F32)
        if ntn == 4:
            far_copy(a, r).wait_recv()
            total = total + m.br_[a, r].astype(F32)
        return total

    @pl.loop(0, R)
    def _(r):
        cm = m.mix[row(r), C + LANES : V]
        gate = nn(m.nrm[row(r), :], m.wall[:, Z:])
        m.zv[row(r), :] = gate.astype(BF16)
        m.dy[row(r), :] = nn(m.cv[row(r), :], m.wo[...])
        m.ys[row(r), :] = nn(cm, m.sin[r])
        squares = jnp.zeros((T, LANES), F32)
        inner = jnp.zeros((T, LANES), F32)
        for p in range(pairs):
            carried = m.ys[row(r), pair(p)] * widened(m.cols[row(r), :], LEAD, p)
            m.ys[row(r), pair(p)] = carried
            ssd = m.ins[row(r), pair(p)] + carried + m.par[6:7, pair(p)] * m.mix[row(r), pair(p)].astype(F32)
            m.ssd[row(r), pair(p)] = ssd
            gate = m.zv[row(r), pair(p)].astype(F32)
            gated = ssd * (gate * sigmoid(gate))
            m.gated[row(r), pair(p)] = gated
            scaled = gated * m.par[5:6, pair(p)]
            m.yg[row(r), pair(p)] = scaled.astype(BF16)
            squares = squares + gated * gated
            inner = inner + scaled * m.dy[row(r), pair(p)]
        squares = jnp.sum(squares, axis=-1, keepdims=True)
        inner = jnp.sum(inner, axis=-1, keepdims=True)
        both = jnp.where(lane == 0, squares, jnp.where(lane == 1, inner, 0.0))
        m.sums[t, r] = jnp.transpose(both)[0:8, :]
        for k in range(1, ntn):
            sums_copy(r, k).start()
        give(0, r, nt(m.yg[row(r), :], m.wo[...]))

    @pl.loop(0, R)
    def _(r):
        chip_sum(0, r)
        for k in range(1, ntn):
            sums_arrived(r, at_ten(k))
        total = m.sums[0, r]
        for who in range(1, ntn):
            total = total + m.sums[who, r]
        scale = lax.rsqrt(total[0:1] * (1.0 / (C * ntn)) + EPS)
        inner = total[1:2] * (1.0 / (C * ntn)) * scale * scale * scale
        m.tot[0:1, :] = scale
        m.tot[1:2, :] = inner
        columns = jnp.transpose(m.tot[...])
        m.rms[row(r), :] = columns
        scale = jnp.broadcast_to(columns[:, 0:1], (T, LANES))
        inner = jnp.broadcast_to(columns[:, 1:2], (T, LANES))
        for p in range(pairs):
            gated, dy, ssd = m.gated[row(r), pair(p)], m.dy[row(r), pair(p)], m.ssd[row(r), pair(p)]
            gate = m.zv[row(r), pair(p)].astype(F32)
            gain = m.par[5:6, pair(p)]
            normal = gated * scale
            m.sm[t, 5:6, pair(p)] += jnp.sum(dy * normal, axis=0, keepdims=True)
            m.yg[row(r), pair(p)] = (normal * gain).astype(BF16)
            d_gated = scale * dy * gain - gated * inner
            logistic = sigmoid(gate)
            m.dcat[row(r), Z + p * LANES : Z + (p + 1) * LANES] = (
                d_gated * ssd * (logistic * (1.0 + gate * (1.0 - logistic)))
            ).astype(BF16)
            d_ssd = d_gated * (gate * logistic)
            m.ssd[row(r), pair(p)] = d_ssd
            m.wds[row(r), pair(p)] = (d_ssd * widened(m.cols[row(r), :], LEAD, p)).astype(BF16)
        m.local[r] = tn(m.mix[row(r), C + LANES : V], m.wds[row(r), :])

        @pl.when(c == nc - 1)
        def _():
            m.gsend[r] = m.local[r].astype(BF16)
            if nc > 1:
                grad_copy(r).start()

    gall, gyr, gzs, gzr = (m.ga0, m.ga1, m.ga2), (m.gy0, m.gy1, m.gy2), (m.gz0, m.gz1, m.gz2), (m.gr0, m.gr1, m.gr2)
    tall = (rp, rp, rp + HALO)

    def rs_dp(part, j, k):
        cc = at_ctx(j)
        return copy(
            gall[part].at[rows_at(at_dp(k) * nc + cc, tall[part])],
            gyr[part].at[k - 1, rows_at(cc, tall[part])],
            m.ry_send.at[part, j, k - 1],
            m.ry_recv.at[part, j, k - 1],
            (at_dp(k), c, t),
        )

    def rs_ctx(part, j):
        cc = at_ctx(j)
        return copy(
            gzs[part].at[rows_at(cc, tall[part])],
            gzr[part].at[c],
            m.rz_send.at[part, j],
            m.rz_recv.at[part, c],
            (d, cc, t),
        )

    def rs_arrived(part, cc):
        copy(gzr[part].at[cc], gzr[part].at[cc], m.rz_send.at[part, 0], m.rz_recv.at[part, cc], (d, c, t)).wait_recv()

    def rs_start(part):
        for j in list(range(1, nc)) + [0]:
            for k in range(1, nd):
                rs_dp(part, j, k).start()

    def rs_middle(part, j):
        cc = at_ctx(j)
        total = gall[part][rows_at(d * nc + cc, tall[part]), :].astype(F32)
        for k in range(1, nd):
            rs_dp(part, j, k).wait_recv()
            total = total + gyr[part][k - 1, rows_at(cc, tall[part]), :].astype(F32)
        own = j == 0

        def keep():
            gzr[part][c] = total.astype(BF16)

        def send():
            gzs[part][rows_at(cc, tall[part]), :] = total.astype(BF16)
            rs_ctx(part, j).start()

        if isinstance(j, int):
            keep() if own else send()
        else:
            pl.when(own)(keep)
            pl.when(jnp.logical_not(own))(send)

    def rs_end(part):
        for k in range(1, nc):
            rs_arrived(part, at_ctx(k))
        total = gzr[part][0].astype(F32)
        for cc in range(1, nc):
            total = total + gzr[part][cc].astype(F32)
        return total

    def rs_sent(part):
        for j in range(nc):
            for k in range(1, nd):
                rs_dp(part, j, k).wait_send()
            if j:
                rs_ctx(part, j).wait_send()

    m.ga1[:, C:] = nn(m.cott[...], m.yg[...]).astype(BF16)
    m.ga1[:, :C] = nn(m.nrmt[...], m.dcat[:, Z:]).astype(BF16)
    rs_start(1)

    @pl.loop(0, R)
    def _(r):
        b, cm = m.mix[row(r), C : C + LANES], m.mix[row(r), C + LANES : V]
        m.scores[...] = nt(b, cm) * m.next[r].astype(F32)
        start = pl.multiple_of(r * T, 16)
        for a in range(0, T, LANES):
            rows, here, after = slice(a, a + LANES), pl.ds(start + a, LANES), pl.ds(start + a, T - a)
            losses = jnp.zeros((LANES, LANES), F32)
            for p in range(pairs):
                ds_pair = m.ssd[after, pair(p)].astype(BF16)
                xs_pair = m.xs[here, pair(p)]
                both = []
                for h in (2 * p, 2 * p + 1):
                    pick = low_lanes[:LANES] if h % 2 == 0 else ~low_lanes[:LANES]
                    decay = jnp.exp(jnp.minimum(m.runr[r, h : h + 1, a:] - m.cols[here, h : h + 1], 0.0))
                    weight = decay * m.scores[rows, a:]
                    both.append(nn(weight.astype(BF16), ds_pair))
                    d_weight = nt(jnp.where(pick, xs_pair, jnp.zeros_like(xs_pair)), ds_pair)
                    flow = d_weight * weight
                    if h == 0:
                        m.dsc[rows, a:] = d_weight * decay
                    else:
                        m.dsc[rows, a:] += d_weight * decay
                    losses = jnp.where(lane[:LANES] == h, jnp.sum(flow, axis=1, keepdims=True), losses)
                    down = jnp.sum(flow, axis=0, keepdims=True)
                    if a == 0:
                        m.drow[r, h : h + 1, :] = down
                    else:
                        m.drow[r, h : h + 1, a:] += down
                m.ins[here, pair(p)] = jnp.where(low_lanes[:LANES], both[0], both[1])
            m.drun[here, :] = exact_right(m.ssd[here, :] * m.ys[here, :], fold_run) - losses
            d_scores = (m.dsc[rows, a:] * m.next[r, rows, a:].astype(F32)).astype(BF16)
            m.gated[here, :LANES] = nn(d_scores, m.mix[after, C + LANES : V])
            d_after = tn(d_scores, m.mix[here, C : C + LANES])
            if a == 0:
                m.gated[after, LANES:S] = d_after
            else:
                m.gated[after, LANES:S] += d_after

        @pl.when(c < nc - 1)
        def _():
            grad_copy(r).wait_recv()

            @pl.when(c > 0)
            def _():
                m.gsend[r] = (m.local[r] + kept(r) * m.gin[r].astype(F32)).astype(BF16)
                grad_copy(r).start()

    def final_out(r):
        value = m.hv[mine(r), :].astype(F32) + m.rms[mine(r), 0:1] * full_sum(0, r)
        m.ov[mine(r), :] = value.astype(BF16)
        back_copy(0, r).start()

    def adjoint(r):
        b = m.mix[row(r), C : C + LANES]
        grad = m.gin[r]
        ring = lax.rem(r, 2)
        for p in range(pairs):
            trailing = widened(m.cols[row(r), :], TRAIL, p)
            reach = nn(b, m.gin[r, :, pair(p)]) * trailing
            x = m.mix[row(r), pair(p)].astype(F32)
            d_xs = m.ins[row(r), pair(p)] + reach
            d_ssd = m.ssd[row(r), pair(p)]
            m.prod[:, pair(p)] = m.xs[row(r), pair(p)].astype(F32) * reach
            m.prod[:, C + p * LANES : C + (p + 1) * LANES] = d_xs * x
            m.sm[t, 7:8, LANES + p * LANES : 2 * LANES + p * LANES] += jnp.sum(d_ssd * x, axis=0, keepdims=True)
            m.dcf[ring, :, pair(p)] = (
                d_xs * widened(m.cols[row(r), :], STEP, p) + m.par[6:7, pair(p)] * d_ssd
            ) * m.slope[row(r), pair(p)]
        m.dcf[ring, :, C : C + LANES] = (
            m.gated[row(r), :LANES] + nt(m.xt[row(r), :], grad)
        ) * m.slope[row(r), C : C + LANES]
        m.dcf[ring, :, C + LANES :] = (
            m.gated[row(r), LANES:S] + nt(m.wds[row(r), :], m.sin[r])
        ) * m.slope[row(r), C + LANES :]

        @pl.when(c > 0)
        def _():
            m.edge[r] = m.dcf[ring, 0:EDGE, :]
            edge_copy(r).start()

        m.drun[row(r), :] += exact_right(m.prod[:, :C], fold_through) + exact_right(m.prod[:, C:], fold_step)
        joint = jnp.sum(grad.astype(F32) * m.sin[r].astype(F32), axis=0, keepdims=True)
        joint = exact_right(jnp.broadcast_to(joint, (8, C)), fold_run)[0:1]
        last = m.cols[pl.ds(r * T + T - 1, 1), :]
        kept_lanes = jnp.concatenate([last[:, LEAD : LEAD + H], jnp.zeros((1, LANES - H), F32)], axis=1)
        m.drun[pl.ds(r * T + T - 1, 1), :] += joint * kept_lanes
        turned = jnp.transpose(m.drun[row(r), :])
        through = jnp.sum(turned[GROUP : 2 * GROUP], axis=1, keepdims=True)
        d_run = turned[0:GROUP] + m.drow[r]
        d_run = d_run + jnp.where(iota((GROUP, T), 1) == T - 1, through, 0.0)
        d_growth = exact_rows(d_run, m.lower[...])
        d_step = turned[2 * GROUP : 3 * GROUP] + rate_col * d_growth
        d_pre = d_step * sigmoid(m.pre[:, row(r)])
        m.hacc[0:GROUP, :] += d_pre
        m.hacc[GROUP : 2 * GROUP, :] += m.step[:, row(r)] * d_growth * rate_col
        d_pre = jnp.where(iota((GROUP, T), 0) < H, d_pre, 0.0)
        m.gstep[...] += nn(jnp.concatenate([d_pre, jnp.zeros_like(d_pre)], axis=0).astype(BF16), m.nrm[row(r), :])
        m.tot[0:GROUP, :] = d_pre
        m.dcat[row(r), V:Z] = jnp.transpose(m.tot[...]).astype(BF16)

    def finish(r):
        @pl.when(c < nc - 1)
        def _():
            edge_copy(r).wait_recv()

        ring = lax.rem(r, 2)
        for a in range(0, V, WIDE):
            part = slice(a, min(a + WIDE, V))
            d_conv = m.dcf[ring, :, part]
            low = d_conv.astype(BF16)
            after = m.dce[r, :, part]
            after = jnp.concatenate([after, jnp.zeros_like(after)], axis=0).astype(BF16)
            value = m.v[row(r), part].astype(F32)
            m.sm[t, 4:5, part] += jnp.sum(d_conv, axis=0, keepdims=True)
            m.sm[t, 0:1, part] += jnp.sum(d_conv * value, axis=0, keepdims=True)
            d_v = d_conv * m.par[0:1, part]
            for j in range(1, z.K):
                moved = nn(m.up[r, j - 1], low)
                last = nn(m.late[r, j - 1], after)
                moved = jnp.concatenate([moved[: T - HALO], moved[T - HALO :] + last], axis=0)
                d_v = d_v + moved * m.par[j : j + 1, part]
                m.sm[t, j : j + 1, part] += jnp.sum(moved * value, axis=0, keepdims=True)
            m.dcat[row(r), part] = d_v.astype(BF16)

        value = nt(m.dcat[row(r), :], m.wall[...])
        give(1, r, value)
        u = m.hv[row(r), :].astype(F32)
        mean = jnp.sum(u * u, axis=-1, keepdims=True) * (1.0 / z.d_true)
        m.sm[t, 6:7, :D] += jnp.sum(value * (u * lax.rsqrt(mean + EPS)), axis=0, keepdims=True)

    m.tot[...] = jnp.zeros_like(m.tot)

    @pl.loop(0, max(R + 2, nc))
    def _(i):
        @pl.when(i < R)
        def _():
            final_out(i)
            adjoint(i)

        @pl.when(i < nc)
        def _():
            rs_middle(1, lax.rem(i + 1, nc))

        @pl.when((i >= 1) & (i < R + 1))
        def _():
            finish(i - 1)

        @pl.when((i >= 2) & (i < R + 2))
        def _():
            chip_sum(1, i - 2)

    width = S // ntn
    quarters = [m.dcat[:, C + k * width : C + (k + 1) * width] for k in range(ntn)]
    value = nn(m.nrmt[...], jnp.concatenate(quarters[0::2] + quarters[1::2], axis=1))

    def share_copy():
        return copy(m.shs, m.shr, m.sh_send.at[0], m.sh_recv.at[0], (d, c, across))

    m.shk[...] = jnp.where(odd == 0, value[:, : z.Q], value[:, z.Q :])
    m.shs[...] = jnp.where(odd == 0, value[:, z.Q :], value[:, : z.Q]).astype(BF16)
    share_copy().start()

    def small_ten(k):
        return copy(m.sm.at[t], m.sm.at[t], m.st_send.at[k], m.st_recv.at[t], (d, c, at_ten(k)))

    def small_dp(k):
        return copy(m.sd.at[d], m.sd.at[d], m.sd_send.at[k], m.sd_recv.at[d], (at_dp(k), c, t))

    def small_ctx(k):
        return copy(m.sc.at[c], m.sc.at[c], m.sc_send.at[k], m.sc_recv.at[c], (d, at_ctx(k), t))

    def arrived(buf, sems, who):
        copy(buf.at[who], buf.at[who], sems.at[who], sems.at[who], (d, c, t)).wait_recv()

    m.tile[...] = jnp.zeros_like(m.tile)
    m.tile[0 : 2 * GROUP, :] = jnp.broadcast_to(
        jnp.sum(m.hacc[...], axis=1, keepdims=True), (2 * GROUP, LANES)
    )
    m.sm[t, 7:8, 0:LANES] = jnp.transpose(m.tile[...])[0:1, :]
    for k in range(1, ntn):
        small_ten(k).start()

    m.ga0[...] = nn(m.nrmt[...], m.dcat[:, :C]).astype(BF16)
    share_copy().wait_recv()
    for b in range(nd * nc):
        here = slice(b * rp, (b + 1) * rp)
        there = b * (rp + HALO)
        m.ga2[there : there + rp, :] = (m.shk[here, :] + m.shr[here, :].astype(F32)).astype(BF16)
        steps = m.gstep[:, here]
        m.ga2[there + rp : there + rp + HALO, :] = jnp.concatenate(
            [steps, jnp.zeros((HALO, LANES - rp), F32)], axis=1
        ).astype(BF16)
    rs_start(2)
    rs_start(0)

    for k in range(1, ntn):
        arrived(m.sm, m.st_recv, at_ten(k))
    common = m.sm[0]
    for who in range(1, ntn):
        common = common + m.sm[who]
    rows8, lanes8 = iota((8, z.WL), 0), iota((8, z.WL), 1)
    shared_here = (rows8 == 6) | ((rows8 < 5) & (lanes8 >= C))
    m.sd[d] = jnp.where(shared_here, common, m.sm[t])
    for k in range(1, nd):
        small_dp(k).start()

    def store(a, r):
        return pltpu.make_async_copy((m.ov, m.iv)[a].at[row(r)], (m.out, m.ing)[a].at[row(r)], m.l_out.at[a, r])

    for r in range(R):
        back_arrived(0, r)
        store(0, r).start()
    for j in list(range(1, nc)) + [0]:
        rs_middle(2, j)

    @pl.loop(0, R)
    def _(r):
        u = m.hv[mine(r), :].astype(F32)
        mean = jnp.sum(u * u, axis=-1, keepdims=True) * (1.0 / z.d_true)
        scale = lax.rsqrt(mean + EPS)
        unit = u * scale
        d_unit = full_sum(1, r) * gain_in
        inner = jnp.sum(d_unit * unit, axis=-1, keepdims=True) * (1.0 / z.d_true)
        value = m.cv[mine(r), :].astype(F32) + scale * (d_unit - unit * inner)
        m.iv[mine(r), :] = value.astype(BF16)
        back_copy(1, r).start()

        @pl.when(r < nc)
        def _():
            rs_middle(0, lax.rem(r + 1, nc))

    for j in range(R + 1, nc + 1):
        rs_middle(0, j % nc)

    for k in range(1, nd):
        arrived(m.sd, m.sd_recv, at_dp(k))
    total = m.sd[0]
    for who in range(1, nd):
        total = total + m.sd[who]
    m.sc[c] = total
    for k in range(1, nc):
        small_ctx(k).start()

    def last_copy():
        return copy(m.ls, m.lr, m.sh_send.at[1], m.sh_recv.at[1], (d, c, far))

    value = rs_end(2)
    if ntn == 4:
        m.ls[...] = value
        last_copy().start()
    else:
        m.gw2[...] = value
    m.gw1[...] = rs_end(1)

    for r in range(R):
        back_arrived(1, r)
        store(1, r).start()

    for k in range(1, nc):
        arrived(m.sc, m.sc_recv, at_ctx(k))
    total = m.sc[0]
    for who in range(1, nc):
        total = total + m.sc[who]
    m.small[...] = total

    if ntn == 4:
        last_copy().wait_recv()
        m.gw2[0:rp, :] = m.ls[0:rp, :] + m.lr[0:rp, :]
        m.gw2[rp:, :] = m.ls[rp:, :]
        last_copy().wait_send()

    m.gw0[...] = rs_end(0)

    for a in range(2):
        for r in range(R):
            store(a, r).wait()
            back_copy(a, r).wait_send()
            near_copy(a, r).wait_send()
            if ntn == 4:
                far_copy(a, r).wait_send()
    for p in range(PIECES):
        w_sent(p)
    half_copy().wait_send()
    for part in range(3):
        rs_sent(part)
    for r in range(R):
        for k in range(1, ntn):
            sums_copy(r, k).wait_send()

        @pl.when(c < nc - 1)
        def _():
            halo_copy(r).wait_send()
            state_copy(r).wait_send()

        @pl.when(c > 0)
        def _():
            grad_copy(r).wait_send()
            edge_copy(r).wait_send()

    share_copy().wait_send()
    for k in range(1, ntn):
        small_ten(k).wait_send()
    for k in range(1, nd):
        small_dp(k).wait_send()
    for k in range(1, nc):
        small_ctx(k).wait_send()


def finishing(z, out, ing, gw0, gw1, gw2, small, *outs):
    (o_out, o_ing, norm, heads, shared, step, taps, bias, staps, sbias, dsb, drate, dskip, gain, outw, tile, sems) = outs
    C, S, D, H, rp, rows = z.C, z.S, z.D, z.H, z.rp, z.rows
    V = C + S
    head = C // H
    moves = [pltpu.make_async_copy(out, o_out, sems.at[0]), pltpu.make_async_copy(ing, o_ing, sems.at[1])]
    for move in moves:
        move.start()
    norm[...] = small[6, :D]
    heads[:, 0, :] = gw1[0:rows, :C]
    heads[:, 1, :] = gw0[0:rows, :]
    width = S // z.ntn
    tile[...] = jnp.zeros_like(tile)
    tile[0:rp, :] = gw2[0:rp, :]
    pair = jnp.transpose(tile[...])
    if z.ntn == 4:
        upper = lax.axis_index("tensor") >= 2
        pair = jnp.where(upper, pair[width:], pair[:width])
    shared[...] = pair[:, 0:rows]
    step[...] = gw2[rp : rp + H, 0:rows]
    taps[...] = small[0 : z.K, :C]
    bias[...] = small[4, :C]
    staps[...] = small[0 : z.K, C:V]
    sbias[...] = small[4, C:V]
    dsb[...] = small[7, :H]
    drate[...] = small[7, GROUP : GROUP + H]
    lanes = iota((1, H), 1)
    skip = jnp.zeros((1, H), F32)
    for h in range(H):
        begin = LANES + h * head
        skip = jnp.where(lanes == h, jnp.sum(small[7:8, begin : begin + head], axis=1, keepdims=True), skip)
    tile[0:1, 0:H] = skip
    dskip[...] = tile[0, 0:H]
    gain[...] = small[5, :C]
    outw[...] = gw1[0:rows, C:]
    for move in moves:
        move.wait()


def on_device(z, hidden_in, segment_ids, norm_gain, head_projection, shared_projection, step_projection,
              conv_heads, bias_heads, conv_shared, bias_shared, step_bias, log_decay, skip_gain, gate_gain,
              output_weight, out_cotangent):
    R, T, D, C, H, S = z.R, z.T, z.D, z.C, z.H, z.S
    rp, nd, nc, ntn, rows = z.rp, z.nd, z.nc, z.ntn, z.rows
    V = C + S
    blocks = nd * nc
    R8 = 8 * -(-R // 8)

    def widen(value):
        if rp == rows:
            return value
        value = value.reshape(value.shape[:-1] + (blocks, rows))
        value = jnp.pad(value, [(0, 0)] * (value.ndim - 1) + [(0, rp - rows)])
        return value.reshape(value.shape[:-2] + (D,))

    def narrow(value):
        if rp == rows:
            return value
        return value.reshape(value.shape[:-1] + (blocks, rp))[..., :rows].reshape(value.shape[:-1] + (z.d_true,))

    def taller(value, dim):
        if rp == rows:
            return value
        return jnp.pad(value, [(0, rp - rows if k == dim else 0) for k in range(value.ndim)])

    dma, vmem = pltpu.SemaphoreType.DMA, pltpu.VMEM
    N = R * T
    half = T // 2
    k0 = max(nd - 1, 1)
    ins = dict(
        hid=widen(hidden_in.reshape(N, z.d_true)), cot=widen(out_cotangent.reshape(N, z.d_true)),
        seg=segment_ids, ng=widen(norm_gain), hp=taller(head_projection, 0),
        shp=taller(shared_projection, 0), stp=taller(step_projection.T, 1), ow=taller(output_weight.T, 0),
        ch=conv_heads, bh=bias_heads, cs=conv_shared, bs=bias_shared, sb=step_bias[None],
        ld=log_decay[None], sk=skip_gain[None], gg=gate_gain,
    )
    outs = dict(
        out=jax.ShapeDtypeStruct((N, D), BF16),
        ing=jax.ShapeDtypeStruct((N, D), BF16),
        gw0=jax.ShapeDtypeStruct((rp, C), F32),
        gw1=jax.ShapeDtypeStruct((rp, 2 * C), F32),
        gw2=jax.ShapeDtypeStruct((rp + HALO, z.Q), F32),
        small=jax.ShapeDtypeStruct((8, z.WL), F32),
    )
    scratch = dict(
        hv=vmem((N, D), BF16), cv=vmem((N, D), BF16), ov=vmem((N, D), BF16), iv=vmem((N, D), BF16),
        wall=vmem((D, V + LANES + C), BF16), wo=vmem((D, C), BF16), wt=vmem((blocks, GROUP, LANES), F32),
        wst=vmem((GROUP, D), F32), hcol=vmem((GROUP, LANES), F32), tile=vmem((LANES, LANES), F32), gain=vmem((8, D), F32), par=vmem((16, V), F32),
        segc=vmem((T, LANES), F32), segr=vmem((R8, T), F32), carried=vmem((R8, T), F32), closing=vmem((R8, T), F32),
        segb=vmem((R8, LANES), F32), sega=vmem((R8, LANES), F32),
        early=vmem((R, z.K - 1, EDGE, HALO), BF16), late=vmem((R, z.K - 1, HALO, HALO), BF16),
        down=vmem((R, z.K - 1, T, T), BF16), up=vmem((R, z.K - 1, T, T), BF16), lower=vmem((T, T), BF16), upper=vmem((T, T), BF16),
        past=vmem((R, T, T), BF16), next=vmem((R, T, T), BF16),
        hh=vmem((R * HALO, D), BF16), nrmh=vmem((R * HALO, D), BF16), vh=vmem((R * HALO, V), BF16),
        nrm=vmem((N, D), BF16), nrmt=vmem((D, N), BF16), cott=vmem((D, N), BF16),
        v=vmem((N, V), BF16), mix=vmem((N, V), BF16), slope=vmem((N, V), F32),
        pre=vmem((GROUP, N), F32), step=vmem((GROUP, N), F32), cols=vmem((N, LANES), F32), xt=vmem((N, C), BF16),
        runr=vmem((R, 8, T), F32), xs=vmem((N, C), BF16),
        fresh=vmem((R, LANES, C), F32), local=vmem((R, LANES, C), F32),
        ssend=vmem((R, LANES, C), BF16), sin=vmem((R, LANES, C), BF16),
        gsend=vmem((R, LANES, C), BF16), gin=vmem((R, LANES, C), BF16),
        scores=vmem((T, T), F32), dsc=vmem((T, T), F32), drow=vmem((R, GROUP, T), F32), tot=vmem((LANES, T), F32),
        ins=vmem((N, C), F32), ys=vmem((N, C), F32), ssd=vmem((N, C), F32), zv=vmem((N, C), BF16),
        gated=vmem((N, max(C, S)), F32), dy=vmem((N, C), F32),
        yg=vmem((N, C), BF16), wds=vmem((N, C), BF16),
        rms=vmem((N, LANES), F32), sums=vmem((ntn, R, 8, T), F32),
        as_=vmem((2, R, half, D), BF16), ar_=vmem((2, R, half, D), BF16),
        bs_=vmem((2, R, half, D), BF16), br_=vmem((2, R, half, D), BF16), keep=vmem((R, half, D), F32),
        ga0=vmem((D, C), BF16), ga1=vmem((D, 2 * C), BF16), ga2=vmem((blocks * (rp + HALO), z.Q), BF16),
        gy0=vmem((k0, nc * rp, C), BF16), gy1=vmem((k0, nc * rp, 2 * C), BF16), gy2=vmem((k0, nc * (rp + HALO), z.Q), BF16),
        gz0=vmem((nc * rp, C), BF16), gz1=vmem((nc * rp, 2 * C), BF16), gz2=vmem((nc * (rp + HALO), z.Q), BF16),
        gr0=vmem((nc, rp, C), BF16), gr1=vmem((nc, rp, 2 * C), BF16), gr2=vmem((nc, rp + HALO, z.Q), BF16),
        drun=vmem((N, LANES), F32), dcf=vmem((2, T, V), F32), edge=vmem((R, EDGE, V), F32),
        dce=vmem((R, EDGE, V), F32), dcat=vmem((N, V + LANES + C), BF16),
        prod=vmem((T, 2 * C), F32), hacc=vmem((2 * GROUP, T), F32), gstep=vmem((HALO, D), F32),
        shs=vmem((D, z.Q), BF16), shr=vmem((D, z.Q), BF16), shk=vmem((D, z.Q), F32),
        ls=vmem((rp + HALO, z.Q), F32), lr=vmem((rp + HALO, z.Q), F32),
        sm=vmem((ntn, 8, z.WL), F32), sd=vmem((nd, 8, z.WL), F32), sc=vmem((nc, 8, z.WL), F32),
        l_in=dma((2,)), l_out=dma((2, R)),
        wz_send=dma((PIECES, 2, nc)), wd_send=dma((PIECES, nc, nd)), w_recv=dma((PIECES, nd, nc)),
        h_send=dma((R,)), h_recv=dma((R,)),
        s_send=dma((R,)), s_recv=dma((R,)), g_send=dma((R,)), g_recv=dma((R,)), e_send=dma((R,)), e_recv=dma((R,)),
        x_send=dma((R, ntn)), x_recv=dma((R, ntn)),
        a_send=dma((2, R)), a_recv=dma((2, R)), b_send=dma((2, R)), b_recv=dma((2, R)),
        c_send=dma((2, R)), c_recv=dma((2, R)),
        ry_send=dma((3, nc, k0)), ry_recv=dma((3, nc, k0)), rz_send=dma((3, nc)), rz_recv=dma((3, nc)),
        sh_send=dma((3,)), sh_recv=dma((3,)),
        st_send=dma((ntn,)), st_recv=dma((ntn,)), sd_send=dma((nd,)), sd_recv=dma((nd,)),
        sc_send=dma((nc,)), sc_recv=dma((nc,)),
    )
    names = list(ins) + list(outs) + list(scratch)
    whole = pl.BlockSpec(memory_space=pltpu.VMEM)
    large = pl.BlockSpec(memory_space=pl.ANY)
    raw = pl.pallas_call(
        functools.partial(kernel, z, names),
        out_shape=list(outs.values()),
        in_specs=[large] * 2 + [whole] * (len(ins) - 2),
        out_specs=[large] * 2 + [whole] * (len(outs) - 2),
        scratch_shapes=list(scratch.values()),
        compiler_params=pltpu.CompilerParams(
            collective_id=0, has_side_effects=True, vmem_limit_bytes=z.limit
        ),
    )(*ins.values())

    shapes = [
        ((N, D), BF16), ((N, D), BF16), ((D,), F32), ((rows, 2, C), F32), ((S // ntn, rows), F32), ((H, rows), F32),
        ((z.K, C), F32), ((C,), F32), ((z.K, S), F32), ((S,), F32), ((H,), F32), ((H,), F32), ((H,), F32),
        ((C,), F32), ((rows, C), F32),
    ]
    outs = pl.pallas_call(
        functools.partial(finishing, z),
        out_shape=[jax.ShapeDtypeStruct(*shape) for shape in shapes],
        in_specs=[whole] * 6,
        out_specs=[large] * 2 + [whole] * (len(shapes) - 2),
        scratch_shapes=[vmem((LANES, LANES), F32), dma((2,))],
        compiler_params=pltpu.CompilerParams(vmem_limit_bytes=16 << 20),
    )(*raw)
    (block_out, input_grad, norm, heads, shared, step, taps, bias, staps, sbias, dsb, drate, dskip, gain, outw) = outs
    return (
        narrow(block_out).reshape(hidden_in.shape),
        narrow(input_grad).reshape(hidden_in.shape),
        narrow(norm),
        heads, shared.T, step.T, taps, bias, staps, sbias, dsb, drate, dskip, gain, outw.T,
    )


def solution(mesh):
    nd, nc, ntn = (mesh.shape[name] for name in ("dp", "context", "tensor"))

    def body(*args):
        hidden, heads, shared = args[0], args[3], args[4]
        micro, seqs, tokens, width = hidden.shape
        rows = heads.shape[0]
        rp = -(-rows // 16) * 16
        inner = heads.shape[2]
        z = types.SimpleNamespace(
            R=micro * seqs, T=tokens, d_true=width, D=rp * nd * nc, rows=rows, rp=rp, nd=nd, nc=nc, ntn=ntn,
            C=inner, H=args[10].shape[0], S=shared.shape[1], K=args[6].shape[0],
            Q=shared.shape[1] // 2, limit=62 << 20,
        )
        z.WL = max(inner + z.S, z.D, LANES + inner)
        return on_device(z, *args)

    return jax.shard_map(
        body,
        mesh=mesh,
        in_specs=(
            P(None, "dp", "context", None),
            P(None, "dp", None),
            P(),
            P(("dp", "context"), None, "tensor"),
            P(("dp", "context"), None),
            P(("dp", "context"), "tensor"),
            P(None, "tensor"),
            P("tensor"),
            P(),
            P(),
            P("tensor"),
            P("tensor"),
            P("tensor"),
            P("tensor"),
            P("tensor", ("dp", "context")),
            P(None, "dp", "context", None),
        ),
        out_specs=(
            P(None, "dp", "context", None),
            P(None, "dp", "context", None),
            P(),
            P(("dp", "context"), None, "tensor"),
            P(("dp", "context"), "tensor"),
            P(("dp", "context"), "tensor"),
            P(None, "tensor"),
            P("tensor"),
            P(),
            P(),
            P("tensor"),
            P("tensor"),
            P("tensor"),
            P("tensor"),
            P("tensor", ("dp", "context")),
        ),
        check_vma=False,
    )
```

time: 246 us -> 132 us (0.54)
  Pallas kernels: 228 us -> 124 us
  local copies, waits for them, and re-layouts: 13 us -> 6.23 us
  other arithmetic: 3.84 us -> 0 us
    pallas_call x1, Pallas kernels: 98.3 us -> 2.56 us  [on_device(): pl.pallas_call(functools.partial(finishing, z), out_shape=[jax.ShapeDtype...]
    pallas_call x1, Pallas kernels: 130 us -> 122 us  [on_device(): pl.pallas_call(functools.partial(kernel, z, names), out_shape=list(outs.v...]
    pallas_call x3 -> x0, other arithmetic: 3.84 us -> none  [on_device(): pl.pallas_call(functools.partial(finishing, z), out_shape=[jax.ShapeDtype...]
    broadcast_in_dim x3 -> x0, local copies, waits for them, and re-layouts: 3.76 us -> none  [the longest x1 1.27 us: on_device(): norm_gain[None]]
    unnamed x6 -> x12, local copies, waits for them, and re-layouts: 9.28 us -> 6.23 us
where the time goes in v3:
time: 132 us; the launch traced here: 131 us
  Pallas kernels  124 us (94%)
  local copies, waits for them, and re-layouts  6.23 us (5%)
    pallas_call x1, Pallas kernels, on_device(): pl.pallas_call(functools.partial(kernel, z, names), out_shape=list(outs.v...  122 us
    unnamed x12, local copies, waits for them, and re-layouts  6.23 us

profile of v3, /device:TPU:0, one launch (start us, length us, event | category | flops | bytes accessed | tf_op | source)
XLA Modules:
  0.0 131.3 jit_solution(2196266863415389235)
XLA Ops:
  0.7 121.9 %shard_map.271 = (bf16[1024,768]{1,0:T(8,128)(2,1)}, bf16[1024,768]{1,0:T(8,128)(2,1)}, f32[96,384]{1,0:T(8,128)}, f32[96,768]{1,0:T(8,128)}, f32[112,128]{1,0:T(8,128)}, /*index=5*/f32[8,768]{1,0:T(8,128)}) custom-call(bf16[1024,768]{1,0:T(8,128)(2,1)} %bitcast.12, bf16[1024,768]{1,0:T(8,128)(2,1)} %bitcast.13, s32[2,2,1024]{2,1,0:T(2,128)} %refs_2_.1, ...), custom_call_target="tpu_custom_call" | custom-call | tf_op jit(solution)/shard_map/pallas_call | solution.py:1063
  122.5 0.0 copy-start
  122.6 1.4 %copy-done = bf16[1024,768]{1,0:T(8,128)(2,1)S(1)} copy-done((bf16[1024,768]{1,0:T(8,128)(2,1)S(1)}, bf16[1024,768]{1,0:T(8,128)(2,1)}, u32[]{:S(2)}) %copy-start) | copy-done | bytes 1572888
  124.0 0.0 copy-start.1
  124.0 1.4 %copy-done.1 = bf16[1024,768]{1,0:T(8,128)(2,1)S(1)} copy-done((bf16[1024,768]{1,0:T(8,128)(2,1)S(1)}, bf16[1024,768]{1,0:T(8,128)(2,1)}, u32[]{:S(2)}) %copy-start.1) | copy-done | bytes 1572888
  125.4 0.0 copy-start.2
  125.4 1.0 copy-done.2
  126.3 0.0 copy-start.3
  126.3 0.9 copy-done.3
  127.2 0.0 copy-start.4
  127.2 0.8 copy-done.4
  128.1 0.0 copy-start.5
  128.1 0.7 copy-done.5
  128.8 2.6 %shard_map.272 = (bf16[1024,768]{1,0:T(8,128)(2,1)}, bf16[1024,768]{1,0:T(8,128)(2,1)}, f32[768]{0:T(1024)}, f32[96,2,384]{2,1,0:T(2,128)}, f32[64,96]{1,0:T(8,1...) custom-call(bf16[1024,768]{1,0:T(8,128)(2,1)S(1)} %copy-done, ...), custom_call_target="tpu_custom_call" | custom-call | tf_op jit(solution)/shard_map/pallas_call | solution.py:1079
Async XLA Ops:
  122.5 1.4 %copy-start = (bf16[1024,768]{1,0:T(8,128)(2,1)S(1)}, bf16[1024,768]{1,0:T(8,128)(2,1)}, u32[]{:S(2)}) copy-start(bf16[1024,768]{1,0:T(8,128)(2,1)} %get-tuple-element.36.out) | copy-start | bytes 4718596
  124.0 1.4 %copy-start.1 = (bf16[1024,768]{1,0:T(8,128)(2,1)S(1)}, bf16[1024,768]{1,0:T(8,128)(2,1)}, u32[]{:S(2)}) copy-start(bf16[1024,768]{1,0:T(8,128)(2,1)} %get-tuple-element.37.ing) | copy-start | bytes 4718596
  125.4 1.0 copy-start.2
  126.3 0.9 copy-start.3
  127.2 0.8 copy-start.4
  128.1 0.7 copy-start.5

commit v4 on v3

--- a/solution.py
+++ b/solution.py
@@ -15,7 +15,7 @@
 LANES = 128
 HALO = 16
 EDGE = 8
-PIECES = 5
+PIECES = 4
 WIDE = 256
 GROUP = 8
 
@@ -68,6 +68,8 @@
     head = C // H
     V = C + S
     Z = V + LANES
+    Q = z.Q
+    BX, CX = slice(0, Q), slice(Q + C, V)
     half = T // 2
     d, c, t = lax.axis_index("dp"), lax.axis_index("context"), lax.axis_index("tensor")
     odd = lax.rem(t, 2)
@@ -112,70 +114,85 @@
     for peer in peers:
         pl.semaphore_signal(barrier, inc=1, device_id=peer, device_id_type=MESH)
 
-    m.wall[block(d, c), 0:C] = m.hp[:, 1, :]
-    m.wall[block(d, c), lanes_at(C + odd * z.Q, z.Q)] = jnp.where(odd == 0, m.shp[:, : z.Q], m.shp[:, z.Q :])
+    m.wall[block(d, c), Q : Q + C] = m.hp[:, 1, :]
+    m.wall[block(d, c), lanes_at(odd * (Q + C), Q)] = jnp.where(odd == 0, m.shp[:, :Q], m.shp[:, Q:])
     m.wt[d * nc + c] = jnp.zeros((GROUP, LANES), F32)
     m.wt[d * nc + c, 0:H, 0:rp] = m.stp[...].astype(F32)
     pl.semaphore_wait(barrier, len(peers))
 
-    def slot(p, dd, cc):
-        if p == 2:
+    def subs(p):
+        return z.SUB if p == 0 else 1
+
+    def slot(p, dd, cc, u):
+        if p == 1:
             return m.wt.at[dd * nc + cc]
-        if p == 4:
+        if p == 3:
             return m.wo.at[block(dd, cc)]
-        place, size = ((0, C), (C + odd * z.Q, z.Q), None, (Z, C))[p]
-        return m.wall.at[block(dd, cc), lanes_at(place, size)]
-
-    def w_ctx(p, s, right):
-        to = c + s if right else c - s
-        here = slot(p, d, c)
-        return copy(here, here, m.wz_send.at[p, int(right), s], m.w_recv.at[p, d, c], (d, to, t))
-
-    def w_dp(p, cc, k):
-        here = slot(p, d, cc)
-        return copy(here, here, m.wd_send.at[p, cc, k], m.w_recv.at[p, d, cc], (at_dp(k), c, t))
-
-    def w_arrived(p, dd, cc):
-        there = slot(p, dd, cc)
-        copy(there, there, m.wd_send.at[p, cc, 0], m.w_recv.at[p, dd, cc], (d, c, t)).wait_recv()
+        place, size = ((odd * Q, Q + C), None, (Z, C))[p]
+        rows = rp // subs(p)
+        return m.wall.at[rows_at((dd * nc + cc) * subs(p) + u, rows), lanes_at(place, size)]
+
+    def w_ctx(p, u, s, right):
+        cc, to = (c - s, c + 1) if right else (c + s, c - 1)
+        here = slot(p, d, cc, u)
+        return copy(here, here, m.wz_send.at[p, int(right), s, u], m.w_recv.at[p, d, cc, u], (d, to, t))
+
+    def w_dp(p, u, cc, k):
+        here = slot(p, d, cc, u)
+        return copy(here, here, m.wd_send.at[p, cc, k, u], m.w_recv.at[p, d, cc, u], (at_dp(k), c, t))
+
+    def w_arrived(p, u, dd, cc):
+        there = slot(p, dd, cc, u)
+        copy(there, there, m.wd_send.at[p, cc, 0, u], m.w_recv.at[p, dd, cc, u], (d, c, t)).wait_recv()
+
+    def w_each(p, s, act):
+        for u in range(subs(p)):
+            if s < nc - 1:
+                pl.when((c - s >= 0) & (c < nc - 1))(lambda: act(w_ctx(p, u, s, True)))
+                pl.when((c + s < nc) & (c > 0))(lambda: act(w_ctx(p, u, s, False)))
+            for k in range(1, nd):
+                if s == 0:
+                    act(w_dp(p, u, c, k))
+                else:
+                    pl.when(c - s >= 0)(lambda: act(w_dp(p, u, c - s, k)))
+                    pl.when(c + s < nc)(lambda: act(w_dp(p, u, c + s, k)))
 
     def w_start(p):
-        for k in range(1, nd):
-            w_dp(p, c, k).start()
-        for s in range(1, nc):
-            pl.when(c + s < nc)(lambda: w_ctx(p, s, True).start())
-            pl.when(c - s >= 0)(lambda: w_ctx(p, s, False).start())
-
-    def w_relay(p):
-        def one(cc):
-            w_arrived(p, d, cc)
-            for k in range(1, nd):
-                w_dp(p, cc, k).start()
-
-        for s in range(1, nc):
-            pl.when(c - s >= 0)(lambda: one(c - s))
-            pl.when(c + s < nc)(lambda: one(c + s))
+        w_each(p, 0, lambda one: one.start())
+
+    def w_step(p, s):
+        for u in range(subs(p)):
+            for right in (True, False):
+                cc = c - s if right else c + s
+
+                @pl.when((cc >= 0) & (cc < nc))
+                def _():
+                    w_arrived(p, u, d, cc)
+                    if s < nc - 1:
+                        pl.when(c < nc - 1 if right else c > 0)(lambda: w_ctx(p, u, s, right).start())
+                    for k in range(1, nd):
+                        w_dp(p, u, cc, k).start()
 
     def w_rest(p):
         for k in range(1, nd):
             for cc in range(nc):
-                w_arrived(p, at_dp(k), cc)
+                for u in range(subs(p)):
+                    w_arrived(p, u, at_dp(k), cc)
 
     def w_sent(p):
-        for cc in range(nc):
-            for k in range(1, nd):
-                w_dp(p, cc, k).wait_send()
-        for s in range(1, nc):
-            pl.when(c + s < nc)(lambda: w_ctx(p, s, True).wait_send())
-            pl.when(c - s >= 0)(lambda: w_ctx(p, s, False).wait_send())
-
-    def half_copy():
-        here = m.wall.at[:, lanes_at(C + odd * z.Q, z.Q)]
-        return copy(here, here, m.sh_send.at[2], m.sh_recv.at[2], (d, c, across))
-
-    def half_arrived():
-        there = m.wall.at[:, lanes_at(C + (1 - odd) * z.Q, z.Q)]
-        copy(there, there, m.sh_send.at[2], m.sh_recv.at[2], (d, c, across)).wait_recv()
+        for s in range(nc):
+            w_each(p, s, lambda one: one.wait_send())
+
+    def half_rows(dd):
+        return rows_at(dd, nc * rp)
+
+    def half_copy(k):
+        here = m.wall.at[half_rows(at_dp(k)), lanes_at(odd * (Q + C), Q)]
+        return copy(here, here, m.wh_send.at[k], m.wh_recv.at[k], (d, c, across))
+
+    def half_arrived(k):
+        there = m.wall.at[half_rows(at_dp(k)), lanes_at((1 - odd) * (Q + C), Q)]
+        copy(there, there, m.wh_send.at[k], m.wh_recv.at[k], (d, c, across)).wait_recv()
 
     def halo_copy(r):
         return copy(
@@ -186,8 +203,8 @@
             (d, c + 1, t),
         )
 
-    for p in range(3):
-        w_start(p)
+    w_start(0)
+    w_start(1)
     load(0).wait()
 
     @pl.when(c < nc - 1)
@@ -198,10 +215,13 @@
     m.wall[block(d, c), Z:] = m.hp[:, 0, :]
     m.wo[block(d, c), :] = m.ow[...]
 
-    m.par[0 : z.K, :C] = m.ch[...]
-    m.par[0 : z.K, C:] = m.cs[...]
-    m.par[4:5, :C] = m.bh[...][None]
-    m.par[4:5, C:] = m.bs[...][None]
+    m.par[0 : z.K, BX] = m.cs[:, :Q]
+    m.par[0 : z.K, Q : Q + C] = m.ch[...]
+    m.par[0 : z.K, CX] = m.cs[:, Q:]
+    m.par[5:6, :S] = m.bs[...][None]
+    m.par[4:5, BX] = m.par[5:6, :Q]
+    m.par[4:5, Q : Q + C] = m.bh[...][None]
+    m.par[4:5, CX] = m.par[5:6, Q:S]
     m.par[5:6, :C] = m.gg[...][None]
     for h in range(H):
         m.par[6:7, h * head : (h + 1) * head] = jnp.broadcast_to(m.sk[0:1, h : h + 1], (1, head))
@@ -271,13 +291,26 @@
         m.nrm[row(r), :] = value
         m.nrmt[:, row(r)] = jnp.transpose(value)
 
-    w_relay(0)
-    w_start(3)
     load(1).wait()
 
     @pl.loop(0, R)
     def _(r):
         m.cott[:, row(r)] = jnp.transpose(m.cv[row(r), :])
+
+    reach = iota((HALO, HALO), 1) - HALO - iota((HALO, HALO), 0)
+    ahead = iota((HALO, HALO), 1) + HALO - iota((HALO, HALO), 0)
+    m.early[...] = jnp.zeros_like(m.early)
+    for r in range(R):
+        near = m.segc[0:HALO, r : r + 1] == m.segb[r : r + 1, LANES - HALO : LANES]
+        late = m.segc[T - HALO : T, r : r + 1] == m.sega[r : r + 1, 0:HALO]
+        for j in range(1, z.K):
+            first = ((r * (z.K - 1)) + j - 1) * HALO
+            m.early[first : first + HALO, r * HALO : (r + 1) * HALO] = (near & (reach == -j)).astype(BF16)
+            m.late[r, (j - 1) * HALO : j * HALO, :] = (late & (ahead == j)).astype(BF16)
+
+    w_step(0, 1)
+    w_start(2)
+    w_step(1, 1)
 
     @pl.when(c > 0)
     def _():
@@ -285,10 +318,20 @@
             halo_copy(r).wait_recv()
 
     m.nrmh[...] = normalize(m.hh[...]).astype(BF16)
-    w_relay(1)
-    w_relay(2)
-    w_start(4)
+    for s in range(2, nc):
+        w_step(0, s)
+        w_step(1, s)
+    half_copy(0).start()
+    w_start(3)
+    w_rest(1)
+
+    m.tile[...] = jnp.zeros_like(m.tile)
+    for b in range(nd * nc):
+        m.tile[0:GROUP, :] = m.wt[b]
+        m.wall[b * rp : (b + 1) * rp, V:Z] = jnp.transpose(m.tile[...])[0:rp, :].astype(BF16)
     w_rest(0)
+    for k in range(1, nd):
+        half_copy(k).start()
 
     low_lanes = iota((T, LANES), 1) < head
     lane = iota((T, LANES), 1)
@@ -322,59 +365,61 @@
     def pair(p):
         return slice(p * LANES, (p + 1) * LANES)
 
-    def convolve(r, lanes):
-        reach = iota((EDGE, HALO), 1) - HALO - iota((EDGE, HALO), 0)
-        seg = m.past[r]
-        for a in range(lanes[0], lanes[1], WIDE):
-            part = slice(a, min(a + WIDE, lanes[1]))
-            value = m.v[row(r), part]
-            before = m.vh[rows_at(r, HALO), part]
-            conv = value.astype(F32) * m.par[0:1, part] + m.par[4:5, part]
-            first = jnp.zeros((EDGE, conv.shape[1]), F32)
-            for j in range(1, z.K):
-                tap = m.par[j : j + 1, part]
-                conv = conv + nn(m.down[r, j - 1], value) * tap
-                first = first + nn(m.early[r, j - 1], before) * tap
-            conv = jnp.concatenate([conv[0:EDGE] + first, conv[EDGE:]], axis=0)
-            logistic = sigmoid(conv)
-            m.mix[row(r), part] = (conv * logistic).astype(BF16)
-            m.slope[row(r), part] = logistic * (1.0 + conv * (1.0 - logistic))
-
-    reach = iota((HALO, HALO), 1) - HALO - iota((HALO, HALO), 0)
-    ahead = iota((HALO, HALO), 1) + HALO - iota((HALO, HALO), 0)
-    for r in range(R):
-        near = m.segc[0:HALO, r : r + 1] == m.segb[r : r + 1, LANES - HALO : LANES]
-        late = m.segc[T - HALO : T, r : r + 1] == m.sega[r : r + 1, 0:HALO]
-        for j in range(1, z.K):
-            m.early[r, j - 1] = (near & (reach == -j)).astype(BF16)[0:EDGE]
-            m.late[r, j - 1] = (late & (ahead == j)).astype(BF16)
-
-    m.vh[:, :C] = nn(m.nrmh[...], m.wall[:, :C]).astype(BF16)
+    def lanes_of(p):
+        return slice(Q + p * LANES, Q + (p + 1) * LANES)
+
+    def serve_state(r):
+        state_copy(r).wait_recv()
+
+        @pl.when(c < nc - 1)
+        def _():
+            m.ssend[r] = (m.fresh[r] + kept(r) * m.sin[r].astype(F32)).astype(BF16)
+            state_copy(r).start()
+
+    def serve_grad(r):
+        grad_copy(r).wait_recv()
+
+        @pl.when(c > 0)
+        def _():
+            m.gsend[r] = (m.local[r] + kept(r) * m.gin[r].astype(F32)).astype(BF16)
+            grad_copy(r).start()
+
+    hops = nc - 1 - c
+    soon = R == 4 and nc > 2
+    if soon:
+        state_late = (c > 2) | ((c == 2) & (nc > 3))
+        grad_late = hops > 2
+    else:
+        state_late, grad_late = c > 0, hops > 0
+
+    def state_point(place, r):
+        if soon:
+            for who, item in place:
+                @pl.when((c == who) & r)
+                def _():
+                    serve_state(item)
+
+    def grad_point(place, r):
+        if soon:
+            for who, item in place:
+                @pl.when((hops == who) & r)
+                def _():
+                    serve_grad(item)
+
+    for k in range(nd):
+        half_arrived(k)
+    halo_v = nn(m.nrmh[...], m.wall[:, :V]).astype(BF16)
+    m.hfix[...] = nn(m.early[...], halo_v)
 
     @pl.loop(0, R)
     def _(r):
-        m.v[row(r), :C] = nn(m.nrm[row(r), :], m.wall[:, :C]).astype(BF16)
-        convolve(r, (0, C))
-
-    w_rest(1)
-    half_copy().start()
-    w_rest(2)
-    m.wst[...] = jnp.concatenate([m.wt[b, :, 0:rp] for b in range(nd * nc)], axis=1)
-    raw = nn(
-        jnp.concatenate([m.wst[...], jnp.zeros((GROUP, D), F32)], axis=0).astype(BF16), m.nrmt[...]
-    )[0:GROUP]
-    pre = raw.astype(BF16).astype(F32) + bias_col
-    m.pre[...] = pre
-    m.step[...] = jnp.maximum(pre, 0.0) + jnp.log1p(jnp.exp(-jnp.abs(pre)))
-
-    m.tile[...] = jnp.zeros_like(m.tile)
-    for b in range(nd * nc):
-        m.tile[0:GROUP, :] = m.wt[b]
-        m.wall[b * rp : (b + 1) * rp, V:Z] = jnp.transpose(m.tile[...])[0:rp, :].astype(BF16)
-
-    @pl.loop(0, R)
-    def _(r):
-        step = m.step[:, row(r)]
+        acc = nn(m.nrm[row(r), :], m.wall[:, :Z])
+        m.v[row(r), :] = acc[:, :V].astype(BF16)
+        raw = jnp.transpose(acc[:, V:].astype(BF16).astype(F32))[0:GROUP]
+        pre = raw + bias_col
+        step = jnp.maximum(pre, 0.0) + jnp.log1p(jnp.exp(-jnp.abs(pre)))
+        m.pre[:, row(r)] = pre
+        m.step[:, row(r)] = step
         run = exact_rows(step * rate_col, m.upper[...])
         m.runr[r] = run
         m.tot[0:GROUP, :] = run
@@ -382,29 +427,42 @@
         m.tot[2 * GROUP : 3 * GROUP, :] = jnp.exp(run) * m.carried[pl.ds(r, 1), :]
         m.tot[3 * GROUP : 4 * GROUP, :] = jnp.exp(run[:, T - 1 : T] - run) * m.closing[pl.ds(r, 1), :]
         m.cols[row(r), :] = jnp.transpose(m.tot[...])
+        for a in range(0, V, WIDE):
+            part = slice(a, min(a + WIDE, V))
+            value = m.v[row(r), part]
+            conv = value.astype(F32) * m.par[0:1, part] + m.par[4:5, part]
+            first = jnp.zeros((EDGE, conv.shape[1]), F32)
+            for j in range(1, z.K):
+                tap = m.par[j : j + 1, part]
+                conv = conv + nn(m.down[r, j - 1], value) * tap
+                first = first + m.hfix[pl.ds((r * (z.K - 1) + j - 1) * HALO, EDGE), part] * tap
+            conv = jnp.concatenate([conv[0:EDGE] + first, conv[EDGE:]], axis=0)
+            logistic = sigmoid(conv)
+            m.mix[row(r), part] = (conv * logistic).astype(BF16)
+            m.slope[row(r), part] = logistic * (1.0 + conv * (1.0 - logistic))
+        state_point([(1, 0)], r == 2)
+        state_point([(1, 1)], r == 3)
         for p in range(pairs):
-            scaled = m.mix[row(r), pair(p)].astype(F32) * widened(m.cols[row(r), :], STEP, p)
+            scaled = m.mix[row(r), lanes_of(p)].astype(F32) * widened(m.cols[row(r), :], STEP, p)
             m.xs[row(r), pair(p)] = scaled.astype(BF16)
             m.xt[row(r), pair(p)] = (scaled * widened(m.cols[row(r), :], TRAIL, p)).astype(BF16)
-
-    half_arrived()
-    w_relay(3)
-    m.vh[:, C:] = nn(m.nrmh[...], m.wall[:, C:V]).astype(BF16)
+        m.fresh[r] = tn(m.mix[row(r), BX], m.xt[row(r), :])
+
+        @pl.when(c == 0)
+        def _():
+            m.ssend[r] = m.fresh[r].astype(BF16)
+            state_copy(r).start()
+
+        for s in range(1, min(nc, R + 1)):
+            pl.when(r == s - 1)(lambda: w_step(2, s))
+
+    for s in range(R + 1, nc):
+        w_step(2, s)
+    state_point([(2, 0)], True)
 
     @pl.loop(0, R)
     def _(r):
-        m.v[row(r), C:] = nn(m.nrm[row(r), :], m.wall[:, C:V]).astype(BF16)
-        convolve(r, (C, V))
-        m.fresh[r] = tn(m.mix[row(r), C : C + LANES], m.xt[row(r), :])
-
-        @pl.when(c == 0)
-        def _():
-            m.ssend[r] = m.fresh[r].astype(BF16)
-            state_copy(r).start()
-
-    @pl.loop(0, R)
-    def _(r):
-        b, cm = m.mix[row(r), C : C + LANES], m.mix[row(r), C + LANES : V]
+        b, cm = m.mix[row(r), BX], m.mix[row(r), CX]
         m.scores[...] = nt(cm, b) * m.past[r].astype(F32)
         for p in range(pairs):
             for a in range(0, T, LANES):
@@ -416,19 +474,16 @@
                     weight = (decay * m.scores[rows, :seen]).astype(BF16)
                     both.append(nn(weight, m.xs[pl.ds(pl.multiple_of(r * T, 16), seen), pair(p)]))
                 m.ins[here, pair(p)] = jnp.where(low_lanes[:LANES], both[0], both[1])
-
-        @pl.when(c > 0)
-        def _():
-            state_copy(r).wait_recv()
-
-            @pl.when(c < nc - 1)
-            def _():
-                m.ssend[r] = (m.fresh[r] + kept(r) * m.sin[r].astype(F32)).astype(BF16)
-                state_copy(r).start()
-
-    w_relay(4)
+        for s in range(1, min(nc, R + 1)):
+            pl.when(r == s - 1)(lambda: w_step(3, s))
+        state_point([(1, 2)], r == 0)
+        state_point([(2, 1)], r == 2)
+
+    for s in range(R + 1, nc):
+        w_step(3, s)
+    state_point([(1, 3)], True)
+    w_rest(2)
     w_rest(3)
-    w_rest(4)
 
     def sums_copy(r, k):
         return copy(
@@ -479,9 +534,15 @@
             total = total + m.br_[a, r].astype(F32)
         return total
 
-    @pl.loop(0, R)
-    def _(r):
-        cm = m.mix[row(r), C + LANES : V]
+    def serve_late(r):
+        if soon and nc > 3:
+            pl.when((c > 2) | (r >= 2))(lambda: serve_state(r))
+        else:
+            serve_state(r)
+
+    def gating(r):
+        pl.when(state_late)(lambda: serve_late(r))
+        cm = m.mix[row(r), CX]
         gate = nn(m.nrm[row(r), :], m.wall[:, Z:])
         m.zv[row(r), :] = gate.astype(BF16)
         m.dy[row(r), :] = nn(m.cv[row(r), :], m.wo[...])
@@ -491,7 +552,7 @@
         for p in range(pairs):
             carried = m.ys[row(r), pair(p)] * widened(m.cols[row(r), :], LEAD, p)
             m.ys[row(r), pair(p)] = carried
-            ssd = m.ins[row(r), pair(p)] + carried + m.par[6:7, pair(p)] * m.mix[row(r), pair(p)].astype(F32)
+            ssd = m.ins[row(r), pair(p)] + carried + m.par[6:7, pair(p)] * m.mix[row(r), lanes_of(p)].astype(F32)
             m.ssd[row(r), pair(p)] = ssd
             gate = m.zv[row(r), pair(p)].astype(F32)
             gated = ssd * (gate * sigmoid(gate))
@@ -508,9 +569,7 @@
             sums_copy(r, k).start()
         give(0, r, nt(m.yg[row(r), :], m.wo[...]))
 
-    @pl.loop(0, R)
-    def _(r):
-        chip_sum(0, r)
+    def ungating(r):
         for k in range(1, ntn):
             sums_arrived(r, at_ten(k))
         total = m.sums[0, r]
@@ -539,13 +598,25 @@
             d_ssd = d_gated * (gate * logistic)
             m.ssd[row(r), pair(p)] = d_ssd
             m.wds[row(r), pair(p)] = (d_ssd * widened(m.cols[row(r), :], LEAD, p)).astype(BF16)
-        m.local[r] = tn(m.mix[row(r), C + LANES : V], m.wds[row(r), :])
+        m.local[r] = tn(m.mix[row(r), CX], m.wds[row(r), :])
 
         @pl.when(c == nc - 1)
         def _():
             m.gsend[r] = m.local[r].astype(BF16)
             if nc > 1:
                 grad_copy(r).start()
+
+    @pl.loop(0, R + 1)
+    def _(i):
+        pl.when(i < R)(lambda: gating(i))
+
+        @pl.when(i >= 1)
+        def _():
+            ungating(i - 1)
+
+        grad_point([(1, 0)], i == 3)
+        grad_point([(1, 1)], i == 4)
+        pl.when(i >= 1)(lambda: chip_sum(0, i - 1))
 
     gall, gyr, gzs, gzr = (m.ga0, m.ga1, m.ga2), (m.gy0, m.gy1, m.gy2), (m.gz0, m.gz1, m.gz2), (m.gr0, m.gr1, m.gr2)
     tall = (rp, rp, rp + HALO)
@@ -617,10 +688,11 @@
     m.ga1[:, C:] = nn(m.cott[...], m.yg[...]).astype(BF16)
     m.ga1[:, :C] = nn(m.nrmt[...], m.dcat[:, Z:]).astype(BF16)
     rs_start(1)
+    grad_point([(1, 2), (2, 0)], True)
 
     @pl.loop(0, R)
     def _(r):
-        b, cm = m.mix[row(r), C : C + LANES], m.mix[row(r), C + LANES : V]
+        b, cm = m.mix[row(r), BX], m.mix[row(r), CX]
         m.scores[...] = nt(b, cm) * m.next[r].astype(F32)
         start = pl.multiple_of(r * T, 16)
         for a in range(0, T, LANES):
@@ -650,21 +722,16 @@
                 m.ins[here, pair(p)] = jnp.where(low_lanes[:LANES], both[0], both[1])
             m.drun[here, :] = exact_right(m.ssd[here, :] * m.ys[here, :], fold_run) - losses
             d_scores = (m.dsc[rows, a:] * m.next[r, rows, a:].astype(F32)).astype(BF16)
-            m.gated[here, :LANES] = nn(d_scores, m.mix[after, C + LANES : V])
-            d_after = tn(d_scores, m.mix[here, C : C + LANES])
+            m.gated[here, :LANES] = nn(d_scores, m.mix[after, CX])
+            d_after = tn(d_scores, m.mix[here, BX])
             if a == 0:
                 m.gated[after, LANES:S] = d_after
             else:
                 m.gated[after, LANES:S] += d_after
 
-        @pl.when(c < nc - 1)
-        def _():
-            grad_copy(r).wait_recv()
-
-            @pl.when(c > 0)
-            def _():
-                m.gsend[r] = (m.local[r] + kept(r) * m.gin[r].astype(F32)).astype(BF16)
-                grad_copy(r).start()
+        grad_point([(1, 3), (2, 1)], r == 0)
+        grad_point([(2, 2)], r == 1)
+        grad_point([(2, 3)], r == 2)
 
     def final_out(r):
         value = m.hv[mine(r), :].astype(F32) + m.rms[mine(r), 0:1] * full_sum(0, r)
@@ -672,27 +739,28 @@
         back_copy(0, r).start()
 
     def adjoint(r):
-        b = m.mix[row(r), C : C + LANES]
+        pl.when(grad_late)(lambda: serve_grad(r))
+        b = m.mix[row(r), BX]
         grad = m.gin[r]
         ring = lax.rem(r, 2)
         for p in range(pairs):
             trailing = widened(m.cols[row(r), :], TRAIL, p)
             reach = nn(b, m.gin[r, :, pair(p)]) * trailing
-            x = m.mix[row(r), pair(p)].astype(F32)
+            x = m.mix[row(r), lanes_of(p)].astype(F32)
             d_xs = m.ins[row(r), pair(p)] + reach
             d_ssd = m.ssd[row(r), pair(p)]
             m.prod[:, pair(p)] = m.xs[row(r), pair(p)].astype(F32) * reach
             m.prod[:, C + p * LANES : C + (p + 1) * LANES] = d_xs * x
             m.sm[t, 7:8, LANES + p * LANES : 2 * LANES + p * LANES] += jnp.sum(d_ssd * x, axis=0, keepdims=True)
-            m.dcf[ring, :, pair(p)] = (
+            m.dcf[ring, :, lanes_of(p)] = (
                 d_xs * widened(m.cols[row(r), :], STEP, p) + m.par[6:7, pair(p)] * d_ssd
-            ) * m.slope[row(r), pair(p)]
-        m.dcf[ring, :, C : C + LANES] = (
+            ) * m.slope[row(r), lanes_of(p)]
+        m.dcf[ring, :, BX] = (
             m.gated[row(r), :LANES] + nt(m.xt[row(r), :], grad)
-        ) * m.slope[row(r), C : C + LANES]
-        m.dcf[ring, :, C + LANES :] = (
+        ) * m.slope[row(r), BX]
+        m.dcf[ring, :, CX] = (
             m.gated[row(r), LANES:S] + nt(m.wds[row(r), :], m.sin[r])
-        ) * m.slope[row(r), C + LANES :]
+        ) * m.slope[row(r), CX]
 
         @pl.when(c > 0)
         def _():
@@ -725,24 +793,27 @@
             edge_copy(r).wait_recv()
 
         ring = lax.rem(r, 2)
+        edge = m.dce[r]
+        edge = jnp.concatenate([edge, jnp.zeros_like(edge)], axis=0).astype(BF16)
+        m.lfix[...] = nn(m.late[r], edge)
         for a in range(0, V, WIDE):
             part = slice(a, min(a + WIDE, V))
             d_conv = m.dcf[ring, :, part]
             low = d_conv.astype(BF16)
-            after = m.dce[r, :, part]
-            after = jnp.concatenate([after, jnp.zeros_like(after)], axis=0).astype(BF16)
             value = m.v[row(r), part].astype(F32)
             m.sm[t, 4:5, part] += jnp.sum(d_conv, axis=0, keepdims=True)
             m.sm[t, 0:1, part] += jnp.sum(d_conv * value, axis=0, keepdims=True)
             d_v = d_conv * m.par[0:1, part]
             for j in range(1, z.K):
                 moved = nn(m.up[r, j - 1], low)
-                last = nn(m.late[r, j - 1], after)
-                moved = jnp.concatenate([moved[: T - HALO], moved[T - HALO :] + last], axis=0)
+                moved = jnp.concatenate(
+                    [moved[: T - HALO], moved[T - HALO :] + m.lfix[(j - 1) * HALO : j * HALO, part]], axis=0
+                )
                 d_v = d_v + moved * m.par[j : j + 1, part]
                 m.sm[t, j : j + 1, part] += jnp.sum(moved * value, axis=0, keepdims=True)
             m.dcat[row(r), part] = d_v.astype(BF16)
 
+    def finish_norm(r):
         value = nt(m.dcat[row(r), :], m.wall[...])
         give(1, r, value)
         u = m.hv[row(r), :].astype(F32)
@@ -751,7 +822,7 @@
 
     m.tot[...] = jnp.zeros_like(m.tot)
 
-    @pl.loop(0, max(R + 2, nc))
+    @pl.loop(0, max(R + 1, nc))
     def _(i):
         @pl.when(i < R)
         def _():
@@ -766,12 +837,17 @@
         def _():
             finish(i - 1)
 
-        @pl.when((i >= 2) & (i < R + 2))
+        @pl.when((i >= 1) & (i < R))
+        def _():
+            finish_norm(i - 1)
+
+        @pl.when((i >= 2) & (i < R + 1))
         def _():
             chip_sum(1, i - 2)
 
     width = S // ntn
-    quarters = [m.dcat[:, C + k * width : C + (k + 1) * width] for k in range(ntn)]
+    starts = [k * width + (C if k * width >= Q else 0) for k in range(ntn)]
+    quarters = [m.dcat[:, first : first + width] for first in starts]
     value = nn(m.nrmt[...], jnp.concatenate(quarters[0::2] + quarters[1::2], axis=1))
 
     def share_copy():
@@ -793,15 +869,7 @@
     def arrived(buf, sems, who):
         copy(buf.at[who], buf.at[who], sems.at[who], sems.at[who], (d, c, t)).wait_recv()
 
-    m.tile[...] = jnp.zeros_like(m.tile)
-    m.tile[0 : 2 * GROUP, :] = jnp.broadcast_to(
-        jnp.sum(m.hacc[...], axis=1, keepdims=True), (2 * GROUP, LANES)
-    )
-    m.sm[t, 7:8, 0:LANES] = jnp.transpose(m.tile[...])[0:1, :]
-    for k in range(1, ntn):
-        small_ten(k).start()
-
-    m.ga0[...] = nn(m.nrmt[...], m.dcat[:, :C]).astype(BF16)
+    m.ga0[...] = nn(m.nrmt[...], m.dcat[:, Q : Q + C]).astype(BF16)
     share_copy().wait_recv()
     for b in range(nd * nc):
         here = slice(b * rp, (b + 1) * rp)
@@ -813,6 +881,16 @@
         ).astype(BF16)
     rs_start(2)
     rs_start(0)
+    finish_norm(R - 1)
+    m.tile[...] = jnp.zeros_like(m.tile)
+    m.tile[0 : 2 * GROUP, :] = jnp.broadcast_to(
+        jnp.sum(m.hacc[...], axis=1, keepdims=True), (2 * GROUP, LANES)
+    )
+    m.sm[t, 7:8, 0:LANES] = jnp.transpose(m.tile[...])[0:1, :]
+    for k in range(1, ntn):
+        small_ten(k).start()
+
+    chip_sum(1, R - 1)
 
     for k in range(1, ntn):
         arrived(m.sm, m.st_recv, at_ten(k))
@@ -820,7 +898,7 @@
     for who in range(1, ntn):
         common = common + m.sm[who]
     rows8, lanes8 = iota((8, z.WL), 0), iota((8, z.WL), 1)
-    shared_here = (rows8 == 6) | ((rows8 < 5) & (lanes8 >= C))
+    shared_here = (rows8 == 6) | ((rows8 < 5) & ((lanes8 < Q) | (lanes8 >= Q + C)))
     m.sd[d] = jnp.where(shared_here, common, m.sm[t])
     for k in range(1, nd):
         small_dp(k).start()
@@ -901,7 +979,8 @@
                 far_copy(a, r).wait_send()
     for p in range(PIECES):
         w_sent(p)
-    half_copy().wait_send()
+    for k in range(nd):
+        half_copy(k).wait_send()
     for part in range(3):
         rs_sent(part)
     for r in range(R):
@@ -947,10 +1026,12 @@
         pair = jnp.where(upper, pair[width:], pair[:width])
     shared[...] = pair[:, 0:rows]
     step[...] = gw2[rp : rp + H, 0:rows]
-    taps[...] = small[0 : z.K, :C]
-    bias[...] = small[4, :C]
-    staps[...] = small[0 : z.K, C:V]
-    sbias[...] = small[4, C:V]
+    Q = z.Q
+    taps[...] = small[0 : z.K, Q : Q + C]
+    bias[...] = small[4, Q : Q + C]
+    staps[:, :Q] = small[0 : z.K, :Q]
+    staps[:, Q:] = small[0 : z.K, Q + C : V]
+    sbias[...] = jnp.concatenate([small[4:5, :Q], small[4:5, Q + C : V]], axis=1)[0]
     dsb[...] = small[7, :H]
     drate[...] = small[7, GROUP : GROUP + H]
     lanes = iota((1, H), 1)
@@ -1014,13 +1095,14 @@
     scratch = dict(
         hv=vmem((N, D), BF16), cv=vmem((N, D), BF16), ov=vmem((N, D), BF16), iv=vmem((N, D), BF16),
         wall=vmem((D, V + LANES + C), BF16), wo=vmem((D, C), BF16), wt=vmem((blocks, GROUP, LANES), F32),
-        wst=vmem((GROUP, D), F32), hcol=vmem((GROUP, LANES), F32), tile=vmem((LANES, LANES), F32), gain=vmem((8, D), F32), par=vmem((16, V), F32),
+        hcol=vmem((GROUP, LANES), F32), tile=vmem((LANES, LANES), F32), gain=vmem((8, D), F32), par=vmem((16, V), F32),
         segc=vmem((T, LANES), F32), segr=vmem((R8, T), F32), carried=vmem((R8, T), F32), closing=vmem((R8, T), F32),
         segb=vmem((R8, LANES), F32), sega=vmem((R8, LANES), F32),
-        early=vmem((R, z.K - 1, EDGE, HALO), BF16), late=vmem((R, z.K - 1, HALO, HALO), BF16),
+        early=vmem((R * (z.K - 1) * HALO, R * HALO), BF16), late=vmem((R, (z.K - 1) * HALO, HALO), BF16),
+        hfix=vmem((R * (z.K - 1) * HALO, V), F32), lfix=vmem(((z.K - 1) * HALO, V), F32),
         down=vmem((R, z.K - 1, T, T), BF16), up=vmem((R, z.K - 1, T, T), BF16), lower=vmem((T, T), BF16), upper=vmem((T, T), BF16),
         past=vmem((R, T, T), BF16), next=vmem((R, T, T), BF16),
-        hh=vmem((R * HALO, D), BF16), nrmh=vmem((R * HALO, D), BF16), vh=vmem((R * HALO, V), BF16),
+        hh=vmem((R * HALO, D), BF16), nrmh=vmem((R * HALO, D), BF16),
         nrm=vmem((N, D), BF16), nrmt=vmem((D, N), BF16), cott=vmem((D, N), BF16),
         v=vmem((N, V), BF16), mix=vmem((N, V), BF16), slope=vmem((N, V), F32),
         pre=vmem((GROUP, N), F32), step=vmem((GROUP, N), F32), cols=vmem((N, LANES), F32), xt=vmem((N, C), BF16),
@@ -1046,14 +1128,15 @@
         ls=vmem((rp + HALO, z.Q), F32), lr=vmem((rp + HALO, z.Q), F32),
         sm=vmem((ntn, 8, z.WL), F32), sd=vmem((nd, 8, z.WL), F32), sc=vmem((nc, 8, z.WL), F32),
         l_in=dma((2,)), l_out=dma((2, R)),
-        wz_send=dma((PIECES, 2, nc)), wd_send=dma((PIECES, nc, nd)), w_recv=dma((PIECES, nd, nc)),
+        wz_send=dma((PIECES, 2, nc, z.SUB)), wd_send=dma((PIECES, nc, nd, z.SUB)), w_recv=dma((PIECES, nd, nc, z.SUB)),
+        wh_send=dma((nd,)), wh_recv=dma((nd,)),
         h_send=dma((R,)), h_recv=dma((R,)),
         s_send=dma((R,)), s_recv=dma((R,)), g_send=dma((R,)), g_recv=dma((R,)), e_send=dma((R,)), e_recv=dma((R,)),
         x_send=dma((R, ntn)), x_recv=dma((R, ntn)),
         a_send=dma((2, R)), a_recv=dma((2, R)), b_send=dma((2, R)), b_recv=dma((2, R)),
         c_send=dma((2, R)), c_recv=dma((2, R)),
         ry_send=dma((3, nc, k0)), ry_recv=dma((3, nc, k0)), rz_send=dma((3, nc)), rz_recv=dma((3, nc)),
-        sh_send=dma((3,)), sh_recv=dma((3,)),
+        sh_send=dma((2,)), sh_recv=dma((2,)),
         st_send=dma((ntn,)), st_recv=dma((ntn,)), sd_send=dma((nd,)), sd_recv=dma((nd,)),
         sc_send=dma((nc,)), sc_recv=dma((nc,)),
     )
@@ -1082,7 +1165,7 @@
         in_specs=[whole] * 6,
         out_specs=[large] * 2 + [whole] * (len(shapes) - 2),
         scratch_shapes=[vmem((LANES, LANES), F32), dma((2,))],
-        compiler_params=pltpu.CompilerParams(vmem_limit_bytes=16 << 20),
+        compiler_params=pltpu.CompilerParams(vmem_limit_bytes=z.limit),
     )(*raw)
     (block_out, input_grad, norm, heads, shared, step, taps, bias, staps, sbias, dsb, drate, dskip, gain, outw) = outs
     return (
@@ -1106,6 +1189,7 @@
             R=micro * seqs, T=tokens, d_true=width, D=rp * nd * nc, rows=rows, rp=rp, nd=nd, nc=nc, ntn=ntn,
             C=inner, H=args[10].shape[0], S=shared.shape[1], K=args[6].shape[0],
             Q=shared.shape[1] // 2, limit=62 << 20,
+            SUB=3 if rp % 48 == 0 else 1,
         )
         z.WL = max(inner + z.S, z.D, LANES + inner)
         return on_device(z, *args)

time: 132 us -> 116 us (0.88)
  Pallas kernels: 124 us -> 114 us
  local copies, waits for them, and re-layouts: 6.23 us -> 0 us
    pallas_call x1, Pallas kernels: 122 us -> 110 us  [on_device(): pl.pallas_call(functools.partial(kernel, z, names), out_shape=list(outs.v...]
    unnamed x12 -> x0, local copies, waits for them, and re-layouts: 6.23 us -> none
    pallas_call x1, Pallas kernels: 2.56 us -> 4.48 us  [on_device(): pl.pallas_call(functools.partial(finishing, z), out_shape=[jax.ShapeDtype...]
where the time goes in v4:
time: 116 us; the launch traced here: 115 us
  Pallas kernels  114 us (98%)
    pallas_call x1, Pallas kernels, on_device(): pl.pallas_call(functools.partial(kernel, z, names), out_shape=list(outs.v...  110 us
    pallas_call x1, Pallas kernels, on_device(): pl.pallas_call(functools.partial(finishing, z), out_shape=[jax.ShapeDtype...  4.48 us

profile of v4, /device:TPU:0, one launch (start us, length us, event | category | flops | bytes accessed | tf_op | source)
XLA Modules:
  0.0 114.9 jit_solution(8560824284836680388)
XLA Ops:
  0.7 109.6 %shard_map.271 = (bf16[1024,768]{1,0:T(8,128)(2,1)}, bf16[1024,768]{1,0:T(8,128)(2,1)}, f32[96,384]{1,0:T(8,128)}, f32[96,768]{1,0:T(8,128)}, f32[112,128]{1,0:T(8,128)}, /*index=5*/f32[8,768]{1,0:T(8,128)}) custom-call(bf16[1024,768]{1,0:T(8,128)(2,1)} %bitcast.12, bf16[1024,768]{1,0:T(8,128)(2,1)} %bitcast.13, s32[2,2,1024]{2,1,0:T(2,128)} %refs_2_.1, ...), custom_call_target="tpu_custom_call" | custom-call | tf_op jit(solution)/shard_map/pallas_call | solution.py:1146
  110.3 4.5 %shard_map.272 = (bf16[1024,768]{1,0:T(8,128)(2,1)}, bf16[1024,768]{1,0:T(8,128)(2,1)}, f32[768]{0:T(1024)}, f32[96,2,384]{2,1,0:T(2,128)}, f32[64,96]{1,0:T(8,1...) custom-call(bf16[1024,768]{1,0:T(8,128)(2,1)} %get-tuple-element.36., ...), custom_call_target="tpu_custom_call" | custom-call | tf_op jit(solution)/shard_map/pallas_call | solution.py:1162

commit v5 on v4

--- a/solution.py
+++ b/solution.py
@@ -108,8 +108,8 @@
     load(0).start()
     load(1).start()
     barrier = pltpu.get_barrier_semaphore()
-    peers = [(d, at_ctx(k), t) for k in range(1, nc)]
-    peers += [(at_dp(k), c, t) for k in range(1, nd)]
+    others = [(at_dp(k), at_ctx(j), t) for k in range(nd) for j in range(nc) if k or j]
+    peers = list(others)
     peers += [(d, c, at_ten(k)) for k in range(1, ntn)]
     for peer in peers:
         pl.semaphore_signal(barrier, inc=1, device_id=peer, device_id_type=MESH)
@@ -280,7 +280,7 @@
         m.gin[...] = jnp.zeros_like(m.gin)
         m.dce[...] = jnp.zeros_like(m.dce)
 
-    m.sm[t] = jnp.zeros((8, z.WL), F32)
+    m.sm[...] = jnp.zeros_like(m.sm)
     m.hacc[...] = jnp.zeros_like(m.hacc)
     m.drow[...] = jnp.zeros_like(m.drow)
     m.gstep[...] = jnp.zeros_like(m.gstep)
@@ -309,8 +309,8 @@
             m.late[r, (j - 1) * HALO : j * HALO, :] = (late & (ahead == j)).astype(BF16)
 
     w_step(0, 1)
+    w_step(1, 1)
     w_start(2)
-    w_step(1, 1)
 
     @pl.when(c > 0)
     def _():
@@ -321,8 +321,10 @@
     for s in range(2, nc):
         w_step(0, s)
         w_step(1, s)
+        if s == 2:
+            w_start(3)
     half_copy(0).start()
-    w_start(3)
+    w_step(2, 1)
     w_rest(1)
 
     m.tile[...] = jnp.zeros_like(m.tile)
@@ -332,6 +334,9 @@
     w_rest(0)
     for k in range(1, nd):
         half_copy(k).start()
+    w_step(3, 1)
+    if nc > 2:
+        w_step(2, 2)
 
     low_lanes = iota((T, LANES), 1) < head
     lane = iota((T, LANES), 1)
@@ -453,11 +458,11 @@
             m.ssend[r] = m.fresh[r].astype(BF16)
             state_copy(r).start()
 
-        for s in range(1, min(nc, R + 1)):
-            pl.when(r == s - 1)(lambda: w_step(2, s))
-
-    for s in range(R + 1, nc):
-        w_step(2, s)
+        for s in range(2, nc):
+            pl.when(r == min(s - 2, R - 1))(lambda: w_step(3, s))
+        for s in range(3, nc):
+            pl.when(r == min(s - 3, R - 1))(lambda: w_step(2, s))
+
     state_point([(2, 0)], True)
 
     @pl.loop(0, R)
@@ -474,13 +479,9 @@
                     weight = (decay * m.scores[rows, :seen]).astype(BF16)
                     both.append(nn(weight, m.xs[pl.ds(pl.multiple_of(r * T, 16), seen), pair(p)]))
                 m.ins[here, pair(p)] = jnp.where(low_lanes[:LANES], both[0], both[1])
-        for s in range(1, min(nc, R + 1)):
-            pl.when(r == s - 1)(lambda: w_step(3, s))
         state_point([(1, 2)], r == 0)
         state_point([(2, 1)], r == 2)
 
-    for s in range(R + 1, nc):
-        w_step(3, s)
     state_point([(1, 3)], True)
     w_rest(2)
     w_rest(3)
@@ -588,7 +589,7 @@
             gate = m.zv[row(r), pair(p)].astype(F32)
             gain = m.par[5:6, pair(p)]
             normal = gated * scale
-            m.sm[t, 5:6, pair(p)] += jnp.sum(dy * normal, axis=0, keepdims=True)
+            m.sm[5:6, pair(p)] += jnp.sum(dy * normal, axis=0, keepdims=True)
             m.yg[row(r), pair(p)] = (normal * gain).astype(BF16)
             d_gated = scale * dy * gain - gated * inner
             logistic = sigmoid(gate)
@@ -616,7 +617,12 @@
 
         grad_point([(1, 0)], i == 3)
         grad_point([(1, 1)], i == 4)
-        pl.when(i >= 1)(lambda: chip_sum(0, i - 1))
+
+        @pl.when(i == R - 1)
+        def _():
+            pl.loop(0, R - 1)(lambda r: chip_sum(0, r))
+
+        pl.when(i == R)(lambda: chip_sum(0, R - 1))
 
     gall, gyr, gzs, gzr = (m.ga0, m.ga1, m.ga2), (m.gy0, m.gy1, m.gy2), (m.gz0, m.gz1, m.gz2), (m.gr0, m.gr1, m.gr2)
     tall = (rp, rp, rp + HALO)
@@ -742,7 +748,6 @@
         pl.when(grad_late)(lambda: serve_grad(r))
         b = m.mix[row(r), BX]
         grad = m.gin[r]
-        ring = lax.rem(r, 2)
         for p in range(pairs):
             trailing = widened(m.cols[row(r), :], TRAIL, p)
             reach = nn(b, m.gin[r, :, pair(p)]) * trailing
@@ -751,20 +756,23 @@
             d_ssd = m.ssd[row(r), pair(p)]
             m.prod[:, pair(p)] = m.xs[row(r), pair(p)].astype(F32) * reach
             m.prod[:, C + p * LANES : C + (p + 1) * LANES] = d_xs * x
-            m.sm[t, 7:8, LANES + p * LANES : 2 * LANES + p * LANES] += jnp.sum(d_ssd * x, axis=0, keepdims=True)
-            m.dcf[ring, :, lanes_of(p)] = (
+            m.sm[7:8, LANES + p * LANES : 2 * LANES + p * LANES] += jnp.sum(d_ssd * x, axis=0, keepdims=True)
+            m.dy[row(r), pair(p)] = (
                 d_xs * widened(m.cols[row(r), :], STEP, p) + m.par[6:7, pair(p)] * d_ssd
             ) * m.slope[row(r), lanes_of(p)]
-        m.dcf[ring, :, BX] = (
+        m.gated[row(r), :Q] = (
             m.gated[row(r), :LANES] + nt(m.xt[row(r), :], grad)
         ) * m.slope[row(r), BX]
-        m.dcf[ring, :, CX] = (
+        m.gated[row(r), Q:S] = (
             m.gated[row(r), LANES:S] + nt(m.wds[row(r), :], m.sin[r])
         ) * m.slope[row(r), CX]
 
         @pl.when(c > 0)
         def _():
-            m.edge[r] = m.dcf[ring, 0:EDGE, :]
+            first = pl.ds(pl.multiple_of(r * T, 16), EDGE)
+            m.edge[r, :, BX] = m.gated[first, :Q]
+            m.edge[r, :, Q : Q + C] = m.dy[first, :]
+            m.edge[r, :, CX] = m.gated[first, Q:S]
             edge_copy(r).start()
 
         m.drun[row(r), :] += exact_right(m.prod[:, :C], fold_through) + exact_right(m.prod[:, C:], fold_step)
@@ -792,17 +800,18 @@
         def _():
             edge_copy(r).wait_recv()
 
-        ring = lax.rem(r, 2)
         edge = m.dce[r]
         edge = jnp.concatenate([edge, jnp.zeros_like(edge)], axis=0).astype(BF16)
         m.lfix[...] = nn(m.late[r], edge)
-        for a in range(0, V, WIDE):
-            part = slice(a, min(a + WIDE, V))
-            d_conv = m.dcf[ring, :, part]
+        cuts = [(m.gated, 0, 0, Q), (m.gated, Q, Q + C, Q)]
+        cuts += [(m.dy, a, Q + a, min(WIDE, C - a)) for a in range(0, C, WIDE)]
+        for held, place, first, size in cuts:
+            part = slice(first, first + size)
+            d_conv = held[row(r), place : place + size]
             low = d_conv.astype(BF16)
             value = m.v[row(r), part].astype(F32)
-            m.sm[t, 4:5, part] += jnp.sum(d_conv, axis=0, keepdims=True)
-            m.sm[t, 0:1, part] += jnp.sum(d_conv * value, axis=0, keepdims=True)
+            m.sm[4:5, part] += jnp.sum(d_conv, axis=0, keepdims=True)
+            m.sm[0:1, part] += jnp.sum(d_conv * value, axis=0, keepdims=True)
             d_v = d_conv * m.par[0:1, part]
             for j in range(1, z.K):
                 moved = nn(m.up[r, j - 1], low)
@@ -810,7 +819,7 @@
                     [moved[: T - HALO], moved[T - HALO :] + m.lfix[(j - 1) * HALO : j * HALO, part]], axis=0
                 )
                 d_v = d_v + moved * m.par[j : j + 1, part]
-                m.sm[t, j : j + 1, part] += jnp.sum(moved * value, axis=0, keepdims=True)
+                m.sm[j : j + 1, part] += jnp.sum(moved * value, axis=0, keepdims=True)
             m.dcat[row(r), part] = d_v.astype(BF16)
 
     def finish_norm(r):
@@ -818,32 +827,55 @@
         give(1, r, value)
         u = m.hv[row(r), :].astype(F32)
         mean = jnp.sum(u * u, axis=-1, keepdims=True) * (1.0 / z.d_true)
-        m.sm[t, 6:7, :D] += jnp.sum(value * (u * lax.rsqrt(mean + EPS)), axis=0, keepdims=True)
+        m.sm[6:7, :D] += jnp.sum(value * (u * lax.rsqrt(mean + EPS)), axis=0, keepdims=True)
 
     m.tot[...] = jnp.zeros_like(m.tot)
 
-    @pl.loop(0, max(R + 1, nc))
-    def _(i):
-        @pl.when(i < R)
-        def _():
-            final_out(i)
-            adjoint(i)
-
-        @pl.when(i < nc)
-        def _():
-            rs_middle(1, lax.rem(i + 1, nc))
-
-        @pl.when((i >= 1) & (i < R + 1))
-        def _():
-            finish(i - 1)
-
-        @pl.when((i >= 1) & (i < R))
-        def _():
-            finish_norm(i - 1)
-
-        @pl.when((i >= 2) & (i < R + 1))
-        def _():
-            chip_sum(1, i - 2)
+    def first_sums(j, upward):
+        up = c + j < nc
+        pl.when(up if upward else jnp.logical_not(up))(lambda: rs_middle(1, j))
+
+    @pl.loop(0, R)
+    def _(r):
+        pl.when(r == 0)(lambda: final_out(0))
+        adjoint(r)
+        for j in range(1, min(nc, 3)):
+            pl.when(r == min(2 * j - 2, R - 1))(lambda: first_sums(j, True))
+
+    @pl.loop(0, R)
+    def _(r):
+        finish(r)
+        finish_norm(r)
+        for k in range(1, R):
+            pl.when(r == (k - 1 if k < R - 1 else R - 1))(lambda: final_out(k))
+        for j in range(3, nc):
+            pl.when(r == min(j - 3, R - 1))(lambda: first_sums(j, True))
+        for j in range(1, nc):
+            pl.when(r == min(j - 1, R - 1))(lambda: first_sums(j, False))
+        pl.when(r == R - 1)(lambda: rs_middle(1, 0))
+        pl.when(r >= 1)(lambda: chip_sum(1, r - 1))
+
+    def small_copy(index):
+        return copy(m.sa.at[d * nc + c], m.sa.at[d * nc + c], m.sa_send.at[index], m.sa_recv.at[d * nc + c], others[index])
+
+    def small_arrived(dd, cc):
+        there = m.sa.at[dd * nc + cc]
+        copy(there, there, m.sa_send.at[0], m.sa_recv.at[dd * nc + cc], (d, c, t)).wait_recv()
+
+    def common_copy(k):
+        return copy(m.sb2.at[t], m.sb2.at[t], m.st_send.at[k], m.st_recv.at[t], (d, c, at_ten(k)))
+
+    def common_arrived(who):
+        copy(m.sb2.at[who], m.sb2.at[who], m.st_send.at[0], m.st_recv.at[who], (d, c, t)).wait_recv()
+
+    m.tile[...] = jnp.zeros_like(m.tile)
+    m.tile[0 : 2 * GROUP, :] = jnp.broadcast_to(
+        jnp.sum(m.hacc[...], axis=1, keepdims=True), (2 * GROUP, LANES)
+    )
+    m.sm[7:8, 0:LANES] = jnp.transpose(m.tile[...])[0:1, :]
+    m.sa[d * nc + c] = jnp.concatenate([m.sm[...], jnp.zeros_like(m.sm)], axis=0).astype(BF16)
+    for index in range(len(others)):
+        small_copy(index).start()
 
     width = S // ntn
     starts = [k * width + (C if k * width >= Q else 0) for k in range(ntn)]
@@ -856,18 +888,6 @@
     m.shk[...] = jnp.where(odd == 0, value[:, : z.Q], value[:, z.Q :])
     m.shs[...] = jnp.where(odd == 0, value[:, z.Q :], value[:, : z.Q]).astype(BF16)
     share_copy().start()
-
-    def small_ten(k):
-        return copy(m.sm.at[t], m.sm.at[t], m.st_send.at[k], m.st_recv.at[t], (d, c, at_ten(k)))
-
-    def small_dp(k):
-        return copy(m.sd.at[d], m.sd.at[d], m.sd_send.at[k], m.sd_recv.at[d], (at_dp(k), c, t))
-
-    def small_ctx(k):
-        return copy(m.sc.at[c], m.sc.at[c], m.sc_send.at[k], m.sc_recv.at[c], (d, at_ctx(k), t))
-
-    def arrived(buf, sems, who):
-        copy(buf.at[who], buf.at[who], sems.at[who], sems.at[who], (d, c, t)).wait_recv()
 
     m.ga0[...] = nn(m.nrmt[...], m.dcat[:, Q : Q + C]).astype(BF16)
     share_copy().wait_recv()
@@ -881,39 +901,15 @@
         ).astype(BF16)
     rs_start(2)
     rs_start(0)
-    finish_norm(R - 1)
-    m.tile[...] = jnp.zeros_like(m.tile)
-    m.tile[0 : 2 * GROUP, :] = jnp.broadcast_to(
-        jnp.sum(m.hacc[...], axis=1, keepdims=True), (2 * GROUP, LANES)
-    )
-    m.sm[t, 7:8, 0:LANES] = jnp.transpose(m.tile[...])[0:1, :]
-    for k in range(1, ntn):
-        small_ten(k).start()
-
     chip_sum(1, R - 1)
 
-    for k in range(1, ntn):
-        arrived(m.sm, m.st_recv, at_ten(k))
-    common = m.sm[0]
-    for who in range(1, ntn):
-        common = common + m.sm[who]
-    rows8, lanes8 = iota((8, z.WL), 0), iota((8, z.WL), 1)
-    shared_here = (rows8 == 6) | ((rows8 < 5) & ((lanes8 < Q) | (lanes8 >= Q + C)))
-    m.sd[d] = jnp.where(shared_here, common, m.sm[t])
-    for k in range(1, nd):
-        small_dp(k).start()
+    def last_copy():
+        return copy(m.ls, m.lr, m.sh_send.at[1], m.sh_recv.at[1], (d, c, far))
 
     def store(a, r):
         return pltpu.make_async_copy((m.ov, m.iv)[a].at[row(r)], (m.out, m.ing)[a].at[row(r)], m.l_out.at[a, r])
 
-    for r in range(R):
-        back_arrived(0, r)
-        store(0, r).start()
-    for j in list(range(1, nc)) + [0]:
-        rs_middle(2, j)
-
-    @pl.loop(0, R)
-    def _(r):
+    def input_row(r):
         u = m.hv[mine(r), :].astype(F32)
         mean = jnp.sum(u * u, axis=-1, keepdims=True) * (1.0 / z.d_true)
         scale = lax.rsqrt(mean + EPS)
@@ -924,51 +920,62 @@
         m.iv[mine(r), :] = value.astype(BF16)
         back_copy(1, r).start()
 
-        @pl.when(r < nc)
+    for dd in range(nd):
+        for cc in range(nc):
+            pl.when((dd != d) | (cc != c))(lambda: small_arrived(dd, cc))
+    total = m.sa[0].astype(F32)
+    for who in range(1, nd * nc):
+        total = total + m.sa[who].astype(F32)
+    m.sb2[t] = total[0:8]
+    for k in range(1, ntn):
+        common_copy(k).start()
+    for r in range(R):
+        back_arrived(0, r)
+        store(0, r).start()
+    for j in list(range(1, nc)) + [0]:
+        rs_middle(2, j)
+    m.gw1[...] = rs_end(1)
+
+    @pl.loop(0, R)
+    def _(r):
+        input_row(r)
+        pl.when(r >= 1)(lambda: back_arrived(1, r - 1))
+        pl.when(r >= 1)(lambda: store(1, r - 1).start())
+
+        @pl.when(r == 0)
         def _():
-            rs_middle(0, lax.rem(r + 1, nc))
-
-    for j in range(R + 1, nc + 1):
-        rs_middle(0, j % nc)
-
-    for k in range(1, nd):
-        arrived(m.sd, m.sd_recv, at_dp(k))
-    total = m.sd[0]
-    for who in range(1, nd):
-        total = total + m.sd[who]
-    m.sc[c] = total
-    for k in range(1, nc):
-        small_ctx(k).start()
-
-    def last_copy():
-        return copy(m.ls, m.lr, m.sh_send.at[1], m.sh_recv.at[1], (d, c, far))
-
-    value = rs_end(2)
-    if ntn == 4:
-        m.ls[...] = value
-        last_copy().start()
-    else:
-        m.gw2[...] = value
-    m.gw1[...] = rs_end(1)
-
-    for r in range(R):
-        back_arrived(1, r)
-        store(1, r).start()
-
-    for k in range(1, nc):
-        arrived(m.sc, m.sc_recv, at_ctx(k))
-    total = m.sc[0]
-    for who in range(1, nc):
-        total = total + m.sc[who]
-    m.small[...] = total
-
+            rs_middle(0, 1 % nc)
+
+        @pl.when(r == 1)
+        def _():
+            for j in list(range(2, nc)) + ([0] if nc > 1 else []):
+                rs_middle(0, j)
+
+        @pl.when(r == min(2, R - 1))
+        def _():
+            value = rs_end(2)
+            if ntn == 4:
+                m.ls[...] = value
+                last_copy().start()
+            else:
+                m.gw2[...] = value
+
+    for k in range(1, ntn):
+        common_arrived(at_ten(k))
+    common = m.sb2[0]
+    for who in range(1, ntn):
+        common = common + m.sb2[who]
+    rows8, lanes8 = iota((8, z.WL), 0), iota((8, z.WL), 1)
+    shared_here = (rows8 == 6) | ((rows8 < 5) & ((lanes8 < Q) | (lanes8 >= Q + C)))
+    m.small[...] = jnp.where(shared_here, common, m.sb2[t])
+    m.gw0[...] = rs_end(0)
     if ntn == 4:
         last_copy().wait_recv()
         m.gw2[0:rp, :] = m.ls[0:rp, :] + m.lr[0:rp, :]
         m.gw2[rp:, :] = m.ls[rp:, :]
         last_copy().wait_send()
-
-    m.gw0[...] = rs_end(0)
+    back_arrived(1, R - 1)
+    store(1, R - 1).start()
 
     for a in range(2):
         for r in range(R):
@@ -998,12 +1005,10 @@
             edge_copy(r).wait_send()
 
     share_copy().wait_send()
+    for index in range(len(others)):
+        small_copy(index).wait_send()
     for k in range(1, ntn):
-        small_ten(k).wait_send()
-    for k in range(1, nd):
-        small_dp(k).wait_send()
-    for k in range(1, nc):
-        small_ctx(k).wait_send()
+        common_copy(k).wait_send()
 
 
 def finishing(z, out, ing, gw0, gw1, gw2, small, *outs):
@@ -1121,12 +1126,12 @@
         gy0=vmem((k0, nc * rp, C), BF16), gy1=vmem((k0, nc * rp, 2 * C), BF16), gy2=vmem((k0, nc * (rp + HALO), z.Q), BF16),
         gz0=vmem((nc * rp, C), BF16), gz1=vmem((nc * rp, 2 * C), BF16), gz2=vmem((nc * (rp + HALO), z.Q), BF16),
         gr0=vmem((nc, rp, C), BF16), gr1=vmem((nc, rp, 2 * C), BF16), gr2=vmem((nc, rp + HALO, z.Q), BF16),
-        drun=vmem((N, LANES), F32), dcf=vmem((2, T, V), F32), edge=vmem((R, EDGE, V), F32),
+        drun=vmem((N, LANES), F32), edge=vmem((R, EDGE, V), F32),
         dce=vmem((R, EDGE, V), F32), dcat=vmem((N, V + LANES + C), BF16),
         prod=vmem((T, 2 * C), F32), hacc=vmem((2 * GROUP, T), F32), gstep=vmem((HALO, D), F32),
         shs=vmem((D, z.Q), BF16), shr=vmem((D, z.Q), BF16), shk=vmem((D, z.Q), F32),
         ls=vmem((rp + HALO, z.Q), F32), lr=vmem((rp + HALO, z.Q), F32),
-        sm=vmem((ntn, 8, z.WL), F32), sd=vmem((nd, 8, z.WL), F32), sc=vmem((nc, 8, z.WL), F32),
+        sm=vmem((8, z.WL), F32), sa=vmem((blocks, 16, z.WL), BF16), sb2=vmem((ntn, 8, z.WL), F32),
         l_in=dma((2,)), l_out=dma((2, R)),
         wz_send=dma((PIECES, 2, nc, z.SUB)), wd_send=dma((PIECES, nc, nd, z.SUB)), w_recv=dma((PIECES, nd, nc, z.SUB)),
         wh_send=dma((nd,)), wh_recv=dma((nd,)),
@@ -1137,8 +1142,7 @@
         c_send=dma((2, R)), c_recv=dma((2, R)),
         ry_send=dma((3, nc, k0)), ry_recv=dma((3, nc, k0)), rz_send=dma((3, nc)), rz_recv=dma((3, nc)),
         sh_send=dma((2,)), sh_recv=dma((2,)),
-        st_send=dma((ntn,)), st_recv=dma((ntn,)), sd_send=dma((nd,)), sd_recv=dma((nd,)),
-        sc_send=dma((nc,)), sc_recv=dma((nc,)),
+        st_send=dma((ntn,)), st_recv=dma((ntn,)), sa_send=dma((max(blocks - 1, 1),)), sa_recv=dma((blocks,)),
     )
     names = list(ins) + list(outs) + list(scratch)
     whole = pl.BlockSpec(memory_space=pltpu.VMEM)

time: 116 us -> 109 us (0.940)
  Pallas kernels: 114 us -> 107 us
    pallas_call x1, Pallas kernels: 110 us -> 103 us  [on_device(): pl.pallas_call(functools.partial(kernel, z, names), out_shape=list(outs.v...]
where the time goes in v5:
time: 109 us; the launch traced here: 108 us
  Pallas kernels  107 us (98%)
    pallas_call x1, Pallas kernels, on_device(): pl.pallas_call(functools.partial(kernel, z, names), out_shape=list(outs.v...  103 us
    pallas_call x1, Pallas kernels, on_device(): pl.pallas_call(functools.partial(finishing, z), out_shape=[jax.ShapeDtype...  4.48 us

profile of v5, /device:TPU:0, one launch (start us, length us, event | category | flops | bytes accessed | tf_op | source)
XLA Modules:
  0.0 107.8 jit_solution(17649593008108725660)
XLA Ops:
  0.7 102.5 %shard_map.271 = (bf16[1024,768]{1,0:T(8,128)(2,1)}, bf16[1024,768]{1,0:T(8,128)(2,1)}, f32[96,384]{1,0:T(8,128)}, f32[96,768]{1,0:T(8,128)}, f32[112,128]{1,0:T(8,128)}, /*index=5*/f32[8,768]{1,0:T(8,128)}) custom-call(bf16[1024,768]{1,0:T(8,128)(2,1)} %bitcast.12, bf16[1024,768]{1,0:T(8,128)(2,1)} %bitcast.13, s32[2,2,1024]{2,1,0:T(2,128)} %refs_2_.1, ...), custom_call_target="tpu_custom_call" | custom-call | tf_op jit(solution)/shard_map/pallas_call | solution.py:1150
  103.2 4.5 %shard_map.272 = (bf16[1024,768]{1,0:T(8,128)(2,1)}, bf16[1024,768]{1,0:T(8,128)(2,1)}, f32[768]{0:T(1024)}, f32[96,2,384]{2,1,0:T(2,128)}, f32[64,96]{1,0:T(8,1...) custom-call(bf16[1024,768]{1,0:T(8,128)(2,1)} %get-tuple-element.36., ...), custom_call_target="tpu_custom_call" | custom-call | tf_op jit(solution)/shard_map/pallas_call | solution.py:1166

commit v6 on v5

--- a/solution.py
+++ b/solution.py
@@ -607,16 +607,15 @@
             if nc > 1:
                 grad_copy(r).start()
 
-    @pl.loop(0, R + 1)
+    @pl.loop(0, R + 2)
     def _(i):
         pl.when(i < R)(lambda: gating(i))
 
-        @pl.when(i >= 1)
-        def _():
-            ungating(i - 1)
-
-        grad_point([(1, 0)], i == 3)
-        grad_point([(1, 1)], i == 4)
+        @pl.when(i >= 2)
+        def _():
+            ungating(i - 2)
+
+        grad_point([(1, 0)], i == R + 1)
 
         @pl.when(i == R - 1)
         def _():
@@ -694,7 +693,7 @@
     m.ga1[:, C:] = nn(m.cott[...], m.yg[...]).astype(BF16)
     m.ga1[:, :C] = nn(m.nrmt[...], m.dcat[:, Z:]).astype(BF16)
     rs_start(1)
-    grad_point([(1, 2), (2, 0)], True)
+    grad_point([(1, 1), (1, 2), (2, 0)], True)
 
     @pl.loop(0, R)
     def _(r):
@@ -845,15 +844,14 @@
     @pl.loop(0, R)
     def _(r):
         finish(r)
-        finish_norm(r)
-        for k in range(1, R):
-            pl.when(r == (k - 1 if k < R - 1 else R - 1))(lambda: final_out(k))
+        pl.when(r == 0)(lambda: finish_norm(0))
+        pl.when(r == min(1, R - 1))(lambda: chip_sum(1, 0))
+        for k in range(1, R - 1):
+            pl.when(r == min(2 * k - 1, R - 1))(lambda: final_out(k))
         for j in range(3, nc):
-            pl.when(r == min(j - 3, R - 1))(lambda: first_sums(j, True))
+            pl.when(r == min(j - 1, R - 1))(lambda: first_sums(j, True))
         for j in range(1, nc):
             pl.when(r == min(j - 1, R - 1))(lambda: first_sums(j, False))
-        pl.when(r == R - 1)(lambda: rs_middle(1, 0))
-        pl.when(r >= 1)(lambda: chip_sum(1, r - 1))
 
     def small_copy(index):
         return copy(m.sa.at[d * nc + c], m.sa.at[d * nc + c], m.sa_send.at[index], m.sa_recv.at[d * nc + c], others[index])
@@ -867,15 +865,6 @@
 
     def common_arrived(who):
         copy(m.sb2.at[who], m.sb2.at[who], m.st_send.at[0], m.st_recv.at[who], (d, c, t)).wait_recv()
-
-    m.tile[...] = jnp.zeros_like(m.tile)
-    m.tile[0 : 2 * GROUP, :] = jnp.broadcast_to(
-        jnp.sum(m.hacc[...], axis=1, keepdims=True), (2 * GROUP, LANES)
-    )
-    m.sm[7:8, 0:LANES] = jnp.transpose(m.tile[...])[0:1, :]
-    m.sa[d * nc + c] = jnp.concatenate([m.sm[...], jnp.zeros_like(m.sm)], axis=0).astype(BF16)
-    for index in range(len(others)):
-        small_copy(index).start()
 
     width = S // ntn
     starts = [k * width + (C if k * width >= Q else 0) for k in range(ntn)]
@@ -901,6 +890,23 @@
         ).astype(BF16)
     rs_start(2)
     rs_start(0)
+
+    @pl.loop(1, R)
+    def _(r):
+        finish_norm(r)
+        pl.when(r == min(2, R - 1))(lambda: final_out(R - 1))
+        pl.when(r == 1)(lambda: rs_middle(1, 0))
+        pl.when(r >= 2)(lambda: chip_sum(1, r - 1))
+
+    m.tile[...] = jnp.zeros_like(m.tile)
+    m.tile[0 : 2 * GROUP, :] = jnp.broadcast_to(
+        jnp.sum(m.hacc[...], axis=1, keepdims=True), (2 * GROUP, LANES)
+    )
+    m.sm[7:8, 0:LANES] = jnp.transpose(m.tile[...])[0:1, :]
+    m.sa[d * nc + c] = jnp.concatenate([m.sm[:, : z.WL // 2], m.sm[:, z.WL // 2 :]], axis=0).astype(BF16)
+    for index in range(len(others)):
+        small_copy(index).start()
+
     chip_sum(1, R - 1)
 
     def last_copy():
@@ -920,15 +926,6 @@
         m.iv[mine(r), :] = value.astype(BF16)
         back_copy(1, r).start()
 
-    for dd in range(nd):
-        for cc in range(nc):
-            pl.when((dd != d) | (cc != c))(lambda: small_arrived(dd, cc))
-    total = m.sa[0].astype(F32)
-    for who in range(1, nd * nc):
-        total = total + m.sa[who].astype(F32)
-    m.sb2[t] = total[0:8]
-    for k in range(1, ntn):
-        common_copy(k).start()
     for r in range(R):
         back_arrived(0, r)
         store(0, r).start()
@@ -945,6 +942,18 @@
         @pl.when(r == 0)
         def _():
             rs_middle(0, 1 % nc)
+
+        @pl.when(r == min(2, R - 1))
+        def _():
+            for dd in range(nd):
+                for cc in range(nc):
+                    pl.when((dd != d) | (cc != c))(lambda: small_arrived(dd, cc))
+            total = m.sa[0].astype(F32)
+            for who in range(1, nd * nc):
+                total = total + m.sa[who].astype(F32)
+            m.sb2[t] = jnp.concatenate([total[0:8], total[8:16]], axis=1)
+            for k in range(1, ntn):
+                common_copy(k).start()
 
         @pl.when(r == 1)
         def _():
@@ -1131,7 +1140,7 @@
         prod=vmem((T, 2 * C), F32), hacc=vmem((2 * GROUP, T), F32), gstep=vmem((HALO, D), F32),
         shs=vmem((D, z.Q), BF16), shr=vmem((D, z.Q), BF16), shk=vmem((D, z.Q), F32),
         ls=vmem((rp + HALO, z.Q), F32), lr=vmem((rp + HALO, z.Q), F32),
-        sm=vmem((8, z.WL), F32), sa=vmem((blocks, 16, z.WL), BF16), sb2=vmem((ntn, 8, z.WL), F32),
+        sm=vmem((8, z.WL), F32), sa=vmem((blocks, 16, z.WL // 2), BF16), sb2=vmem((ntn, 8, z.WL), F32),
         l_in=dma((2,)), l_out=dma((2, R)),
         wz_send=dma((PIECES, 2, nc, z.SUB)), wd_send=dma((PIECES, nc, nd, z.SUB)), w_recv=dma((PIECES, nd, nc, z.SUB)),
         wh_send=dma((nd,)), wh_recv=dma((nd,)),

time: 109 us -> 104 us (0.954)
  Pallas kernels: 107 us -> 103 us
    pallas_call x1, Pallas kernels: 103 us -> 98.2 us  [on_device(): pl.pallas_call(functools.partial(kernel, z, names), out_shape=list(outs.v...]
where the time goes in v6:
time: 104 us; the launch traced here: 103 us
  Pallas kernels  103 us (99%)
    pallas_call x1, Pallas kernels, on_device(): pl.pallas_call(functools.partial(kernel, z, names), out_shape=list(outs.v...  98.2 us
    pallas_call x1, Pallas kernels, on_device(): pl.pallas_call(functools.partial(finishing, z), out_shape=[jax.ShapeDtype...  4.48 us

profile of v6, /device:TPU:0, one launch (start us, length us, event | category | flops | bytes accessed | tf_op | source)
XLA Modules:
  0.0 103.5 jit_solution(11450776111897620393)
XLA Ops:
  0.7 98.2 %shard_map.271 = (bf16[1024,768]{1,0:T(8,128)(2,1)}, bf16[1024,768]{1,0:T(8,128)(2,1)}, f32[96,384]{1,0:T(8,128)}, f32[96,768]{1,0:T(8,128)}, f32[112,128]{1,0:T(8,128)}, /*index=5*/f32[8,768]{1,0:T(8,128)}) custom-call(bf16[1024,768]{1,0:T(8,128)(2,1)} %bitcast.12, bf16[1024,768]{1,0:T(8,128)(2,1)} %bitcast.13, s32[2,2,1024]{2,1,0:T(2,128)} %refs_2_.1, ...), custom_call_target="tpu_custom_call" | custom-call | tf_op jit(solution)/shard_map/pallas_call | solution.py:1159
  98.8 4.5 %shard_map.272 = (bf16[1024,768]{1,0:T(8,128)(2,1)}, bf16[1024,768]{1,0:T(8,128)(2,1)}, f32[768]{0:T(1024)}, f32[96,2,384]{2,1,0:T(2,128)}, f32[64,96]{1,0:T(8,1...) custom-call(bf16[1024,768]{1,0:T(8,128)(2,1)} %get-tuple-element.36., ...), custom_call_target="tpu_custom_call" | custom-call | tf_op jit(solution)/shard_map/pallas_call | solution.py:1175

commit v7 on v6

--- a/solution.py
+++ b/solution.py
@@ -109,16 +109,22 @@
     load(1).start()
     barrier = pltpu.get_barrier_semaphore()
     others = [(at_dp(k), at_ctx(j), t) for k in range(nd) for j in range(nc) if k or j]
-    peers = list(others)
+    peers = [(at_dp(k), c, t) for k in range(1, nd)]
     peers += [(d, c, at_ten(k)) for k in range(1, ntn)]
     for peer in peers:
         pl.semaphore_signal(barrier, inc=1, device_id=peer, device_id_type=MESH)
+    for here, step in ((c > 0, -1), (c < nc - 1, 1)):
+
+        @pl.when(here)
+        def _():
+            pl.semaphore_signal(barrier, inc=1, device_id=(d, c + step, t), device_id_type=MESH)
+
 
     m.wall[block(d, c), Q : Q + C] = m.hp[:, 1, :]
     m.wall[block(d, c), lanes_at(odd * (Q + C), Q)] = jnp.where(odd == 0, m.shp[:, :Q], m.shp[:, Q:])
     m.wt[d * nc + c] = jnp.zeros((GROUP, LANES), F32)
     m.wt[d * nc + c, 0:H, 0:rp] = m.stp[...].astype(F32)
-    pl.semaphore_wait(barrier, len(peers))
+    pl.semaphore_wait(barrier, len(peers) + (c > 0).astype(jnp.int32) + (c < nc - 1).astype(jnp.int32))
 
     def subs(p):
         return z.SUB if p == 0 else 1
@@ -509,11 +515,11 @@
         return copy(m.bs_.at[a, r], m.br_.at[a, r], m.b_send.at[a, r], m.b_recv.at[a, r], (d, c, far))
 
     def back_copy(a, r):
-        out = (m.ov, m.iv)[a].at[mine(r)]
+        out = (m.out, m.ing)[a].at[mine(r)]
         return copy(out, out, m.c_send.at[a, r], m.c_recv.at[a, r], (d, c, across))
 
     def back_arrived(a, r):
-        out = (m.ov, m.iv)[a].at[theirs(r)]
+        out = (m.out, m.ing)[a].at[theirs(r)]
         copy(out, out, m.c_send.at[a, r], m.c_recv.at[a, r], (d, c, across)).wait_recv()
 
     def give(a, r, value):
@@ -740,7 +746,7 @@
 
     def final_out(r):
         value = m.hv[mine(r), :].astype(F32) + m.rms[mine(r), 0:1] * full_sum(0, r)
-        m.ov[mine(r), :] = value.astype(BF16)
+        m.out[mine(r), :] = value.astype(BF16)
         back_copy(0, r).start()
 
     def adjoint(r):
@@ -912,9 +918,6 @@
     def last_copy():
         return copy(m.ls, m.lr, m.sh_send.at[1], m.sh_recv.at[1], (d, c, far))
 
-    def store(a, r):
-        return pltpu.make_async_copy((m.ov, m.iv)[a].at[row(r)], (m.out, m.ing)[a].at[row(r)], m.l_out.at[a, r])
-
     def input_row(r):
         u = m.hv[mine(r), :].astype(F32)
         mean = jnp.sum(u * u, axis=-1, keepdims=True) * (1.0 / z.d_true)
@@ -923,12 +926,11 @@
         d_unit = full_sum(1, r) * gain_in
         inner = jnp.sum(d_unit * unit, axis=-1, keepdims=True) * (1.0 / z.d_true)
         value = m.cv[mine(r), :].astype(F32) + scale * (d_unit - unit * inner)
-        m.iv[mine(r), :] = value.astype(BF16)
+        m.ing[mine(r), :] = value.astype(BF16)
         back_copy(1, r).start()
 
     for r in range(R):
         back_arrived(0, r)
-        store(0, r).start()
     for j in list(range(1, nc)) + [0]:
         rs_middle(2, j)
     m.gw1[...] = rs_end(1)
@@ -937,7 +939,6 @@
     def _(r):
         input_row(r)
         pl.when(r >= 1)(lambda: back_arrived(1, r - 1))
-        pl.when(r >= 1)(lambda: store(1, r - 1).start())
 
         @pl.when(r == 0)
         def _():
@@ -984,11 +985,9 @@
         m.gw2[rp:, :] = m.ls[rp:, :]
         last_copy().wait_send()
     back_arrived(1, R - 1)
-    store(1, R - 1).start()
 
     for a in range(2):
         for r in range(R):
-            store(a, r).wait()
             back_copy(a, r).wait_send()
             near_copy(a, r).wait_send()
             if ntn == 4:
@@ -1099,15 +1098,15 @@
         ld=log_decay[None], sk=skip_gain[None], gg=gate_gain,
     )
     outs = dict(
-        out=jax.ShapeDtypeStruct((N, D), BF16),
-        ing=jax.ShapeDtypeStruct((N, D), BF16),
-        gw0=jax.ShapeDtypeStruct((rp, C), F32),
-        gw1=jax.ShapeDtypeStruct((rp, 2 * C), F32),
-        gw2=jax.ShapeDtypeStruct((rp + HALO, z.Q), F32),
-        small=jax.ShapeDtypeStruct((8, z.WL), F32),
+        out=pltpu.VMEM((N, D), BF16),
+        ing=pltpu.VMEM((N, D), BF16),
+        gw0=pltpu.VMEM((rp, C), F32),
+        gw1=pltpu.VMEM((rp, 2 * C), F32),
+        gw2=pltpu.VMEM((rp + HALO, z.Q), F32),
+        small=pltpu.VMEM((8, z.WL), F32),
     )
     scratch = dict(
-        hv=vmem((N, D), BF16), cv=vmem((N, D), BF16), ov=vmem((N, D), BF16), iv=vmem((N, D), BF16),
+        hv=vmem((N, D), BF16), cv=vmem((N, D), BF16),
         wall=vmem((D, V + LANES + C), BF16), wo=vmem((D, C), BF16), wt=vmem((blocks, GROUP, LANES), F32),
         hcol=vmem((GROUP, LANES), F32), tile=vmem((LANES, LANES), F32), gain=vmem((8, D), F32), par=vmem((16, V), F32),
         segc=vmem((T, LANES), F32), segr=vmem((R8, T), F32), carried=vmem((R8, T), F32), closing=vmem((R8, T), F32),
@@ -1141,7 +1140,7 @@
         shs=vmem((D, z.Q), BF16), shr=vmem((D, z.Q), BF16), shk=vmem((D, z.Q), F32),
         ls=vmem((rp + HALO, z.Q), F32), lr=vmem((rp + HALO, z.Q), F32),
         sm=vmem((8, z.WL), F32), sa=vmem((blocks, 16, z.WL // 2), BF16), sb2=vmem((ntn, 8, z.WL), F32),
-        l_in=dma((2,)), l_out=dma((2, R)),
+        l_in=dma((2,)),
         wz_send=dma((PIECES, 2, nc, z.SUB)), wd_send=dma((PIECES, nc, nd, z.SUB)), w_recv=dma((PIECES, nd, nc, z.SUB)),
         wh_send=dma((nd,)), wh_recv=dma((nd,)),
         h_send=dma((R,)), h_recv=dma((R,)),
@@ -1160,7 +1159,7 @@
         functools.partial(kernel, z, names),
         out_shape=list(outs.values()),
         in_specs=[large] * 2 + [whole] * (len(ins) - 2),
-        out_specs=[large] * 2 + [whole] * (len(outs) - 2),
+        out_specs=[whole] * len(outs),
         scratch_shapes=list(scratch.values()),
         compiler_params=pltpu.CompilerParams(
             collective_id=0, has_side_effects=True, vmem_limit_bytes=z.limit
@@ -1179,7 +1178,7 @@
         out_specs=[large] * 2 + [whole] * (len(shapes) - 2),
         scratch_shapes=[vmem((LANES, LANES), F32), dma((2,))],
         compiler_params=pltpu.CompilerParams(vmem_limit_bytes=z.limit),
-    )(*raw)
+    )(*[pltpu.with_memory_space_constraint(value, pltpu.VMEM) for value in raw])
     (block_out, input_grad, norm, heads, shared, step, taps, bias, staps, sbias, dsb, drate, dskip, gain, outw) = outs
     return (
         narrow(block_out).reshape(hidden_in.shape),
@@ -1201,7 +1200,7 @@
         z = types.SimpleNamespace(
             R=micro * seqs, T=tokens, d_true=width, D=rp * nd * nc, rows=rows, rp=rp, nd=nd, nc=nc, ntn=ntn,
             C=inner, H=args[10].shape[0], S=shared.shape[1], K=args[6].shape[0],
-            Q=shared.shape[1] // 2, limit=62 << 20,
+            Q=shared.shape[1] // 2, limit=59 << 20,
             SUB=3 if rp % 48 == 0 else 1,
         )
         z.WL = max(inner + z.S, z.D, LANES + inner)

time: 104 us -> 98.7 us (0.949)
  Pallas kernels: 103 us -> 97.4 us
    pallas_call x1, Pallas kernels: 98.2 us -> 94.8 us  [on_device(): pl.pallas_call(functools.partial(kernel, z, names), out_shape=list(outs.v...]
    pallas_call x1, Pallas kernels: 4.48 us -> 2.57 us  [on_device(): pl.pallas_call(functools.partial(finishing, z), out_shape=[jax.ShapeDtype...]
where the time goes in v7:
time: 98.7 us; the launch traced here: 98.2 us
  Pallas kernels  97.4 us (99%)
    pallas_call x1, Pallas kernels, on_device(): pl.pallas_call(functools.partial(kernel, z, names), out_shape=list(outs.v...  94.8 us
    pallas_call x1, Pallas kernels, on_device(): pl.pallas_call(functools.partial(finishing, z), out_shape=[jax.ShapeDtype...  2.57 us

profile of v7, /device:TPU:0, one launch (start us, length us, event | category | flops | bytes accessed | tf_op | source)
XLA Modules:
  0.0 98.2 jit_solution(10915164077481435455)
XLA Ops:
  0.7 94.8 %shard_map.271 = (bf16[1024,768]{1,0:T(8,128)(2,1)S(1)}, bf16[1024,768]{1,0:T(8,128)(2,1)S(1)}, f32[96,384]{1,0:T(8,128)S(1)}, f32[96,768]{1,0:T(8,128)S(1)}, f3...) custom-call(bf16[1024,768]{1,0:T(8,128)(2,1)} %bitcast.12, bf16[1024,768]{1,0:T(8,128)(2,1)} %bitcast.13, ...), custom_call_target="tpu_custom_call" | custom-call | tf_op jit(solution)/shard_map/pallas_call | solution.py:1158
  95.5 2.6 %shard_map.272 = (bf16[1024,768]{1,0:T(8,128)(2,1)}, bf16[1024,768]{1,0:T(8,128)(2,1)}, f32[768]{0:T(1024)}, f32[96,2,384]{2,1,0:T(2,128)}, f32[64,96]{1,0:T(8,1...) custom-call(bf16[1024,768]{1,0:T(8,128)(2,1)S(1)} %get-tuple-element, ...), custom_call_target="tpu_custom_call" | custom-call | tf_op jit(solution)/shard_map/pallas_call | solution.py:1174

commit v8 on v7

--- a/solution.py
+++ b/solution.py
@@ -105,8 +105,6 @@
     def load(which):
         return pltpu.make_async_copy((m.hid, m.cot)[which], (m.hv, m.cv)[which], m.l_in.at[which])
 
-    load(0).start()
-    load(1).start()
     barrier = pltpu.get_barrier_semaphore()
     others = [(at_dp(k), at_ctx(j), t) for k in range(nd) for j in range(nc) if k or j]
     peers = [(at_dp(k), c, t) for k in range(1, nd)]
@@ -120,6 +118,15 @@
             pl.semaphore_signal(barrier, inc=1, device_id=(d, c + step, t), device_id_type=MESH)
 
 
+    small_loads = []
+    for index, name in enumerate(z.small):
+        small_loads.append(pltpu.make_async_copy(getattr(m, name), getattr(m, name + "_v"), m.a_in.at[index]))
+        small_loads[-1].start()
+        setattr(m, name, getattr(m, name + "_v"))
+    load(0).start()
+    load(1).start()
+    for one in small_loads:
+        one.wait()
     m.wall[block(d, c), Q : Q + C] = m.hp[:, 1, :]
     m.wall[block(d, c), lanes_at(odd * (Q + C), Q)] = jnp.where(odd == 0, m.shp[:, :Q], m.shp[:, Q:])
     m.wt[d * nc + c] = jnp.zeros((GROUP, LANES), F32)
@@ -850,8 +857,8 @@
     @pl.loop(0, R)
     def _(r):
         finish(r)
-        pl.when(r == 0)(lambda: finish_norm(0))
-        pl.when(r == min(1, R - 1))(lambda: chip_sum(1, 0))
+        pl.when(r < 3)(lambda: finish_norm(r))
+        pl.when((r >= 1) & (r - 1 < 3))(lambda: chip_sum(1, r - 1))
         for k in range(1, R - 1):
             pl.when(r == min(2 * k - 1, R - 1))(lambda: final_out(k))
         for j in range(3, nc):
@@ -897,12 +904,12 @@
     rs_start(2)
     rs_start(0)
 
-    @pl.loop(1, R)
+    @pl.loop(3, R)
     def _(r):
         finish_norm(r)
-        pl.when(r == min(2, R - 1))(lambda: final_out(R - 1))
-        pl.when(r == 1)(lambda: rs_middle(1, 0))
-        pl.when(r >= 2)(lambda: chip_sum(1, r - 1))
+        pl.when(r == max(2, 3))(lambda: final_out(R - 1))
+        pl.when(r == 3)(lambda: rs_middle(1, 0))
+        pl.when(r >= 4)(lambda: chip_sum(1, r - 1))
 
     m.tile[...] = jnp.zeros_like(m.tile)
     m.tile[0 : 2 * GROUP, :] = jnp.broadcast_to(
@@ -1152,13 +1159,17 @@
         sh_send=dma((2,)), sh_recv=dma((2,)),
         st_send=dma((ntn,)), st_recv=dma((ntn,)), sa_send=dma((max(blocks - 1, 1),)), sa_recv=dma((blocks,)),
     )
+    z.small = list(ins)[2:]
+    for name in z.small:
+        scratch[name + "_v"] = vmem(ins[name].shape, ins[name].dtype)
+    scratch["a_in"] = dma((len(z.small),))
     names = list(ins) + list(outs) + list(scratch)
     whole = pl.BlockSpec(memory_space=pltpu.VMEM)
     large = pl.BlockSpec(memory_space=pl.ANY)
     raw = pl.pallas_call(
         functools.partial(kernel, z, names),
         out_shape=list(outs.values()),
-        in_specs=[large] * 2 + [whole] * (len(ins) - 2),
+        in_specs=[large] * len(ins),
         out_specs=[whole] * len(outs),
         scratch_shapes=list(scratch.values()),
         compiler_params=pltpu.CompilerParams(

time: 98.7 us -> 96.2 us (0.975)
  Pallas kernels: 97.4 us -> 95.1 us
    pallas_call x1, Pallas kernels: 94.8 us -> 92.5 us  [on_device(): pl.pallas_call(functools.partial(kernel, z, names), out_shape=list(outs.v...]
where the time goes in v8:
time: 96.2 us; the launch traced here: 95.9 us
  Pallas kernels  95.1 us (99%)
    pallas_call x1, Pallas kernels, on_device(): pl.pallas_call(functools.partial(kernel, z, names), out_shape=list(outs.v...  92.5 us
    pallas_call x1, Pallas kernels, on_device(): pl.pallas_call(functools.partial(finishing, z), out_shape=[jax.ShapeDtype...  2.57 us

profile of v8, /device:TPU:0, one launch (start us, length us, event | category | flops | bytes accessed | tf_op | source)
XLA Modules:
  0.0 95.9 jit_solution(10023823136196096429)
XLA Ops:
  0.7 92.5 %shard_map.271 = (bf16[1024,768]{1,0:T(8,128)(2,1)S(1)}, bf16[1024,768]{1,0:T(8,128)(2,1)S(1)}, f32[96,384]{1,0:T(8,128)S(1)}, f32[96,768]{1,0:T(8,128)S(1)}, f3...) custom-call(bf16[1024,768]{1,0:T(8,128)(2,1)} %bitcast.12, bf16[1024,768]{1,0:T(8,128)(2,1)} %bitcast.13, ...), custom_call_target="tpu_custom_call" | custom-call | tf_op jit(solution)/shard_map/pallas_call | solution.py:1169
  93.2 2.6 %shard_map.272 = (bf16[1024,768]{1,0:T(8,128)(2,1)}, bf16[1024,768]{1,0:T(8,128)(2,1)}, f32[768]{0:T(1024)}, f32[96,2,384]{2,1,0:T(2,128)}, f32[64,96]{1,0:T(8,1...) custom-call(bf16[1024,768]{1,0:T(8,128)(2,1)S(1)} %get-tuple-element, ...), custom_call_target="tpu_custom_call" | custom-call | tf_op jit(solution)/shard_map/pallas_call | solution.py:1185
